TPU v7x, 32 devices: a whole 2x2x4 slice. The times are simulated.
32 devices in a mesh: shot: 4 (over z), gx: 4 (over y, x), gy: 2 (over core).
Axes of the slice: x: 2, y: 2, z: 4, core: 2. Of those that a mesh axis runs over, the one named last changes fastest.
Arguments:
- wave_now: float32 [4, 4, 128, 64, 128], P('shot', None, 'gx', 'gy'), may hold values from -6 to 6
- wave_prev: float32 [4, 4, 128, 64, 128], P('shot', None, 'gx', 'gy'), may hold values from -6 to 6
- vel_coef: float32 [128, 64, 128], P('gx', 'gy'), may hold values from 0.08 to 0.18
- epsilon: float32 [128, 64, 128], P('gx', 'gy'), may hold values from 0.15 to 0.35
- delta: float32 [128, 64, 128], P('gx', 'gy'), may hold values from 0 to 0.15
- tilt: int32 [128, 64, 128], P('gx', 'gy'), may hold values from 0 to 60
- azimuth: int32 [128, 64, 128], P('gx', 'gy'), may hold values from 0 to 359
- aperture: int32 [4, 4, 2], P('shot', 'gx', 'gy'), may hold values 0 or 1
Outputs:
- wave_final: float32 [4, 4, 128, 64, 128], P('shot', None, 'gx', 'gy')
- image: float32 [128, 64, 128], P('gx', 'gy')
All inputs are finite; a program needn't handle non-finite values. No bound on the sum of `aperture` on one device may be relied on, other than what follows from the above.
Results may differ from a plain program's by a relative error of at most 0.00002.
Values sent between devices are 32-bit elements; how exact they have to be, the bound alone decides.
No kernel may reach another device: no remote copies, remote signals or barrier semaphores. Data moves between devices by JAX's collectives and lax.ppermute only.
A program may use at most 128 MiB of HBM per device.

v0:
```python
import math

import jax
import jax.numpy as jnp
from jax import lax
from jax.sharding import PartitionSpec as P

ITERS = 4


def extended(block, sides, width):
    for axis, dim in sides:
        count = lax.axis_size(axis)
        forward = [(i, i + 1) for i in range(count - 1)]
        backward = [(target, source) for source, target in forward]
        low = lax.ppermute(
            lax.slice_in_dim(block, block.shape[dim] - width, None, axis=dim), axis, forward
        )
        high = lax.ppermute(lax.slice_in_dim(block, 0, width, axis=dim), axis, backward)
        block = jnp.concatenate([low, block, high], axis=dim)
    return block


def model_terms(vel_coef, epsilon, delta, tilt, azimuth):
    theta = tilt.astype(jnp.float32) * (math.pi / 180.0)
    phi = azimuth.astype(jnp.float32) * (math.pi / 180.0)
    normal_x = jnp.sin(theta) * jnp.cos(phi)
    normal_y = jnp.sin(theta) * jnp.sin(phi)
    normal_z = jnp.cos(theta)
    gain = 1.0 + 2.0 * epsilon
    root = jnp.sqrt(1.0 + 2.0 * delta)
    return jnp.stack([normal_x, normal_y, normal_z, vel_coef, gain, root], axis=0)


def advance(padded, previous, coef):
    width_x = padded.shape[-3] - 2
    width_y = padded.shape[-2] - 2
    width_z = padded.shape[-1] - 2

    def shifted(off_x, off_y, off_z):
        return padded[
            ...,
            1 + off_x : 1 + off_x + width_x,
            1 + off_y : 1 + off_y + width_y,
            1 + off_z : 1 + off_z + width_z,
        ]

    centre = shifted(0, 0, 0)
    second_x = shifted(1, 0, 0) + shifted(-1, 0, 0) - 2.0 * centre
    second_y = shifted(0, 1, 0) + shifted(0, -1, 0) - 2.0 * centre
    second_z = shifted(0, 0, 1) + shifted(0, 0, -1) - 2.0 * centre
    mixed_xy = 0.25 * (
        shifted(1, 1, 0) - shifted(1, -1, 0) - shifted(-1, 1, 0) + shifted(-1, -1, 0)
    )
    mixed_xz = 0.25 * (
        shifted(1, 0, 1) - shifted(1, 0, -1) - shifted(-1, 0, 1) + shifted(-1, 0, -1)
    )
    mixed_yz = 0.25 * (
        shifted(0, 1, 1) - shifted(0, 1, -1) - shifted(0, -1, 1) + shifted(0, -1, -1)
    )
    normal_x, normal_y, normal_z = (coef[0], coef[1], coef[2])
    speed, gain, root = (coef[3], coef[4], coef[5])
    along = (
        normal_x * normal_x * second_x
        + normal_y * normal_y * second_y
        + normal_z * normal_z * second_z
        + 2.0
        * (
            normal_x * normal_y * mixed_xy
            + normal_x * normal_z * mixed_xz
            + normal_y * normal_z * mixed_yz
        )
    )
    across = second_x + second_y + second_z - along
    pressure = centre[:, 0::2]
    auxiliary = centre[:, 1::2]
    rhs_p = gain * across[:, 0::2] + root * along[:, 1::2]
    rhs_q = root * across[:, 0::2] + along[:, 1::2]
    next_p = 2.0 * pressure - previous[:, 0::2] + speed * rhs_p
    next_q = 2.0 * auxiliary - previous[:, 1::2] + speed * rhs_q
    return jnp.stack([next_p, next_q], axis=2).reshape(centre.shape)


def depth_pad(array):
    return jnp.pad(array, ((0, 0), (0, 0), (0, 0), (0, 0), (1, 1)))


def local(wave_now, wave_prev, vel_coef, epsilon, delta, tilt, azimuth, aperture):
    coef = model_terms(vel_coef, epsilon, delta, tilt, azimuth)
    correlation = jnp.zeros(vel_coef.shape, jnp.float32)
    current, previous = (wave_now, wave_prev)
    for step in range(ITERS):
        widened_now = extended(current, (("gx", 2), ("gy", 3)), 1)
        fresh = advance(depth_pad(widened_now), previous, coef)
        correlation = correlation + fresh[0, 0] * fresh[0, 2]
        previous, current = (current, fresh)
    covered = aperture[0, 0, 0].astype(jnp.float32)
    image = lax.psum(covered * correlation, "shot") / ITERS
    return (current, image)


def solution(mesh):
    return jax.shard_map(
        local,
        mesh=mesh,
        in_specs=(
            P("shot", None, "gx", "gy", None),
            P("shot", None, "gx", "gy", None),
            P("gx", "gy", None),
            P("gx", "gy", None),
            P("gx", "gy", None),
            P("gx", "gy", None),
            P("gx", "gy", None),
            P("shot", "gx", "gy"),
        ),
        out_specs=(P("shot", None, "gx", "gy", None), P("gx", "gy", None)),
        check_vma=False,
    )
```

profile of v0, /device:TPU:28, one launch (start us, length us, event | category | flops | bytes accessed | tf_op | source)
XLA Modules:
  0.0 201.1 jit_solution(13523457433862075428)
XLA Ops:
  8.1 3.4 %collective-permute-start.1 = (f32[1,4,1,32,128]{4,3,2,1,0:T(8,128)S(1)}, f32[1,4,1,32,128]{4,3,2,1,0:T(8,128)S(1)}, u32[]{:S(2)}, u32[]{:S(2)}) collective-permute-start(f32[1,4,1,32,128]{4,3,2,1,0:T(8,128)S(1)} %get-tuple-element.39), channel_id=1, source_target_pairs={{0,2},{2,4},{4,6},{1,3},{3,5},{5,7},{8,10},{10,12},{12,14},{9,11},... | collective-permute-start | bytes 196616 | tf_op jit(solution)/shard_map/ppermute | solution.py:16
  11.5 3.5 %collective-permute-start = (f32[1,4,1,32,128]{4,3,2,1,0:T(8,128)S(1)}, f32[1,4,1,32,128]{4,3,2,1,0:T(8,128)S(1)}, u32[]{:S(2)}, u32[]{:S(2)}) collective-permute-start(f32[1,4,1,32,128]{4,3,2,1,0:T(8,128)S(1)} %get-tuple-element.38), channel_id=1, source_target_pairs={{2,0},{4,2},{6,4},{3,1},{5,3},{7,5},{10,8},{12,10},{14,12},{11,9},... | collective-permute-start | bytes 196616 | tf_op jit(solution)/shard_map/ppermute | solution.py:19
  15.0 6.1 %fusion.61 = (f32[32,32,128]{2,1,0:T(8,128)S(1)}, f32[32,32,128]{2,1,0:T(8,128)S(1)}, f32[32,32,128]{2,1,0:T(8,128)S(1)}, f32[32,32,128]{2,1,0:T(8,128)S(1)}, f3...) fusion(s32[32,32,128]{2,1,0:T(8,128)} %param.14, s32[32,32,128]{2,1,0:T(8,128)} %param.13), kind=kLoop, calls=%fused_computation.183 | loop fusion | flops 1966080 | bytes 4194304 | tf_op jit(solution)/shard_map/mul | solution.py:64
  23.0 3.0 %collective-permute-start.3 = (f32[1,4,34,1,128]{4,3,2,1,0:T(1,128)S(1)}, f32[1,4,34,1,128]{4,3,2,1,0:T(1,128)S(1)}, u32[]{:S(2)}, u32[]{:S(2)}) collective-permute-start(f32[1,4,34,1,128]{4,3,2,1,0:T(1,128)S(1)} %get-tuple-element.30), channel_id=1, source_target_pairs={{0,1},{2,3},{4,5},{6,7},{8,9},{10,11},{12,13},{14,15},{16,17},{18,... | collective-permute-start | bytes 208904 | tf_op jit(solution)/shard_map/ppermute | solution.py:16
  26.9 2.7 %select_maximum_fusion.12 = f32[1,4,34,34,130]{4,3,2,1,0:T(8,128)S(1)} fusion(f32[1,4,34,1,128]{4,3,2,1,0:T(1,128)S(1)} %collective-permute-done.2, f32[1,4,34,32,128]{4,3,2,1,0:T(8,128)S(1)} %constant_dynamic-update-slice_fusion, f32[1,4,34,1,128]{4,3,2,1,0:T(1,128)S(1)} %collective-permute-done.3), kind=kLoop, calls=%fused_computation.14 | loop fusion | flops 4808960 | bytes 4771968 | tf_op jit(solution)/shard_map/concatenate | solution.py:20
  29.7 8.4 %add_subtract_fusion.3 = (f32[1,4,32,32,128]{4,3,2,1,0:T(8,128)S(1)}, f32[1,4,32,32,128]{4,3,2,1,0:T(8,128)S(1)}) fusion(f32[1,4,32,32,128]{4,3,2,1,0:T(8,128)S(1)} %copy-done.2, f32[1,4,1,32,128]{4,3,2,1,0:T(8,128)S(1)} %collective-permute-done.1, f32[1,4,1,32,128]{4,3,2,1,0:T(8,128)S(1)} %collective-permute-done, ...), kind=kLoop, calls=%fused_computation.140 | loop fusion | flops 22544384 | bytes 32907264 | tf_op jit(solution)/shard_map/sub | solution.py:74
  38.2 2.5 %add_bitcast_fusion.7 = (f32[1,2,1,32,32,128]{5,4,3,1,2,0:T(8,128)S(1)}, f32[1,2,1,32,32,128]{5,4,3,1,2,0:T(8,128)S(1)}) fusion(f32[1,4,32,32,128]{4,3,2,1,0:T(8,128)} %param.9, f32[1,4,32,32,128]{4,3,2,1,0:T(8,128)S(1)} %get-tuple-element.9, f32[1,4,32,32,128]{4,3,2,1,0:T(8,128)S(1)} %get-tuple-element.8, f32[1,4,32,32,128]{4,3,2,1,0:T(8,128)S(1)} %copy-done.2, ...), kind=kLoop, calls=%fused_computation.148 | loop fusion | flops 3407872 | bytes 9961472 | tf_op jit(solution)/shard_map/stack | solution.py:81
  41.2 2.4 %collective-permute-start.4 = (f32[1,4,1,32,128]{4,3,2,1,0:T(8,128)S(1)}, f32[1,4,1,32,128]{4,3,2,1,0:T(8,128)S(1)}, u32[]{:S(2)}, u32[]{:S(2)}) collective-permute-start(f32[1,4,1,32,128]{4,3,2,1,0:T(8,128)S(1)} %get-tuple-element.36), channel_id=1, source_target_pairs={{2,0},{4,2},{6,4},{3,1},{5,3},{7,5},{10,8},{12,10},{14,12},{11,9},... | collective-permute-start | bytes 196616 | tf_op jit(solution)/shard_map/ppermute | solution.py:19
  43.6 3.4 %collective-permute-start.5 = (f32[1,4,1,32,128]{4,3,2,1,0:T(8,128)S(1)}, f32[1,4,1,32,128]{4,3,2,1,0:T(8,128)S(1)}, u32[]{:S(2)}, u32[]{:S(2)}) collective-permute-start(f32[1,4,1,32,128]{4,3,2,1,0:T(8,128)S(1)} %get-tuple-element.37), channel_id=1, source_target_pairs={{0,2},{2,4},{4,6},{1,3},{3,5},{5,7},{8,10},{10,12},{12,14},{9,11},... | collective-permute-start | bytes 196616 | tf_op jit(solution)/shard_map/ppermute | solution.py:16
  47.4 3.3 %collective-permute-done.5 = f32[1,4,1,32,128]{4,3,2,1,0:T(8,128)S(1)} collective-permute-done((f32[1,4,1,32,128]{4,3,2,1,0:T(8,128)S(1)}, f32[1,4,1,32,128]{4,3,2,1,0:T(8,128)S(1)}, u32[]{:S(2)}, u32[]{:S(2)}) %collective-permute-start.5) | collective-permute-done | bytes 65568 | tf_op jit(solution)/shard_map/ppermute | solution.py:16
  52.1 3.2 %collective-permute-start.7 = (f32[1,4,34,1,128]{4,3,2,1,0:T(1,128)S(1)}, f32[1,4,34,1,128]{4,3,2,1,0:T(1,128)S(1)}, u32[]{:S(2)}, u32[]{:S(2)}) collective-permute-start(f32[1,4,34,1,128]{4,3,2,1,0:T(1,128)S(1)} %get-tuple-element.29), channel_id=1, source_target_pairs={{0,1},{2,3},{4,5},{6,7},{8,9},{10,11},{12,13},{14,15},{16,17},{18,... | collective-permute-start | bytes 208904 | tf_op jit(solution)/shard_map/ppermute | solution.py:16
  56.0 3.6 %select_maximum_fusion.8 = f32[1,4,34,34,130]{4,3,2,1,0:T(8,128)S(1)} fusion(f32[1,4,34,1,128]{4,3,2,1,0:T(1,128)S(1)} %collective-permute-done.6, f32[1,4,34,1,128]{4,3,2,1,0:T(1,128)S(1)} %collective-permute-done.7, f32[1,4,1,32,128]{4,3,2,1,0:T(8,128)S(1)} %collective-permute-done.4, f32[1,4,32,32,128]{4,3,2,1,0:T(8,128)S(1)} %bitcast.25, ...), kind=kLoop, calls=%fused_computation.10 | loop fusion | flops 7213440 | bytes 4771968 | tf_op jit(solution)/shard_map/concatenate | solution.py:20
  59.6 3.0 %pad_maximum_fusion = (f32[1,4,34,33,128]{4,3,2,1,0:T(8,128)}, f32[1,4,34,33,128]{4,3,2,1,0:T(8,128)}) fusion(f32[1,4,34,1,128]{4,3,2,1,0:T(1,128)S(1)} %collective-permute-done.6, f32[1,4,1,32,128]{4,3,2,1,0:T(8,128)S(1)} %collective-permute-done.4, f32[1,4,32,32,128]{4,3,2,1,0:T(8,128)S(1)} %bitcast.26, ...), kind=kLoop, calls=%fused_computation.25 | loop fusion | flops 3446784 | bytes 6963200 | tf_op jit(solution)/shard_map/concatenate | solution.py:20
  62.5 11.2 %add_subtract_fusion.2 = (f32[1,4,32,32,128]{4,3,2,1,0:T(8,128)}, f32[1,4,32,32,128]{4,3,2,1,0:T(8,128)}) fusion(f32[1,4,32,32,128]{4,3,2,1,0:T(8,128)S(1)} %bitcast.27, f32[1,4,1,32,128]{4,3,2,1,0:T(8,128)S(1)} %collective-permute-done.5, f32[1,4,1,32,128]{4,3,2,1,0:T(8,128)S(1)} %collective-permute-done.4, f32[1,4,34,33,128]{4,3,2,1,0:T(8,128)} %get-tuple-element.27, ...), kind=kLoop, calls=%fused_computation.139 | loop fusion | flops 17301504 | bytes 43122688 | tf_op jit(solution)/shard_map/sub | solution.py:74
  73.7 3.0 %add_bitcast_fusion.5 = (f32[1,2,1,32,32,128]{5,4,3,1,2,0:T(8,128)S(1)}, f32[1,2,1,32,32,128]{5,4,3,1,2,0:T(8,128)S(1)}) fusion(f32[1,4,32,32,128]{4,3,2,1,0:T(8,128)} %get-tuple-element.7, f32[1,4,32,32,128]{4,3,2,1,0:T(8,128)} %get-tuple-element.6, f32[1,4,32,32,128]{4,3,2,1,0:T(8,128)S(1)} %bitcast.28, f32[1,4,32,32,128]{4,3,2,1,0:T(8,128)S(1)} %copy-done.2, ...), kind=kLoop, calls=%fused_computation.146 | loop fusion | flops 3407872 | bytes 9961472 | tf_op jit(solution)/shard_map/stack | solution.py:81
  77.1 1.9 collective-permute-start.8
  79.0 3.9 %collective-permute-start.9 = (f32[1,4,1,32,128]{4,3,2,1,0:T(8,128)S(1)}, f32[1,4,1,32,128]{4,3,2,1,0:T(8,128)S(1)}, u32[]{:S(2)}, u32[]{:S(2)}) collective-permute-start(f32[1,4,1,32,128]{4,3,2,1,0:T(8,128)S(1)} %get-tuple-element.35), channel_id=1, source_target_pairs={{0,2},{2,4},{4,6},{1,3},{3,5},{5,7},{8,10},{10,12},{12,14},{9,11},... | collective-permute-start | bytes 196616 | tf_op jit(solution)/shard_map/ppermute | solution.py:16
  83.3 2.8 %collective-permute-done.9 = f32[1,4,1,32,128]{4,3,2,1,0:T(8,128)S(1)} collective-permute-done((f32[1,4,1,32,128]{4,3,2,1,0:T(8,128)S(1)}, f32[1,4,1,32,128]{4,3,2,1,0:T(8,128)S(1)}, u32[]{:S(2)}, u32[]{:S(2)}) %collective-permute-start.9) | collective-permute-done | bytes 65568 | tf_op jit(solution)/shard_map/ppermute | solution.py:16
  87.6 3.0 %collective-permute-start.11 = (f32[1,4,34,1,128]{4,3,2,1,0:T(1,128)S(1)}, f32[1,4,34,1,128]{4,3,2,1,0:T(1,128)S(1)}, u32[]{:S(2)}, u32[]{:S(2)}) collective-permute-start(f32[1,4,34,1,128]{4,3,2,1,0:T(1,128)S(1)} %get-tuple-element.25), channel_id=1, source_target_pairs={{0,1},{2,3},{4,5},{6,7},{8,9},{10,11},{12,13},{14,15},{16,17},{18,... | collective-permute-start | bytes 208904 | tf_op jit(solution)/shard_map/ppermute | solution.py:16
  91.5 3.6 %select_maximum_fusion.4 = f32[1,4,34,34,130]{4,3,2,1,0:T(8,128)S(1)} fusion(f32[1,4,34,1,128]{4,3,2,1,0:T(1,128)S(1)} %collective-permute-done.10, f32[1,4,34,1,128]{4,3,2,1,0:T(1,128)S(1)} %collective-permute-done.11, f32[1,4,1,32,128]{4,3,2,1,0:T(8,128)S(1)} %collective-permute-done.8, f32[1,4,32,32,128]{4,3,2,1,0:T(8,128)S(1)} %bitcast.33, ...), kind=kLoop, calls=%fused_computation.6 | loop fusion | flops 7213440 | bytes 4771968 | tf_op jit(solution)/shard_map/concatenate | solution.py:20
  95.1 3.0 %pad_maximum_fusion.1 = (f32[1,4,34,33,128]{4,3,2,1,0:T(8,128)}, f32[1,4,34,33,128]{4,3,2,1,0:T(8,128)}) fusion(f32[1,4,34,1,128]{4,3,2,1,0:T(1,128)S(1)} %collective-permute-done.10, f32[1,4,1,32,128]{4,3,2,1,0:T(8,128)S(1)} %collective-permute-done.8, f32[1,4,32,32,128]{4,3,2,1,0:T(8,128)S(1)} %bitcast.34, ...), kind=kLoop, calls=%fused_computation.27 | loop fusion | flops 3446784 | bytes 6963200 | tf_op jit(solution)/shard_map/concatenate | solution.py:20
  98.1 11.2 %add_subtract_fusion.1 = (f32[1,4,32,32,128]{4,3,2,1,0:T(8,128)}, f32[1,4,32,32,128]{4,3,2,1,0:T(8,128)}) fusion(f32[1,4,32,32,128]{4,3,2,1,0:T(8,128)S(1)} %bitcast.35, f32[1,4,1,32,128]{4,3,2,1,0:T(8,128)S(1)} %collective-permute-done.9, f32[1,4,1,32,128]{4,3,2,1,0:T(8,128)S(1)} %collective-permute-done.8, f32[1,4,34,33,128]{4,3,2,1,0:T(8,128)} %get-tuple-element.23, ...), kind=kLoop, calls=%fused_computation.138 | loop fusion | flops 17301504 | bytes 43122688 | tf_op jit(solution)/shard_map/sub | solution.py:74
  109.3 3.0 %add_bitcast_fusion.3 = (f32[1,2,1,32,32,128]{5,4,3,1,2,0:T(8,128)S(1)}, f32[1,2,1,32,32,128]{5,4,3,1,2,0:T(8,128)S(1)}) fusion(f32[1,4,32,32,128]{4,3,2,1,0:T(8,128)} %get-tuple-element.5, f32[1,4,32,32,128]{4,3,2,1,0:T(8,128)} %get-tuple-element.4, f32[1,4,32,32,128]{4,3,2,1,0:T(8,128)S(1)} %bitcast.36, f32[1,4,32,32,128]{4,3,2,1,0:T(8,128)S(1)} %bitcast.29, ...), kind=kLoop, calls=%fused_computation.144 | loop fusion | flops 3407872 | bytes 9961472 | tf_op jit(solution)/shard_map/stack | solution.py:81
  112.7 1.9 collective-permute-start.12
  114.6 4.1 %collective-permute-start.13 = (f32[1,4,1,32,128]{4,3,2,1,0:T(8,128)S(1)}, f32[1,4,1,32,128]{4,3,2,1,0:T(8,128)S(1)}, u32[]{:S(2)}, u32[]{:S(2)}) collective-permute-start(f32[1,4,1,32,128]{4,3,2,1,0:T(8,128)S(1)} %get-tuple-element.33), channel_id=1, source_target_pairs={{0,2},{2,4},{4,6},{1,3},{3,5},{5,7},{8,10},{10,12},{12,14},{9,11},... | collective-permute-start | bytes 196616 | tf_op jit(solution)/shard_map/ppermute | solution.py:16
  118.9 3.0 %collective-permute-done.13 = f32[1,4,1,32,128]{4,3,2,1,0:T(8,128)S(1)} collective-permute-done((f32[1,4,1,32,128]{4,3,2,1,0:T(8,128)S(1)}, f32[1,4,1,32,128]{4,3,2,1,0:T(8,128)S(1)}, u32[]{:S(2)}, u32[]{:S(2)}) %collective-permute-start.13) | collective-permute-done | bytes 65568 | tf_op jit(solution)/shard_map/ppermute | solution.py:16
  123.4 3.0 %collective-permute-start.15 = (f32[1,4,34,1,128]{4,3,2,1,0:T(1,128)S(1)}, f32[1,4,34,1,128]{4,3,2,1,0:T(1,128)S(1)}, u32[]{:S(2)}, u32[]{:S(2)}) collective-permute-start(f32[1,4,34,1,128]{4,3,2,1,0:T(1,128)S(1)} %get-tuple-element.21), channel_id=1, source_target_pairs={{0,1},{2,3},{4,5},{6,7},{8,9},{10,11},{12,13},{14,15},{16,17},{18,... | collective-permute-start | bytes 208904 | tf_op jit(solution)/shard_map/ppermute | solution.py:16
  127.3 3.6 %select_maximum_fusion = f32[1,4,34,34,130]{4,3,2,1,0:T(8,128)S(1)} fusion(f32[1,4,34,1,128]{4,3,2,1,0:T(1,128)S(1)} %collective-permute-done.14, f32[1,4,34,1,128]{4,3,2,1,0:T(1,128)S(1)} %collective-permute-done.15, f32[1,4,1,32,128]{4,3,2,1,0:T(8,128)S(1)} %collective-permute-done.12, f32[1,4,32,32,128]{4,3,2,1,0:T(8,128)S(1)} %bitcast.41, ...), kind=kLoop, calls=%fused_computation.2 | loop fusion | flops 7213440 | bytes 4771968 | tf_op jit(solution)/shard_map/concatenate | solution.py:20
  130.9 3.0 %pad_maximum_fusion.2 = (f32[1,4,34,33,128]{4,3,2,1,0:T(8,128)}, f32[1,4,34,33,128]{4,3,2,1,0:T(8,128)}) fusion(f32[1,4,34,1,128]{4,3,2,1,0:T(1,128)S(1)} %collective-permute-done.14, f32[1,4,1,32,128]{4,3,2,1,0:T(8,128)S(1)} %collective-permute-done.12, f32[1,4,32,32,128]{4,3,2,1,0:T(8,128)S(1)} %bitcast.42, ...), kind=kLoop, calls=%fused_computation.29 | loop fusion | flops 3446784 | bytes 6963200 | tf_op jit(solution)/shard_map/concatenate | solution.py:20
  133.9 13.1 %add_subtract_fusion = (f32[1,4,32,32,128]{4,3,2,1,0:T(8,128)}, f32[1,4,32,32,128]{4,3,2,1,0:T(8,128)}) fusion(f32[1,4,32,32,128]{4,3,2,1,0:T(8,128)} %bitcast.43, f32[1,4,1,32,128]{4,3,2,1,0:T(8,128)S(1)} %collective-permute-done.13, f32[1,4,1,32,128]{4,3,2,1,0:T(8,128)S(1)} %collective-permute-done.12, f32[1,4,34,33,128]{4,3,2,1,0:T(8,128)} %get-tuple-element.19, ...), kind=kLoop, calls=%fused_computation.137 | loop fusion | flops 17301504 | bytes 43122688 | tf_op jit(solution)/shard_map/sub | solution.py:74
  146.9 3.6 %add_bitcast_fusion.1 = (f32[1,2,1,32,32,128]{5,4,3,1,2,0:T(8,128)S(1)}, f32[1,2,1,32,32,128]{5,4,3,1,2,0:T(8,128)S(1)}) fusion(f32[1,4,32,32,128]{4,3,2,1,0:T(8,128)} %bitcast.44, f32[1,4,32,32,128]{4,3,2,1,0:T(8,128)} %get-tuple-element.3, f32[1,4,32,32,128]{4,3,2,1,0:T(8,128)} %get-tuple-element.2, f32[1,4,32,32,128]{4,3,2,1,0:T(8,128)S(1)} %bitcast.37, ...), kind=kLoop, calls=%fused_computation.142 | loop fusion | flops 3407872 | bytes 9961472 | tf_op jit(solution)/shard_map/stack | solution.py:81
  154.4 38.0 %all-reduce.6.cloned.1.call-done = f32[32,32,128]{2,1,0:T(8,128)} async-done(((f32[32,32,128]{2,1,0:T(8,128)}), f32[32,32,128]{2,1,0:T(8,128)}) %all-reduce.6.cloned.1.call-update) | async-done | bytes 524304 | tf_op jit(solution)/shard_map/psum | solution.py:98
  (71 shorter events, 17.3 us)
Async XLA Ops:
  7.2 185.2 %all-reduce.6.cloned.1.call-start = ((), (), s32[]{:S(2)}) async-start(), calls=%async_computation | async-start | bytes 1048576 | tf_op jit(solution)/shard_map/psum | solution.py:98
  8.1 13.0 %collective-permute-start.1 = (f32[1,4,1,32,128]{4,3,2,1,0:T(8,128)S(1)}, f32[1,4,1,32,128]{4,3,2,1,0:T(8,128)S(1)}, u32[]{:S(2)}, u32[]{:S(2)}) collective-permute-start(f32[1,4,1,32,128]{4,3,2,1,0:T(8,128)S(1)} %get-tuple-element.39), channel_id=1, source_target_pairs={{0,2},{2,4},{4,6},{1,3},{3,5},{5,7},{8,10},{10,12},{12,14},{9,11},... | collective-permute-start | bytes 196616 | tf_op jit(solution)/shard_map/ppermute | solution.py:16
  11.5 9.7 %copy-start.2 = (f32[1,4,32,32,128]{4,3,2,1,0:T(8,128)S(1)}, f32[1,4,32,32,128]{4,3,2,1,0:T(8,128)}, u32[]{:S(2)}) copy-start(f32[1,4,32,32,128]{4,3,2,1,0:T(8,128)} %param.8) | copy-start | bytes 6291460
  11.5 9.9 %collective-permute-start = (f32[1,4,1,32,128]{4,3,2,1,0:T(8,128)S(1)}, f32[1,4,1,32,128]{4,3,2,1,0:T(8,128)S(1)}, u32[]{:S(2)}, u32[]{:S(2)}) collective-permute-start(f32[1,4,1,32,128]{4,3,2,1,0:T(8,128)S(1)} %get-tuple-element.38), channel_id=1, source_target_pairs={{2,0},{4,2},{6,4},{3,1},{5,3},{7,5},{10,8},{12,10},{14,12},{11,9},... | collective-permute-start | bytes 196616 | tf_op jit(solution)/shard_map/ppermute | solution.py:19
  21.1 8.6 %copy-start.3 = (f32[32,32,128]{2,1,0:T(8,128)}, f32[32,32,128]{2,1,0:T(8,128)S(1)}, u32[]{:S(2)}) copy-start(f32[32,32,128]{2,1,0:T(8,128)S(1)} %get-tuple-element.40) | copy-start | bytes 1572868
  21.1 8.6 %copy-start.4 = (f32[32,32,128]{2,1,0:T(8,128)}, f32[32,32,128]{2,1,0:T(8,128)S(1)}, u32[]{:S(2)}) copy-start(f32[32,32,128]{2,1,0:T(8,128)S(1)} %get-tuple-element.41) | copy-start | bytes 1572868
  21.1 8.6 %copy-start.5 = (f32[32,32,128]{2,1,0:T(8,128)}, f32[32,32,128]{2,1,0:T(8,128)S(1)}, u32[]{:S(2)}) copy-start(f32[32,32,128]{2,1,0:T(8,128)S(1)} %get-tuple-element.42) | copy-start | bytes 1572868
  21.1 8.6 %copy-start.6 = (f32[32,32,128]{2,1,0:T(8,128)}, f32[32,32,128]{2,1,0:T(8,128)S(1)}, u32[]{:S(2)}) copy-start(f32[32,32,128]{2,1,0:T(8,128)S(1)} %get-tuple-element.43) | copy-start | bytes 1572868
  21.1 8.6 %copy-start.7 = (f32[32,32,128]{2,1,0:T(8,128)}, f32[32,32,128]{2,1,0:T(8,128)S(1)}, u32[]{:S(2)}) copy-start(f32[32,32,128]{2,1,0:T(8,128)S(1)} %get-tuple-element.44) | copy-start | bytes 1572868
  21.1 8.6 %copy-start.8 = (f32[32,32,128]{2,1,0:T(8,128)}, f32[32,32,128]{2,1,0:T(8,128)S(1)}, u32[]{:S(2)}) copy-start(f32[32,32,128]{2,1,0:T(8,128)S(1)} %get-tuple-element.45) | copy-start | bytes 1572868
  21.2 4.9 %copy-start.13 = (f32[32,32,128]{2,1,0:T(8,128)S(1)}, f32[32,32,128]{2,1,0:T(8,128)}, u32[]{:S(2)}) copy-start(f32[32,32,128]{2,1,0:T(8,128)} %param.12) | copy-start | bytes 1572868
  21.2 4.9 %copy-start.14 = (f32[32,32,128]{2,1,0:T(8,128)S(1)}, f32[32,32,128]{2,1,0:T(8,128)}, u32[]{:S(2)}) copy-start(f32[32,32,128]{2,1,0:T(8,128)} %param.11) | copy-start | bytes 1572868
  21.6 4.7 %collective-permute-start.2 = (f32[1,4,34,1,128]{4,3,2,1,0:T(1,128)S(1)}, f32[1,4,34,1,128]{4,3,2,1,0:T(1,128)S(1)}, u32[]{:S(2)}, u32[]{:S(2)}) collective-permute-start(f32[1,4,34,1,128]{4,3,2,1,0:T(1,128)S(1)} %get-tuple-element.31), channel_id=1, source_target_pairs={{1,0},{3,2},{5,4},{7,6},{9,8},{11,10},{13,12},{15,14},{17,16},{19,... | collective-permute-start | bytes 208904 | tf_op jit(solution)/shard_map/ppermute | solution.py:19
  23.0 3.9 %collective-permute-start.3 = (f32[1,4,34,1,128]{4,3,2,1,0:T(1,128)S(1)}, f32[1,4,34,1,128]{4,3,2,1,0:T(1,128)S(1)}, u32[]{:S(2)}, u32[]{:S(2)}) collective-permute-start(f32[1,4,34,1,128]{4,3,2,1,0:T(1,128)S(1)} %get-tuple-element.30), channel_id=1, source_target_pairs={{0,1},{2,3},{4,5},{6,7},{8,9},{10,11},{12,13},{14,15},{16,17},{18,... | collective-permute-start | bytes 208904 | tf_op jit(solution)/shard_map/ppermute | solution.py:16
  26.3 11.9 %copy-start.9 = (f32[32,32,128]{2,1,0:T(8,128)}, f32[32,32,128]{2,1,0:T(8,128)S(1)}, u32[]{:S(2)}) copy-start(f32[32,32,128]{2,1,0:T(8,128)S(1)} %get-tuple-element.46) | copy-start | bytes 1572868
  26.3 11.9 %copy-start.10 = (f32[32,32,128]{2,1,0:T(8,128)}, f32[32,32,128]{2,1,0:T(8,128)S(1)}, u32[]{:S(2)}) copy-start(f32[32,32,128]{2,1,0:T(8,128)S(1)} %get-tuple-element.47) | copy-start | bytes 1572868
  29.7 8.5 %copy-start.11 = (f32[32,32,128]{2,1,0:T(8,128)S(1)}, f32[32,32,128]{2,1,0:T(8,128)}, u32[]{:S(2)}) copy-start(f32[32,32,128]{2,1,0:T(8,128)} %param.10) | copy-start | bytes 1572868
  41.2 6.2 %collective-permute-start.4 = (f32[1,4,1,32,128]{4,3,2,1,0:T(8,128)S(1)}, f32[1,4,1,32,128]{4,3,2,1,0:T(8,128)S(1)}, u32[]{:S(2)}, u32[]{:S(2)}) collective-permute-start(f32[1,4,1,32,128]{4,3,2,1,0:T(8,128)S(1)} %get-tuple-element.36), channel_id=1, source_target_pairs={{2,0},{4,2},{6,4},{3,1},{5,3},{7,5},{10,8},{12,10},{14,12},{11,9},... | collective-permute-start | bytes 196616 | tf_op jit(solution)/shard_map/ppermute | solution.py:19
  43.6 7.1 %collective-permute-start.5 = (f32[1,4,1,32,128]{4,3,2,1,0:T(8,128)S(1)}, f32[1,4,1,32,128]{4,3,2,1,0:T(8,128)S(1)}, u32[]{:S(2)}, u32[]{:S(2)}) collective-permute-start(f32[1,4,1,32,128]{4,3,2,1,0:T(8,128)S(1)} %get-tuple-element.37), channel_id=1, source_target_pairs={{0,2},{2,4},{4,6},{1,3},{3,5},{5,7},{8,10},{10,12},{12,14},{9,11},... | collective-permute-start | bytes 196616 | tf_op jit(solution)/shard_map/ppermute | solution.py:16
  50.8 4.5 %collective-permute-start.6 = (f32[1,4,34,1,128]{4,3,2,1,0:T(1,128)S(1)}, f32[1,4,34,1,128]{4,3,2,1,0:T(1,128)S(1)}, u32[]{:S(2)}, u32[]{:S(2)}) collective-permute-start(f32[1,4,34,1,128]{4,3,2,1,0:T(1,128)S(1)} %get-tuple-element.28), channel_id=1, source_target_pairs={{1,0},{3,2},{5,4},{7,6},{9,8},{11,10},{13,12},{15,14},{17,16},{19,... | collective-permute-start | bytes 208904 | tf_op jit(solution)/shard_map/ppermute | solution.py:19
  52.1 3.9 %collective-permute-start.7 = (f32[1,4,34,1,128]{4,3,2,1,0:T(1,128)S(1)}, f32[1,4,34,1,128]{4,3,2,1,0:T(1,128)S(1)}, u32[]{:S(2)}, u32[]{:S(2)}) collective-permute-start(f32[1,4,34,1,128]{4,3,2,1,0:T(1,128)S(1)} %get-tuple-element.29), channel_id=1, source_target_pairs={{0,1},{2,3},{4,5},{6,7},{8,9},{10,11},{12,13},{14,15},{16,17},{18,... | collective-permute-start | bytes 208904 | tf_op jit(solution)/shard_map/ppermute | solution.py:16
  77.1 6.2 %collective-permute-start.8 = (f32[1,4,1,32,128]{4,3,2,1,0:T(8,128)S(1)}, f32[1,4,1,32,128]{4,3,2,1,0:T(8,128)S(1)}, u32[]{:S(2)}, u32[]{:S(2)}) collective-permute-start(f32[1,4,1,32,128]{4,3,2,1,0:T(8,128)S(1)} %get-tuple-element.34), channel_id=1, source_target_pairs={{2,0},{4,2},{6,4},{3,1},{5,3},{7,5},{10,8},{12,10},{14,12},{11,9},... | collective-permute-start | bytes 196616 | tf_op jit(solution)/shard_map/ppermute | solution.py:19
  79.0 7.1 %collective-permute-start.9 = (f32[1,4,1,32,128]{4,3,2,1,0:T(8,128)S(1)}, f32[1,4,1,32,128]{4,3,2,1,0:T(8,128)S(1)}, u32[]{:S(2)}, u32[]{:S(2)}) collective-permute-start(f32[1,4,1,32,128]{4,3,2,1,0:T(8,128)S(1)} %get-tuple-element.35), channel_id=1, source_target_pairs={{0,2},{2,4},{4,6},{1,3},{3,5},{5,7},{8,10},{10,12},{12,14},{9,11},... | collective-permute-start | bytes 196616 | tf_op jit(solution)/shard_map/ppermute | solution.py:16
  86.3 4.3 %collective-permute-start.10 = (f32[1,4,34,1,128]{4,3,2,1,0:T(1,128)S(1)}, f32[1,4,34,1,128]{4,3,2,1,0:T(1,128)S(1)}, u32[]{:S(2)}, u32[]{:S(2)}) collective-permute-start(f32[1,4,34,1,128]{4,3,2,1,0:T(1,128)S(1)} %get-tuple-element.24), channel_id=1, source_target_pairs={{1,0},{3,2},{5,4},{7,6},{9,8},{11,10},{13,12},{15,14},{17,16},{19,... | collective-permute-start | bytes 208904 | tf_op jit(solution)/shard_map/ppermute | solution.py:19
  87.6 3.9 %collective-permute-start.11 = (f32[1,4,34,1,128]{4,3,2,1,0:T(1,128)S(1)}, f32[1,4,34,1,128]{4,3,2,1,0:T(1,128)S(1)}, u32[]{:S(2)}, u32[]{:S(2)}) collective-permute-start(f32[1,4,34,1,128]{4,3,2,1,0:T(1,128)S(1)} %get-tuple-element.25), channel_id=1, source_target_pairs={{0,1},{2,3},{4,5},{6,7},{8,9},{10,11},{12,13},{14,15},{16,17},{18,... | collective-permute-start | bytes 208904 | tf_op jit(solution)/shard_map/ppermute | solution.py:16
  112.6 18.2 %copy-start = (f32[1,2,2,32,32,128]{5,4,3,2,1,0:T(8,128)}, f32[1,2,2,32,32,128]{5,4,3,2,1,0:T(8,128)S(1)}, u32[]{:S(2)}) copy-start(f32[1,2,2,32,32,128]{5,4,3,2,1,0:T(8,128)S(1)} %copy.14) | copy-start | bytes 6291460
  112.7 6.2 %collective-permute-start.12 = (f32[1,4,1,32,128]{4,3,2,1,0:T(8,128)S(1)}, f32[1,4,1,32,128]{4,3,2,1,0:T(8,128)S(1)}, u32[]{:S(2)}, u32[]{:S(2)}) collective-permute-start(f32[1,4,1,32,128]{4,3,2,1,0:T(8,128)S(1)} %get-tuple-element.32), channel_id=1, source_target_pairs={{2,0},{4,2},{6,4},{3,1},{5,3},{7,5},{10,8},{12,10},{14,12},{11,9},... | collective-permute-start | bytes 196616 | tf_op jit(solution)/shard_map/ppermute | solution.py:19
  114.6 7.4 %collective-permute-start.13 = (f32[1,4,1,32,128]{4,3,2,1,0:T(8,128)S(1)}, f32[1,4,1,32,128]{4,3,2,1,0:T(8,128)S(1)}, u32[]{:S(2)}, u32[]{:S(2)}) collective-permute-start(f32[1,4,1,32,128]{4,3,2,1,0:T(8,128)S(1)} %get-tuple-element.33), channel_id=1, source_target_pairs={{0,2},{2,4},{4,6},{1,3},{3,5},{5,7},{8,10},{10,12},{12,14},{9,11},... | collective-permute-start | bytes 196616 | tf_op jit(solution)/shard_map/ppermute | solution.py:16
  122.1 5.0 %collective-permute-start.14 = (f32[1,4,34,1,128]{4,3,2,1,0:T(1,128)S(1)}, f32[1,4,34,1,128]{4,3,2,1,0:T(1,128)S(1)}, u32[]{:S(2)}, u32[]{:S(2)}) collective-permute-start(f32[1,4,34,1,128]{4,3,2,1,0:T(1,128)S(1)} %get-tuple-element.20), channel_id=1, source_target_pairs={{1,0},{3,2},{5,4},{7,6},{9,8},{11,10},{13,12},{15,14},{17,16},{19,... | collective-permute-start | bytes 208904 | tf_op jit(solution)/shard_map/ppermute | solution.py:19
  123.4 3.9 %collective-permute-start.15 = (f32[1,4,34,1,128]{4,3,2,1,0:T(1,128)S(1)}, f32[1,4,34,1,128]{4,3,2,1,0:T(1,128)S(1)}, u32[]{:S(2)}, u32[]{:S(2)}) collective-permute-start(f32[1,4,34,1,128]{4,3,2,1,0:T(1,128)S(1)} %get-tuple-element.21), channel_id=1, source_target_pairs={{0,1},{2,3},{4,5},{6,7},{8,9},{10,11},{12,13},{14,15},{16,17},{18,... | collective-permute-start | bytes 208904 | tf_op jit(solution)/shard_map/ppermute | solution.py:16
  150.7 2.3 %copy-start.1 = (f32[1,2,2,32,32,128]{5,4,3,2,1,0:T(8,128)S(1)}, f32[1,2,2,32,32,128]{5,4,3,2,1,0:T(8,128)}, u32[]{:S(2)}) copy-start(f32[1,2,2,32,32,128]{5,4,3,2,1,0:T(8,128)} %copy-done) | copy-start | bytes 6291460
  150.9 1.3 copy-start.12
Sparse Core Ops, SparseCore 0:
  154.5 37.8 all-reduce.5
where the time goes:
time: 205 us; the launch traced here: 201 us
  other arithmetic  88.9 us (43%)
  waiting for transfers between devices  50.5 us (25%)
  starting transfers between devices  42.3 us (21%)
  between operations  15.3 us (7%)
  local copies, waits for them, and re-layouts  4.16 us (2%)
    sub x4, other arithmetic, advance(): across = second_x + second_y + second_z - along  44 us
    psum x1, waiting for transfers between devices, local(): image = lax.psum(covered * correlation, 'shot') / ITERS  38 us
    ppermute x8, starting transfers between devices, extended(): lax.ppermute(lax.slice_in_dim(block, block.shape[dim] - width, None, axis...  27.2 us
    concatenate x7, other arithmetic, extended(): block = jnp.concatenate([low, block, high], axis=dim)  22.4 us
    ppermute x8, starting transfers between devices, extended(): lax.ppermute(lax.slice_in_dim(block, 0, width, axis=dim), axis, backward)  15.1 us
    another operation x8, other arithmetic, advance(): return jnp.stack([next_p, next_q], axis=2).reshape(centre.shape)  12.8 us
    ppermute x8, waiting for transfers between devices, extended(): lax.ppermute(lax.slice_in_dim(block, block.shape[dim] - width, None, axis...  11.6 us
    mul x1, other arithmetic, advance(): normal_x * normal_x * second_x + normal_y * normal_y * second_y  6.06 us
  transfers between devices with their start and end apart: 17, of which 11 were waited for; matrix products, arithmetic and copies ran while one was open for 3% of the time, Pallas kernels for 0%

commit v1 on v0

v1 whole, which is shorter than its diff:
```python
import functools
import math

import jax
import jax.numpy as jnp
from jax import lax
from jax.experimental import pallas as pl
from jax.experimental.pallas import tpu as pltpu
from jax.sharding import PartitionSpec as P

ITERS = 4
LANES = 128
TILE = 8
F32 = jnp.float32


def sin_cos(degrees):
    quadrant = jnp.floor(degrees * (1.0 / 90.0) + 0.5)
    angle = (degrees - 90.0 * quadrant) * (math.pi / 180.0)
    square = angle * angle
    sine = angle * (1.0 + square * (-1.0 / 6 + square * (1.0 / 120 + square * (-1.0 / 5040 + square * (1.0 / 362880)))))
    cosine = 1.0 + square * (
        -0.5 + square * (1.0 / 24 + square * (-1.0 / 720 + square * (1.0 / 40320 + square * (-1.0 / 3628800))))
    )
    turn = quadrant - 4.0 * jnp.floor(quadrant * 0.25)
    odd = (turn == 1.0) | (turn == 3.0)
    first = jnp.where(odd, cosine, sine)
    second = jnp.where(odd, sine, cosine)
    return (
        jnp.where(turn >= 2.0, -first, first),
        jnp.where((turn == 1.0) | (turn == 2.0), -second, second),
    )


def model_rows(vel, eps, delta, tilt, azimuth):
    sin_t, cos_t = sin_cos(tilt)
    sin_a, cos_a = sin_cos(azimuth)
    nx, ny, nz = sin_t * cos_a, sin_t * sin_a, cos_t
    gain = 1.0 + 2.0 * eps
    root = jnp.sqrt(1.0 + 2.0 * delta)
    return (
        nx * nx,
        ny * ny,
        nz * nz,
        0.5 * nx * ny,
        0.5 * nx * nz,
        0.5 * ny * nz,
        vel * gain,
        vel * root,
        vel,
    )


def sweep(src, dst, coef, corr, start, count, group, corr_scale=None):
    rows = coef.shape[2]
    lane = lax.broadcasted_iota(jnp.int32, (TILE, LANES), 1)
    first_lane, last_lane = lane == 0, lane == LANES - 1

    def neighbours(value):
        after = jnp.where(last_lane, 0.0, pltpu.roll(value, LANES - 1, 1))
        before = jnp.where(first_lane, 0.0, pltpu.roll(value, 1, 1))
        return after, before

    for pair in range(2):
        for tile in range(rows // TILE):
            row = TILE + tile * TILE

            def plane(field, x):
                centre = src[field, x, row : row + TILE, :]
                above = src[field, x, row + 1 : row + 1 + TILE, :]
                below = src[field, x, row - 1 : row - 1 + TILE, :]
                after, before = neighbours(centre)
                return centre, above - below, after - before, above + below, after + before

            def one(x, carry):
                terms = []
                following = []
                for index in range(2):
                    old, now = carry[index]
                    new = plane(2 * pair + index, x + 1)
                    a, b, c, d, e, g = [coef[i, x, row - TILE : row, :] for i in range(6)]
                    centre, slope_y, _, sum_y, sum_z = now
                    after, before = neighbours(slope_y)
                    twice = centre + centre
                    sum_x = new[0] + old[0]
                    along = (
                        (a * sum_x + b * sum_y)
                        + (c * sum_z - twice)
                        + (d * (new[1] - old[1]) + e * (new[2] - old[2]))
                        + g * (after - before)
                    )
                    laplace = (sum_x + sum_y) + (sum_z - 3.0 * twice) if index == 0 else None
                    terms.append((along, laplace, twice))
                    following.append((now[:3], new))
                (along_p, laplace, twice_p), (along_q, _, twice_q) = terms
                across = laplace - along_p
                vg, vr, v = [coef[i, x, row - TILE : row, :] for i in range(6, 9)]
                p, q = 2 * pair, 2 * pair + 1
                here = (x, slice(row, row + TILE), slice(None))
                new_p = (twice_p - dst[(p,) + here]) + (vg * across + vr * along_q)
                new_q = (twice_q - dst[(q,) + here]) + (vr * across + v * along_q)
                dst[(p,) + here] = new_p
                dst[(q,) + here] = new_q
                if pair == 1:
                    spot = (x, slice(row - TILE, row), slice(None))
                    total = corr[spot] + dst[(0,) + here] * new_p
                    corr[spot] = total
                return tuple(following)

            carry = tuple(
                (plane(2 * pair + index, start - 1)[:3], plane(2 * pair + index, start)) for index in range(2)
            )
            loops = count // group if count > group else 0
            if loops:

                def body(i, carry):
                    for j in range(group):
                        carry = one(start + i * group + j, carry)
                    return carry

                carry = lax.fori_loop(0, loops, body, carry)
            for j in range(loops * group, count):
                carry = one(start + j, carry)


def own_row(second):
    return pl.multiple_of(TILE + TILE * second, TILE)


def copies(pairs, sems):
    out = []
    for i, (source, target) in enumerate(pairs):
        out.append(pltpu.make_async_copy(source, target, sems.at[i]))
        out[-1].start()
    return out


def inner_kernel(
    flags, now, prev, vel, eps, delta, tilt, azimuth, border,
    wave, edge_a, edge_b, edge_c, edge_corr, image,
    buf_a, buf_b, coef, corr, raw, raw_int, raw_border, picture, sems,
):
    second, cover = flags[0], flags[1]
    width_x, width_y = vel.shape[0], vel.shape[1]
    oy = own_row(second)
    hy = pl.multiple_of(TILE + width_y * (1 - second), TILE)
    own = pl.ds(oy, width_y)
    hal = pl.ds(hy, TILE)
    model = copies(
        [
            (vel, raw.at[0]),
            (eps, raw.at[1]),
            (delta, raw.at[2]),
            (tilt, raw_int.at[0]),
            (azimuth, raw_int.at[1]),
            (border.at[pl.ds(8, 5)], raw_border),
        ],
        sems,
    )
    waves = copies(
        [
            (now.at[0], buf_a.at[:, :, own]),
            (prev.at[0], buf_b.at[:, :, own]),
            (border.at[pl.ds(0, 4)], buf_a.at[:, :, hal]),
            (border.at[pl.ds(4, 4)], buf_b.at[:, :, hal]),
        ],
        sems.at[pl.ds(6, 4)],
    )
    pad = jnp.zeros((4, width_x, TILE, LANES), F32)
    for buf in (buf_a, buf_b):
        buf[:, :, 0:TILE, :] = pad
        buf[:, :, TILE + coef.shape[2] :, :] = pad
    corr[...] = jnp.zeros_like(corr)
    for copy in model:
        copy.wait()

    def fill(x, _):
        for tile in range(width_y // TILE):
            rows = slice(tile * TILE, (tile + 1) * TILE)
            parts = model_rows(
                raw[0, x, rows, :],
                raw[1, x, rows, :],
                raw[2, x, rows, :],
                raw_int[0, x, rows, :].astype(F32),
                raw_int[1, x, rows, :].astype(F32),
            )
            for i, part in enumerate(parts):
                coef[i, x, pl.ds(oy - TILE + tile * TILE, TILE), :] = part
        parts = model_rows(*[raw_border[i, x] for i in range(5)])
        for i, part in enumerate(parts):
            coef[i, x, pl.ds(hy - TILE, TILE), :] = part
        return 0

    lax.fori_loop(0, width_x, fill, 0)
    for copy in waves:
        copy.wait()
    bufs = (buf_a, buf_b)
    for step in range(ITERS):
        sweep(bufs[step % 2], bufs[1 - step % 2], coef, corr, 1 + step, width_x - 2 - 2 * step, 3)
    last = bufs[ITERS % 2]
    inside = pl.ds(ITERS, width_x - 2 * ITERS)
    ends = (0, width_x - ITERS)
    pairs = [(last.at[:, inside, own], wave.at[0, :, inside])]
    middle = pl.ds(TILE, coef.shape[2])
    for side in range(2):
        at = pl.ds(ends[side], ITERS)
        wider = pl.ds(ends[side] - side, ITERS + 1)
        pairs += [
            (buf_a.at[:, at, middle], edge_a.at[side]),
            (buf_b.at[:, wider, middle], edge_b.at[side]),
            (coef.at[:, at], edge_c.at[side]),
            (corr.at[at], edge_corr.at[side]),
        ]
    out = copies(pairs, sems)
    scale = cover.astype(F32) / ITERS
    for tile in range(width_y // TILE):
        rows = pl.ds(oy - TILE + tile * TILE, TILE)
        picture[:, tile * TILE : (tile + 1) * TILE, :] = scale * corr[ITERS : width_x - ITERS, rows, :]
    final = pltpu.make_async_copy(picture, image, sems.at[len(pairs)])
    final.start()
    for copy in out:
        copy.wait()
    final.wait()


def border_kernel(
    flags, edge_a, edge_b, edge_c, edge_corr, halo, corner, wave_in,
    wave, image,
    buf_a, buf_b, coef, corr, raw, raw_corner, picture, sems,
):
    second, cover = flags[0], flags[1]
    width_x, width_y = wave.shape[2], wave.shape[3]
    oy = own_row(second)
    hy = pl.multiple_of(TILE + width_y * (1 - second), TILE)
    own = pl.ds(oy, width_y)
    hal = pl.ds(hy, TILE)
    middle = pl.ds(TILE, coef.shape[2])
    fields = 4
    n_now, n_prev = fields * ITERS, fields * (ITERS - 1)
    scale = cover.astype(F32) / ITERS
    pad = jnp.zeros((4, buf_a.shape[1], TILE, LANES), F32)
    for buf in (buf_a, buf_b):
        buf[:, :, 0:TILE, :] = pad
        buf[:, :, TILE + coef.shape[2] :, :] = pad
    for side in range(2):
        own_a, own_b = (ITERS, ITERS) if side == 0 else (1, 0)
        halo_a, halo_b = (0, 1) if side == 0 else (ITERS + 1, ITERS + 1)
        pairs = [
            (edge_a.at[side], buf_a.at[:, pl.ds(own_a, ITERS), middle]),
            (edge_b.at[side], buf_b.at[:, pl.ds(own_b, ITERS + 1), middle]),
            (edge_c.at[side], coef.at[:, pl.ds(own_a, ITERS)]),
            (edge_corr.at[side], corr.at[pl.ds(own_a, ITERS)]),
            (halo.at[side, pl.ds(n_now + n_prev, 5 * (ITERS - 1))], raw),
            (corner.at[side, pl.ds(n_now + n_prev, 5 * (ITERS - 1))], raw_corner),
        ]
        for f in range(fields):
            pairs += [
                (halo.at[side, pl.ds(f * ITERS, ITERS)], buf_a.at[f, pl.ds(halo_a, ITERS), own]),
                (corner.at[side, pl.ds(f * ITERS, ITERS)], buf_a.at[f, pl.ds(halo_a, ITERS), hal]),
                (
                    halo.at[side, pl.ds(n_now + f * (ITERS - 1), ITERS - 1)],
                    buf_b.at[f, pl.ds(halo_b, ITERS - 1), own],
                ),
                (
                    corner.at[side, pl.ds(n_now + f * (ITERS - 1), ITERS - 1)],
                    buf_b.at[f, pl.ds(halo_b, ITERS - 1), hal],
                ),
            ]
        for copy in copies(pairs, sems):
            copy.wait()
        for j in range(ITERS - 1):
            for tile in range(width_y // TILE):
                rows = slice(tile * TILE, (tile + 1) * TILE)
                parts = model_rows(*[raw[i * (ITERS - 1) + j, rows, :] for i in range(5)])
                for i, part in enumerate(parts):
                    coef[i, halo_b + j, pl.ds(oy - TILE + tile * TILE, TILE), :] = part
            parts = model_rows(*[raw_corner[i * (ITERS - 1) + j] for i in range(5)])
            for i, part in enumerate(parts):
                coef[i, halo_b + j, pl.ds(hy - TILE, TILE), :] = part
        bufs = (buf_a, buf_b)
        for step in range(ITERS):
            start = step + 1 if side == 0 else ITERS - step
            sweep(bufs[step % 2], bufs[1 - step % 2], coef, corr, start, ITERS, ITERS)
        last = bufs[ITERS % 2]
        for tile in range(width_y // TILE):
            rows = pl.ds(oy - TILE + tile * TILE, TILE)
            picture[side, :, tile * TILE : (tile + 1) * TILE, :] = scale * corr[own_a : own_a + ITERS, rows, :]
        target = pl.ds(0 if side == 0 else width_x - ITERS, ITERS)
        for copy in copies(
            [
                (last.at[:, pl.ds(own_a, ITERS), own], wave.at[0, :, target]),
                (picture.at[side], image.at[side]),
            ],
            sems,
        ):
            copy.wait()


def any_specs(count):
    return [pl.BlockSpec(memory_space=pl.ANY)] * count


def advance_inner(flags, now, prev, vel, eps, delta, tilt, azimuth, border):
    width_x, width_y = vel.shape[0], vel.shape[1]
    rows = width_y + TILE
    tall = rows + 2 * TILE
    shape = functools.partial(jax.ShapeDtypeStruct, dtype=F32)
    return pl.pallas_call(
        inner_kernel,
        in_specs=[pl.BlockSpec(memory_space=pltpu.SMEM)] + any_specs(8),
        out_specs=any_specs(6),
        out_shape=(
            shape(now.shape),
            shape((2, 4, ITERS, rows, LANES)),
            shape((2, 4, ITERS + 1, rows, LANES)),
            shape((2, 9, ITERS, rows, LANES)),
            shape((2, ITERS, rows, LANES)),
            shape((width_x - 2 * ITERS, width_y, LANES)),
        ),
        scratch_shapes=[
            pltpu.VMEM((4, width_x, tall, LANES), F32),
            pltpu.VMEM((4, width_x, tall, LANES), F32),
            pltpu.VMEM((9, width_x, rows, LANES), F32),
            pltpu.VMEM((width_x, rows, LANES), F32),
            pltpu.VMEM((3, width_x, width_y, LANES), F32),
            pltpu.VMEM((2, width_x, width_y, LANES), jnp.int32),
            pltpu.VMEM((5, width_x, TILE, LANES), F32),
            pltpu.VMEM((width_x - 2 * ITERS, width_y, LANES), F32),
            pltpu.SemaphoreType.DMA((10,)),
        ],
        compiler_params=pltpu.CompilerParams(vmem_limit_bytes=40 * 1024 * 1024),
        cost_estimate=pl.CostEstimate(flops=80_000_000, bytes_accessed=16_000_000, transcendentals=0),
        name="inner_steps",
    )(flags, now, prev, vel, eps, delta, tilt, azimuth, border)


def advance_border(flags, edge_a, edge_b, edge_c, edge_corr, halo, corner, wave):
    width_y = wave.shape[3]
    rows = width_y + TILE
    tall = rows + 2 * TILE
    deep = 2 * ITERS + 1
    shape = functools.partial(jax.ShapeDtypeStruct, dtype=F32)
    return pl.pallas_call(
        border_kernel,
        in_specs=[pl.BlockSpec(memory_space=pltpu.SMEM)] + any_specs(7),
        out_specs=any_specs(2),
        out_shape=(shape(wave.shape), shape((2, ITERS, width_y, LANES))),
        scratch_shapes=[
            pltpu.VMEM((4, deep, tall, LANES), F32),
            pltpu.VMEM((4, deep, tall, LANES), F32),
            pltpu.VMEM((9, deep, rows, LANES), F32),
            pltpu.VMEM((deep, rows, LANES), F32),
            pltpu.VMEM((5 * (ITERS - 1), width_y, LANES), F32),
            pltpu.VMEM((5 * (ITERS - 1), TILE, LANES), F32),
            pltpu.VMEM((2, ITERS, width_y, LANES), F32),
            pltpu.SemaphoreType.DMA((22,)),
        ],
        input_output_aliases={7: 0},
        compiler_params=pltpu.CompilerParams(vmem_limit_bytes=40 * 1024 * 1024),
        cost_estimate=pl.CostEstimate(flops=20_000_000, bytes_accessed=4_000_000, transcendentals=0),
        name="border_steps",
    )(flags, edge_a, edge_b, edge_c, edge_corr, halo, corner, wave)


def cut(array, start, size, axis):
    return lax.dynamic_slice_in_dim(array, start, size, axis=axis)


def swap_y(block, axis, second):
    start = (1 - second) * (block.shape[axis] - TILE)
    return lax.ppermute(cut(block, start, TILE, axis), "gy", [(0, 1), (1, 0)])


def face(now, prev, model, low):
    width_x = now.shape[1]
    parts = []
    for group, size in ((now, ITERS), (prev, ITERS - 1), (model, ITERS - 1)):
        at = 0 if low else width_x - size
        part = lax.slice_in_dim(group, at, at + size, axis=1)
        parts.append(part.reshape((-1,) + part.shape[2:]))
    return jnp.concatenate(parts, axis=0)


def sum_shots(block):
    count = lax.axis_size("shot")
    distance = 1
    while distance < count:
        block = block + lax.ppermute(block, "shot", [(i, i ^ distance) for i in range(count)])
        distance *= 2
    return block


def sum_shots_halves(block):
    count = lax.axis_size("shot")
    part = block.shape[0] // 2
    odd = lax.axis_index("shot") % 2
    near = [(i, i ^ 1) for i in range(count)]
    held = cut(block, odd * part, part, 0) + lax.ppermute(cut(block, (1 - odd) * part, part, 0), "shot", near)
    distance = 2
    while distance < count:
        held = held + lax.ppermute(held, "shot", [(i, i ^ distance) for i in range(count)])
        distance *= 2
    other = lax.ppermute(held, "shot", near)
    return jnp.where(odd == 0, jnp.concatenate([held, other]), jnp.concatenate([other, held]))


def local(wave_now, wave_prev, vel_coef, epsilon, delta, tilt, azimuth, aperture):
    second = lax.axis_index("gy")
    columns = lax.axis_size("gx")
    flags = jnp.stack([second.astype(jnp.int32), aperture[0, 0, 0].astype(jnp.int32)])
    model = jnp.stack([vel_coef, epsilon, delta, tilt.astype(F32), azimuth.astype(F32)])
    start = (1 - second) * (wave_now.shape[3] - TILE)
    rows = jnp.concatenate(
        [cut(wave_now[0], start, TILE, 2), cut(wave_prev[0], start, TILE, 2), cut(model, start, TILE, 2)]
    )
    border = lax.ppermute(rows, "gy", [(0, 1), (1, 0)])
    forward = [(i, i + 1) for i in range(columns - 1)]
    backward = [(i + 1, i) for i in range(columns - 1)]
    from_left = lax.ppermute(face(wave_now[0], wave_prev[0], model, False), "gx", forward)
    from_right = lax.ppermute(face(wave_now[0], wave_prev[0], model, True), "gx", backward)
    wave, edge_a, edge_b, edge_c, edge_corr, inside = advance_inner(
        flags, wave_now, wave_prev, vel_coef, epsilon, delta, tilt, azimuth, border
    )
    inside = sum_shots_halves(inside)
    halo = jnp.stack([from_left, from_right])
    corner = swap_y(halo, 2, second)
    wave, outside = advance_border(flags, edge_a, edge_b, edge_c, edge_corr, halo, corner, wave)
    outside = sum_shots(outside)
    return wave, jnp.concatenate([outside[0], inside, outside[1]])


def solution(mesh):
    return jax.shard_map(
        local,
        mesh=mesh,
        in_specs=(
            P("shot", None, "gx", "gy", None),
            P("shot", None, "gx", "gy", None),
            P("gx", "gy", None),
            P("gx", "gy", None),
            P("gx", "gy", None),
            P("gx", "gy", None),
            P("gx", "gy", None),
            P("shot", "gx", "gy"),
        ),
        out_specs=(P("shot", None, "gx", "gy", None), P("gx", "gy", None)),
        check_vma=False,
    )
```

time: 205 us -> 143 us (0.70); the launches traced: 201 us -> 143 us
  other arithmetic: 88.9 us -> 8.44 us
  Pallas kernels: 0 us -> 53.2 us
  starting transfers between devices: 42.3 us -> 10.2 us
  local copies, waits for them, and re-layouts: 4.16 us -> 18.5 us
  between operations: 15.3 us -> 1.52 us
    pallas_call x0 -> x2, Pallas kernels: none -> 53.2 us  [the longest x1 44.2 us: advance_inner(): pl.pallas_call(inner_kernel, in_specs=[pl.BlockSpec(memory_space=pltpu.SM...]
    sub x4 -> x0, other arithmetic: 44 us -> none  [advance(): across = second_x + second_y + second_z - along]
    ppermute x16 -> x9, waiting for transfers between devices: 12.5 us -> 50.7 us  [the longest x2 15.4 us: sum_shots(): lax.ppermute(block, 'shot', [(i, i ^ distance) for i in range(count)])]
    psum x1 -> x0, waiting for transfers between devices: 38 us -> none  [local(): image = lax.psum(covered * correlation, 'shot') / ITERS]
    ppermute x16 -> x9, starting transfers between devices: 42.2 us -> 10.2 us  [the longest x1 3.47 us: local(): lax.ppermute(face(wave_now[0], wave_prev[0], model, True), 'gx', backward)]
    concatenate x7 -> x4, other arithmetic: 22.4 us -> 2.24 us  [the longest x1 1.31 us: local(): jnp.concatenate([cut(wave_now[0], start, TILE, 2), cut(wave_prev[0], star...]
    unnamed x32 -> x41, local copies, waits for them, and re-layouts: 2.44 us -> 13.4 us
    another operation x8 -> x4, other arithmetic: 12.8 us -> 4.32 us  [the longest x2 2.37 us: local(): halo = jnp.stack([from_left, from_right])]
  transfers between devices with their start and end apart: 17 -> 9, of which waited for: 11 -> 5; matrix products, arithmetic and copies ran while one was open for 3% -> 4% of each run, Pallas kernels for 0% -> 37%
where the time goes in v1:
time: 143 us
  Pallas kernels  53.2 us (37%)
  waiting for transfers between devices  50.7 us (35%)
  local copies, waits for them, and re-layouts  18.5 us (13%)
  starting transfers between devices  10.2 us (7%)
  other arithmetic  8.44 us (6%)
  between operations  1.52 us (1%)
    pallas_call x1, Pallas kernels, advance_inner(): pl.pallas_call(inner_kernel, in_specs=[pl.BlockSpec(memory_space=pltpu.SM...  44.2 us
    ppermute x2, waiting for transfers between devices, sum_shots(): lax.ppermute(block, 'shot', [(i, i ^ distance) for i in range(count)])  15.4 us
    ppermute x1, waiting for transfers between devices, local(): lax.ppermute(face(wave_now[0], wave_prev[0], model, False), 'gx', forward)  15 us
    ppermute x1, waiting for transfers between devices, local(): lax.ppermute(face(wave_now[0], wave_prev[0], model, True), 'gx', backward)  13.5 us
    unnamed x41, local copies, waits for them, and re-layouts  13.4 us
    pallas_call x1, Pallas kernels, advance_border(): pl.pallas_call(border_kernel, in_specs=[pl.BlockSpec(memory_space=pltpu.S...  8.96 us
    ppermute x1, waiting for transfers between devices, sum_shots_halves(): other = lax.ppermute(held, 'shot', near)  6.78 us
    ppermute x1, starting transfers between devices, local(): lax.ppermute(face(wave_now[0], wave_prev[0], model, True), 'gx', backward)  3.47 us
  transfers between devices with their start and end apart: 9, of which 5 were waited for; matrix products, arithmetic and copies ran while one was open for 4% of the time, Pallas kernels for 37%

profile of v1, /device:TPU:28, one launch (start us, length us, event | category | flops | bytes accessed | tf_op | source)
XLA Modules:
  0.0 142.6 jit_solution(8192879122677111900)
XLA Ops:
  0.7 2.0 %bitcast_dynamic-update-slice_fusion.4 = f32[5,32,32,128]{3,2,1,0:T(8,128)} fusion(f32[32,32,128]{2,1,0:T(8,128)} %vel.1), kind=kLoop, calls=%fused_computation.11 | loop fusion | bytes 1048576
  2.6 1.9 %bitcast_dynamic-update-slice_fusion.3 = f32[5,32,32,128]{3,2,1,0:T(8,128)} fusion(f32[5,32,32,128]{3,2,1,0:T(8,128)} %bitcast_dynamic-update-slice_fusion.4, f32[32,32,128]{2,1,0:T(8,128)} %eps.1), kind=kLoop, calls=%fused_computation.10 | loop fusion | bytes 1048576
  4.5 0.8 bitcast_dynamic-update-slice_fusion.2
  5.3 0.8 bitcast_dynamic-update-slice_fusion.1
  6.2 1.9 %bitcast_dynamic-update-slice_fusion = f32[5,32,32,128]{3,2,1,0:T(8,128)} fusion(f32[5,32,32,128]{3,2,1,0:T(8,128)} %bitcast_dynamic-update-slice_fusion.1, s32[32,32,128]{2,1,0:T(8,128)} %azimuth.1), kind=kLoop, calls=%fused_computation.7 | loop fusion | flops 131072 | bytes 1048576 | tf_op jit(solution)/shard_map/stack | solution.py:411
  8.0 1.1 constant_dynamic-slice_fusion.1
  9.2 1.1 dynamic-slice_bitcast_fusion
  10.3 1.3 pad_maximum_fusion
  11.7 1.0 fusion.3
  12.7 1.1 fusion.1
  13.9 3.5 %collective-permute-start.2 = (f32[43,32,128]{2,1,0:T(8,128)S(1)}, f32[43,32,128]{2,1,0:T(8,128)S(1)}, u32[]{:S(2)}, u32[]{:S(2)}) collective-permute-start(f32[43,32,128]{2,1,0:T(8,128)S(1)} %pad_maximum_fusion.3), channel_id=1, source_target_pairs={{2,0},{4,2},{6,4},{3,1},{5,3},{7,5},{10,8},{12,10},{14,12},{11,9},... | collective-permute-start | bytes 2113544 | tf_op jit(solution)/shard_map/ppermute | solution.py:420
  17.5 2.5 %collective-permute-start.1 = (f32[43,32,128]{2,1,0:T(8,128)S(1)}, f32[43,32,128]{2,1,0:T(8,128)S(1)}, u32[]{:S(2)}, u32[]{:S(2)}) collective-permute-start(f32[43,32,128]{2,1,0:T(8,128)S(1)} %pad_maximum_fusion.2), channel_id=1, source_target_pairs={{0,2},{2,4},{4,6},{1,3},{3,5},{5,7},{8,10},{10,12},{12,14},{9,11},... | collective-permute-start | bytes 2113544 | tf_op jit(solution)/shard_map/ppermute | solution.py:419
  20.7 13.5 %collective-permute-done.2 = f32[43,32,128]{2,1,0:T(8,128)S(1)} collective-permute-done((f32[43,32,128]{2,1,0:T(8,128)S(1)}, f32[43,32,128]{2,1,0:T(8,128)S(1)}, u32[]{:S(2)}, u32[]{:S(2)}) %collective-permute-start.2) | collective-permute-done | bytes 704544 | tf_op jit(solution)/shard_map/ppermute | solution.py:420
  34.2 15.0 %collective-permute-done.1 = f32[43,32,128]{2,1,0:T(8,128)S(1)} collective-permute-done((f32[43,32,128]{2,1,0:T(8,128)S(1)}, f32[43,32,128]{2,1,0:T(8,128)S(1)}, u32[]{:S(2)}, u32[]{:S(2)}) %collective-permute-start.1) | collective-permute-done | bytes 704544 | tf_op jit(solution)/shard_map/ppermute | solution.py:419
  49.2 0.8 fusion
  50.3 1.6 %copy-done.1 = f32[1,4,32,32,128]{4,3,2,1,0:T(8,128)S(1)} copy-done((f32[1,4,32,32,128]{4,3,2,1,0:T(8,128)S(1)}, f32[1,4,32,32,128]{4,3,2,1,0:T(8,128)}, u32[]{:S(2)}) %copy-start.1) | copy-done | bytes 2097176
  51.9 1.0 copy-done.5
  52.9 1.0 copy-done.7
  54.0 1.0 copy-done.8
  55.0 44.2 %inner_steps.1 = (f32[1,4,32,32,128]{4,3,2,1,0:T(8,128)}, f32[2,4,4,40,128]{4,3,2,1,0:T(8,128)S(1)}, f32[2,4,5,40,128]{4,3,2,1,0:T(8,128)S(1)}, f32[2,9,4,40,128...) custom-call(s32[2]{0:T(128)S(1)} %pad_add_fusion.flags, ...), custom_call_target="tpu_custom_call" | custom-call | flops 80000000 | bytes 16000000 | tf_op jit(solution)/shard_map/inner_steps/pallas_call | solution.py:308
  99.2 1.1 copy-done.9
  100.4 0.9 copy-done.11
  101.3 0.8 copy-done.13
  103.9 1.5 %pad_maximum_fusion.1.halo = f32[2,43,32,128]{3,2,1,0:T(8,128)S(1)} fusion(f32[1,43,32,128]{3,2,1,0:T(8,128)} %bitcast.34, f32[1,43,32,128]{3,2,1,0:T(8,128)} %bitcast.36), kind=kLoop, calls=%fused_computation.2 | loop fusion | flops 352256 | bytes 2818048 | tf_op jit(solution)/shard_map/stack | solution.py:425
  105.8 9.0 %border_steps.1 = (f32[1,4,32,32,128]{4,3,2,1,0:T(8,128)}, f32[2,4,32,128]{3,2,1,0:T(8,128)S(1)}) custom-call(s32[2]{0:T(128)S(1)} %pad_add_fusion.flags, f32[2,4,4,40,128]{4,3,2,1,0:T(8,128)S(1)} %copy-done.14, f32[2,4,5,40,128]{4,3,2,1,0:T(8,128)S(1)} %copy-done.12, f32[2,9,4,40,128]{4,3,2,1,0:T(8,128)S(1)} %copy-done.10, ...), custom_call_target="tpu_custom_call", output_to_operand_aliasing={{0}: (7, {})} | custom-call | flops 20000000 | bytes 4000000 | tf_op jit(solution)/shard_map/border_steps/pallas_call | solution.py:343
  114.7 1.6 %collective-permute-start.4 = (f32[2,4,32,128]{3,2,1,0:T(8,128)S(1)}, f32[2,4,32,128]{3,2,1,0:T(8,128)S(1)}, u32[]{:S(2)}, u32[]{:S(2)}) collective-permute-start(f32[2,4,32,128]{3,2,1,0:T(8,128)S(1)} %get-tuple-element.16), channel_id=1, source_target_pairs={{0,8},{8,0},{16,24},{24,16},{1,9},{9,1},{17,25},{25,17},{2,10},{10... | collective-permute-start | bytes 393224 | tf_op jit(solution)/shard_map/ppermute | solution.py:388
  116.3 1.0 dynamic-slice_add_fusion
  117.7 2.8 %collective-permute-done.4 = f32[2,4,32,128]{3,2,1,0:T(8,128)S(1)} collective-permute-done((f32[2,4,32,128]{3,2,1,0:T(8,128)S(1)}, f32[2,4,32,128]{3,2,1,0:T(8,128)S(1)}, u32[]{:S(2)}, u32[]{:S(2)}) %collective-permute-start.4) | collective-permute-done | bytes 131104 | tf_op jit(solution)/shard_map/ppermute | solution.py:388
  120.4 1.7 %collective-permute-start.5 = (f32[2,4,32,128]{3,2,1,0:T(8,128)S(1)}, f32[2,4,32,128]{3,2,1,0:T(8,128)S(1)}, u32[]{:S(2)}, u32[]{:S(2)}) collective-permute-start(f32[2,4,32,128]{3,2,1,0:T(8,128)S(1)} %add.29), channel_id=1, source_target_pairs={{0,16},{8,24},{16,0},{24,8},{1,17},{9,25},{17,1},{25,9},{2,18},{10... | collective-permute-start | bytes 393224 | tf_op jit(solution)/shard_map/ppermute | solution.py:388
  122.1 12.6 %collective-permute-done.5 = f32[2,4,32,128]{3,2,1,0:T(8,128)S(1)} collective-permute-done((f32[2,4,32,128]{3,2,1,0:T(8,128)S(1)}, f32[2,4,32,128]{3,2,1,0:T(8,128)S(1)}, u32[]{:S(2)}, u32[]{:S(2)}) %collective-permute-start.5) | collective-permute-done | bytes 131104 | tf_op jit(solution)/shard_map/ppermute | solution.py:388
  134.9 6.8 %collective-permute-done.8 = f32[12,32,128]{2,1,0:T(8,128)S(1)} collective-permute-done((f32[12,32,128]{2,1,0:T(8,128)S(1)}, f32[12,32,128]{2,1,0:T(8,128)S(1)}, u32[]{:S(2)}, u32[]{:S(2)}) %collective-permute-start.8) | collective-permute-done | bytes 196640 | tf_op jit(solution)/shard_map/ppermute | solution.py:403
  141.7 0.8 pad_maximum_fusion.4
  (50 shorter events, 3.1 us)
Async XLA Ops:
  0.6 3.9 %copy-start.4 = (f32[32,32,128]{2,1,0:T(8,128)S(1)}, f32[32,32,128]{2,1,0:T(8,128)}, u32[]{:S(2)}) copy-start(f32[32,32,128]{2,1,0:T(8,128)} %delta.1) | copy-start | bytes 1572868
  0.6 4.7 %copy-start.6 = (s32[32,32,128]{2,1,0:T(8,128)S(1)}, s32[32,32,128]{2,1,0:T(8,128)}, u32[]{:S(2)}) copy-start(s32[32,32,128]{2,1,0:T(8,128)} %tilt.1) | copy-start | bytes 1572868
  4.5 4.7 %copy-start = (f32[1,4,32,32,128]{4,3,2,1,0:T(8,128)S(1)}, f32[1,4,32,32,128]{4,3,2,1,0:T(8,128)}, u32[]{:S(2)}) copy-start(f32[1,4,32,32,128]{4,3,2,1,0:T(8,128)} %now.1) | copy-start | bytes 6291460
  11.7 38.6 %collective-permute-start = (f32[13,32,8,128]{3,2,1,0:T(8,128)}, f32[13,32,8,128]{3,2,1,0:T(8,128)}, u32[]{:S(2)}, u32[]{:S(2)}) collective-permute-start(f32[13,32,8,128]{3,2,1,0:T(8,128)} %pad_maximum_fusion), channel_id=1, source_target_pairs={{0,1},{1,0},{2,3},{3,2},{4,5},{5,4},{6,7},{7,6},{8,9},{9,8},{10,11... | collective-permute-start | bytes 5111816 | tf_op jit(solution)/shard_map/ppermute | solution.py:416
  13.9 36.4 %copy-start.2 = (f32[32,32,128]{2,1,0:T(8,128)S(1)}, f32[32,32,128]{2,1,0:T(8,128)}, u32[]{:S(2)}) copy-start(f32[32,32,128]{2,1,0:T(8,128)} %vel.1) | copy-start | bytes 1572868
  13.9 36.4 %copy-start.3 = (f32[32,32,128]{2,1,0:T(8,128)S(1)}, f32[32,32,128]{2,1,0:T(8,128)}, u32[]{:S(2)}) copy-start(f32[32,32,128]{2,1,0:T(8,128)} %eps.1) | copy-start | bytes 1572868
  13.9 20.2 %collective-permute-start.2 = (f32[43,32,128]{2,1,0:T(8,128)S(1)}, f32[43,32,128]{2,1,0:T(8,128)S(1)}, u32[]{:S(2)}, u32[]{:S(2)}) collective-permute-start(f32[43,32,128]{2,1,0:T(8,128)S(1)} %pad_maximum_fusion.3), channel_id=1, source_target_pairs={{2,0},{4,2},{6,4},{3,1},{5,3},{7,5},{10,8},{12,10},{14,12},{11,9},... | collective-permute-start | bytes 2113544 | tf_op jit(solution)/shard_map/ppermute | solution.py:420
  17.5 31.7 %collective-permute-start.1 = (f32[43,32,128]{2,1,0:T(8,128)S(1)}, f32[43,32,128]{2,1,0:T(8,128)S(1)}, u32[]{:S(2)}, u32[]{:S(2)}) collective-permute-start(f32[43,32,128]{2,1,0:T(8,128)S(1)} %pad_maximum_fusion.2), channel_id=1, source_target_pairs={{0,2},{2,4},{4,6},{1,3},{3,5},{5,7},{8,10},{10,12},{12,14},{9,11},... | collective-permute-start | bytes 2113544 | tf_op jit(solution)/shard_map/ppermute | solution.py:419
  34.2 15.9 %copy-start.17 = (f32[43,32,128]{2,1,0:T(8,128)}, f32[43,32,128]{2,1,0:T(8,128)S(1)}, u32[]{:S(2)}) copy-start(f32[43,32,128]{2,1,0:T(8,128)S(1)} %collective-permute-done.2) | copy-start | bytes 2113540
  49.2 1.0 copy-start.18
  50.0 55.4 %collective-permute-start.3 = (f32[2,43,8,128]{3,2,1,0:T(8,128)}, f32[2,43,8,128]{3,2,1,0:T(8,128)}, u32[]{:S(2)}, u32[]{:S(2)}) collective-permute-start(f32[2,43,8,128]{3,2,1,0:T(8,128)} %fusion), channel_id=1, source_target_pairs={{0,1},{1,0},{2,3},{3,2},{4,5},{5,4},{6,7},{7,6},{8,9},{9,8},{10,11... | collective-permute-start | bytes 1056776 | tf_op jit(solution)/shard_map/ppermute | solution.py:371
  50.3 1.6 %copy-start.1 = (f32[1,4,32,32,128]{4,3,2,1,0:T(8,128)S(1)}, f32[1,4,32,32,128]{4,3,2,1,0:T(8,128)}, u32[]{:S(2)}) copy-start(f32[1,4,32,32,128]{4,3,2,1,0:T(8,128)} %prev.1) | copy-start | bytes 6291460
  51.9 1.0 copy-start.5
  52.9 1.0 copy-start.7
  54.0 1.0 copy-start.8
  99.2 1.1 copy-start.9
  100.4 0.9 copy-start.11
  101.3 0.9 copy-start.13
  102.1 0.7 copy-start.15
  102.8 2.7 %copy-start.12 = (f32[2,4,5,40,128]{4,3,2,1,0:T(8,128)S(1)}, f32[2,4,5,40,128]{4,3,2,1,0:T(8,128)}, u32[]{:S(2)}) copy-start(f32[2,4,5,40,128]{4,3,2,1,0:T(8,128)} %copy-done.11) | copy-start | bytes 2457604
  102.8 2.7 %copy-start.14 = (f32[2,4,4,40,128]{4,3,2,1,0:T(8,128)S(1)}, f32[2,4,4,40,128]{4,3,2,1,0:T(8,128)}, u32[]{:S(2)}) copy-start(f32[2,4,4,40,128]{4,3,2,1,0:T(8,128)} %copy-done.13) | copy-start | bytes 1966084
  102.8 2.7 %copy-start.16 = (f32[2,4,40,128]{3,2,1,0:T(8,128)S(1)}, f32[2,4,40,128]{3,2,1,0:T(8,128)}, u32[]{:S(2)}) copy-start(f32[2,4,40,128]{3,2,1,0:T(8,128)} %copy-done.15) | copy-start | bytes 491524
  103.5 12.9 %collective-permute-start.6 = (f32[12,32,128]{2,1,0:T(8,128)}, f32[12,32,128]{2,1,0:T(8,128)}, u32[]{:S(2)}, u32[]{:S(2)}) collective-permute-start(f32[12,32,128]{2,1,0:T(8,128)} %constant_dynamic-slice_fusion), channel_id=1, source_target_pairs={{0,8},{8,0},{16,24},{24,16},{1,9},{9,1},{17,25},{25,17},{2,10},{10... | collective-permute-start | bytes 589832 | tf_op jit(solution)/shard_map/ppermute | solution.py:398
  103.9 1.9 %copy-start.10 = (f32[2,9,4,40,128]{4,3,2,1,0:T(8,128)S(1)}, f32[2,9,4,40,128]{4,3,2,1,0:T(8,128)}, u32[]{:S(2)}) copy-start(f32[2,9,4,40,128]{4,3,2,1,0:T(8,128)} %copy-done.9) | copy-start | bytes 4423684
  114.7 5.7 %collective-permute-start.4 = (f32[2,4,32,128]{3,2,1,0:T(8,128)S(1)}, f32[2,4,32,128]{3,2,1,0:T(8,128)S(1)}, u32[]{:S(2)}, u32[]{:S(2)}) collective-permute-start(f32[2,4,32,128]{3,2,1,0:T(8,128)S(1)} %get-tuple-element.16), channel_id=1, source_target_pairs={{0,8},{8,0},{16,24},{24,16},{1,9},{9,1},{17,25},{25,17},{2,10},{10... | collective-permute-start | bytes 393224 | tf_op jit(solution)/shard_map/ppermute | solution.py:388
  117.3 17.5 %collective-permute-start.7 = (f32[12,32,128]{2,1,0:T(8,128)S(1)}, f32[12,32,128]{2,1,0:T(8,128)S(1)}, u32[]{:S(2)}, u32[]{:S(2)}) collective-permute-start(f32[12,32,128]{2,1,0:T(8,128)S(1)} %dynamic-slice_add_fusion), channel_id=1, source_target_pairs={{0,16},{8,24},{16,0},{24,8},{1,17},{9,25},{17,1},{25,9},{2,18},{10... | collective-permute-start | bytes 589832 | tf_op jit(solution)/shard_map/ppermute | solution.py:401
  120.4 14.3 %collective-permute-start.5 = (f32[2,4,32,128]{3,2,1,0:T(8,128)S(1)}, f32[2,4,32,128]{3,2,1,0:T(8,128)S(1)}, u32[]{:S(2)}, u32[]{:S(2)}) collective-permute-start(f32[2,4,32,128]{3,2,1,0:T(8,128)S(1)} %add.29), channel_id=1, source_target_pairs={{0,16},{8,24},{16,0},{24,8},{1,17},{9,25},{17,1},{25,9},{2,18},{10... | collective-permute-start | bytes 393224 | tf_op jit(solution)/shard_map/ppermute | solution.py:388
  134.8 6.9 %collective-permute-start.8 = (f32[12,32,128]{2,1,0:T(8,128)S(1)}, f32[12,32,128]{2,1,0:T(8,128)S(1)}, u32[]{:S(2)}, u32[]{:S(2)}) collective-permute-start(f32[12,32,128]{2,1,0:T(8,128)S(1)} %add.35), channel_id=1, source_target_pairs={{0,8},{8,0},{16,24},{24,16},{1,9},{9,1},{17,25},{25,17},{2,10},{10... | collective-permute-start | bytes 589832 | tf_op jit(solution)/shard_map/ppermute | solution.py:403

commit v2 on v0

v2 whole, which is shorter than its diff:
```python
import functools
import math

import jax
import jax.numpy as jnp
from jax import lax
from jax.experimental import pallas as pl
from jax.experimental.pallas import tpu as pltpu
from jax.sharding import PartitionSpec as P

ITERS = 4
LANES = 128
TILE = 8
F32 = jnp.float32


def sin_cos(degrees):
    quadrant = jnp.floor(degrees * (1.0 / 90.0) + 0.5)
    angle = (degrees - 90.0 * quadrant) * (math.pi / 180.0)
    square = angle * angle
    sine = angle * (1.0 + square * (-1.0 / 6 + square * (1.0 / 120 + square * (-1.0 / 5040 + square * (1.0 / 362880)))))
    cosine = 1.0 + square * (
        -0.5 + square * (1.0 / 24 + square * (-1.0 / 720 + square * (1.0 / 40320 + square * (-1.0 / 3628800))))
    )
    turn = quadrant - 4.0 * jnp.floor(quadrant * 0.25)
    odd = (turn == 1.0) | (turn == 3.0)
    first = jnp.where(odd, cosine, sine)
    second = jnp.where(odd, sine, cosine)
    return (
        jnp.where(turn >= 2.0, -first, first),
        jnp.where((turn == 1.0) | (turn == 2.0), -second, second),
    )


def model_rows(vel, eps, delta, tilt, azimuth, mirrored):
    sin_t, cos_t = sin_cos(tilt)
    sin_a, cos_a = sin_cos(azimuth)
    nx, ny, nz = sin_t * cos_a, sin_t * sin_a, cos_t
    gain = 1.0 + 2.0 * eps
    root = jnp.sqrt(1.0 + 2.0 * delta)
    half_x = (-0.5 if mirrored else 0.5) * nx
    return (
        (nx * nx,) * 2,
        (ny * ny,) * 2,
        (half_x * ny,) * 2,
        (half_x * nz,) * 2,
        (0.5 * ny * nz,) * 2,
        (vel * gain, vel),
        (vel * root,) * 2,
    )


FACTORS = 7
SLOTS = 8
REACH = ITERS
CHUNKS = 2


def slot(half, field):
    return 4 * (field % 2) + 2 * half + field // 2


class Rows:
    def __init__(self, width_y, second):
        self.width_y = width_y
        self.total = width_y + REACH + 2
        self.own = 1 + REACH * second
        self.other = 1 + width_y * (1 - second)
        self.second = second

    def flat(self, plane, row, where, size):
        return pl.ds((plane * self.total + row) * SLOTS + where, size, stride=SLOTS)

    def tiles(self):
        return [slice(t, t + TILE) for t in range(0, self.width_y, TILE)]

    def pieces(self):
        return [(rows, TILE, self.own + rows.start) for rows in self.tiles()] + [(None, REACH, self.other)]


def z_terms(value, first_lane, last_lane):
    after = jnp.where(last_lane, 0.0, pltpu.roll(value, LANES - 1, 1))
    before = jnp.where(first_lane, 0.0, pltpu.roll(value, 1, 1))
    return after - before, after + before


def lane_ends(shape=(SLOTS, LANES)):
    lane = lax.broadcasted_iota(jnp.int32, shape, 1)
    return lane == 0, lane == LANES - 1


def sweep(old, new, slopes, sums, coef, planes, layout, step, done):
    count = layout.width_y + REACH - 1 - step
    first = 1 + (1 + step) * layout.second
    edges = lane_ends()
    is_q = lax.broadcasted_iota(jnp.int32, (SLOTS, LANES), 0) >= SLOTS // 2
    around = pl.ds(first - 1, count + 2)
    within = pl.ds(first, count)

    def plane(x):
        f_m, f_0, f_p = [old.at[x + i, around] for i in (-1, 0, 1)]
        g, h = slopes.at[pl.ds(x - 1, 3), around], sums.at[pl.ds(x, 2), around]
        out = new.at[x, within]
        factors = [coef.at[i, x, within] for i in range(FACTORS)]

        def column(j):
            below, above = f_m[j], f_p[j]
            g[2, j], h[1, j] = ahead = z_terms(above, *edges)
            return above - below, above + below, f_0[j], g[1, j], ahead[0]

        before, here = column(0), column(1)
        for j in range(count):
            after = column(j + 2)
            a, b, d, e, k, c1, c2 = [factor[j] for factor in factors]
            sum_z = h[0, j + 1]
            twice = here[2] + here[2]
            base = sum_z - twice
            over_x = here[1] - sum_z
            over_y = (after[2] + before[2]) - sum_z
            along = (
                (base + a * over_x)
                + (b * over_y + d * (after[0] - before[0]))
                + (e * (here[4] - g[0, j + 1]) + k * (after[3] - before[3]))
            )
            across = ((over_x + over_y) + 3.0 * base) - along
            mine = jnp.where(is_q, along, across)
            out[j] = (twice - out[j]) + (c1 * mine + c2 * pltpu.roll(mine, SLOTS // 2, 0))
            before, here = here, after
        done(x)

    for back in (1, 0):
        for j in range(count + 2):
            x, row = planes[0] - back, first - 1 + j
            slopes[x, row], sums[x, row] = z_terms(old[x, row], *edges)
    lax.fori_loop(*planes, lambda x, _: (plane(x), 0)[1], 0)


def seam(part, x, rows):
    low = lax.broadcasted_iota(jnp.int32, (SLOTS, LANES), 0) % 4 < 2
    for j in range(rows):
        value = part[x, j]
        part[x + 1, j] = jnp.where(low, pltpu.roll(value, SLOTS - 2, 0), pltpu.roll(value, 2, 0))


def clear_ends(refs, rows):
    for ref in refs:
        empty = jnp.zeros((ref.shape[0], 1) + ref.shape[2:], F32)
        ref[:, 0:1] = empty
        ref[:, rows - 1 : rows] = empty


def copies(pairs, sems, base=0):
    out = []
    for i, (source, target) in enumerate(pairs):
        out.append(pltpu.make_async_copy(source, target, sems.at[base + i]))
        out[-1].start()
    return out


def flat_view(ref):
    size = 1
    for length in ref.shape[:-1]:
        size *= length
    return ref.reshape(size, ref.shape[-1])


def put_model(coef, layout, plane, half, row, size, raw):
    parts = model_rows(*raw, half == 1)
    for i, both in enumerate(parts):
        flat = flat_view(coef.at[i])
        for field in range(4):
            flat[layout.flat(plane, row, slot(half, field), size), :] = both[field % 2]


def products(flat, layout, plane, half, rows):
    where = [layout.flat(plane, layout.own + rows.start, slot(half, field), TILE) for field in (0, 2)]
    return flat[where[0], :] * flat[where[1], :]


def inner_kernel(
    cover, now, prev, vel, eps, delta, tilt, azimuth, border,
    wave, edge_a, edge_b, edge_c, edge_corr, kept, sent,
    fa, fb, slopes, sums, coef, corr, in_now, in_prev, raw, raw_int, in_border, load_sems, sems, wave_sems,
):
    second, odd = lax.axis_index("gy"), lax.axis_index("shot") % 2
    width_x, width_y = vel.shape[0], vel.shape[1]
    half_x = width_x // 2
    layout = Rows(width_y, second)
    rows = layout.total
    chunk = half_x // CHUNKS
    loads = []
    for c in range(CHUNKS):
        pairs = [(border, in_border)] if c == 0 else []
        for start in (c * chunk, width_x - (c + 1) * chunk):
            at = pl.ds(start, chunk)
            pairs += [(now.at[0, :, at], in_now.at[:, at]), (prev.at[0, :, at], in_prev.at[:, at])]
            pairs += [(array.at[at], raw.at[n, at]) for n, array in enumerate((vel, eps, delta))]
            pairs += [(array.at[at], raw_int.at[n, at]) for n, array in enumerate((tilt, azimuth))]
        loads.append(copies(pairs, load_sems.at[c]))
    clear_ends((fa, fb), rows)

    def fill(i, _):
        for half in range(2):
            x = i if half == 0 else width_x - 1 - i
            for field in range(4):
                for own, size, row in layout.pieces():
                    spot = layout.flat(i, row, slot(half, field), size)
                    if own is None:
                        flat_view(fa)[spot, :] = in_border[field, x]
                        flat_view(fb)[spot, :] = in_border[4 + field, x]
                    else:
                        flat_view(fa)[spot, :] = in_now[field, x, own, :]
                        flat_view(fb)[spot, :] = in_prev[field, x, own, :]
        for half in range(2):
            x = i if half == 0 else width_x - 1 - i
            for own, size, row in layout.pieces():
                if own is None:
                    cells = [in_border[8 + n, x] for n in range(5)]
                else:
                    cells = [raw[n, x, own, :] for n in range(3)]
                    cells += [raw_int[n, x, own, :].astype(F32) for n in range(2)]
                put_model(coef, layout, i, half, row, size, cells)
        return 0

    for c in range(CHUNKS):
        for copy in loads[c]:
            copy.wait()
        lax.fori_loop(c * chunk, (c + 1) * chunk, fill, 0)
    out = copies([(coef.at[:, pl.ds(0, ITERS)], edge_c)], sems, 9)
    seam(fa, half_x - 1, rows)
    bufs = (fa, fb)
    scale = cover[0, 0, 0].astype(F32) / ITERS

    def give_wave(i, half):
        x = i if half == 0 else width_x - 1 - i
        return pltpu.make_async_copy(in_now.at[:, x], wave.at[0, :, x], wave_sems.at[half * half_x + i])

    def finished(step):
        flat = flat_view(bufs[1 - step % 2])

        def done(i):
            for half in range(2):
                x = i if half == 0 else width_x - 1 - i
                for own in layout.tiles():
                    product = products(flat, layout, i, half, own)
                    total = product if step == 0 else corr[x, own, :] + product
                    corr[x, own, :] = scale * total if step == ITERS - 1 else total
                    if step == ITERS - 1:
                        for field in range(4):
                            spot = layout.flat(i, layout.own + own.start, slot(half, field), TILE)
                            in_now[field, x, own, :] = flat[spot, :]
                if step == ITERS - 1:
                    give_wave(i, half).start()

        return done

    for step in range(ITERS):
        old, new = bufs[step % 2], bufs[1 - step % 2]
        sweep(old, new, slopes, sums, coef, (1 + step, half_x), layout, step, finished(step))
        if step < ITERS - 1:
            seam(new, half_x - 1, rows)
        if step == ITERS - 3:
            out += copies([(fa.at[pl.ds(0, ITERS)], edge_a)], sems, 10)
        if step == ITERS - 2:
            far = pl.ds(width_x - ITERS, ITERS)
            out += copies(
                [
                    (fb.at[pl.ds(0, ITERS + 1)], edge_b),
                    (corr.at[pl.ds(0, ITERS)], edge_corr.at[0]),
                    (corr.at[far], edge_corr.at[1]),
                ],
                sems,
                11,
            )
    part = half_x - ITERS
    out += copies(
        [
            (corr.at[pl.ds(ITERS + part * odd, part)], kept),
            (corr.at[pl.ds(ITERS + part * (1 - odd), part)], sent),
        ],
        sems,
        14,
    )
    for copy in out:
        copy.wait()
    for i in range(ITERS, half_x):
        for half in range(2):
            give_wave(i, half).wait()


def border_kernel(
    cover, edge_a, edge_b, edge_c, edge_corr, near, far, corner, wave_in,
    wave, image,
    fa, fb, slopes, sums, coef, corr, sides, corners, in_now, sems,
):
    second, odd = lax.axis_index("gy"), lax.axis_index("gx") % 2
    width_x, width_y = wave.shape[2], wave.shape[3]
    layout = Rows(width_y, second)
    rows = layout.total
    loads = copies(
        [
            (near, sides.at[1 - odd]),
            (far, sides.at[odd]),
            (corner.at[0], corners.at[1 - odd]),
            (corner.at[1], corners.at[odd]),
            (edge_a, fa.at[pl.ds(ITERS, ITERS)]),
            (edge_b, fb.at[pl.ds(ITERS, ITERS + 1)]),
            (edge_corr, corr),
            (edge_c, coef.at[:, pl.ds(ITERS, ITERS)]),
        ],
        sems,
    )
    clear_ends([ref.at[pl.ds(0, ITERS)] for ref in (fa, fb)], rows)
    for copy in loads[:4]:
        copy.wait()
    n_now, n_prev, less = 4 * ITERS, 4 * (ITERS - 1), ITERS - 1

    def cells(half, index, own):
        return corners[half, index] if own is None else sides[half, index, own, :]

    def fill(j, _):
        for half in range(2):
            natural = j if half == 0 else ITERS - 1 - j
            shorter = jnp.maximum(j - 1, 0) if half == 0 else jnp.minimum(ITERS - 1 - j, less - 1)
            for own, size, row in layout.pieces():
                for field in range(4):
                    spot = layout.flat(j, row, slot(half, field), size)
                    flat_view(fa)[spot, :] = cells(half, field * ITERS + natural, own)
                    flat_view(fb)[spot, :] = cells(half, n_now + field * less + shorter, own)
        for half in range(2):
            shorter = jnp.maximum(j - 1, 0) if half == 0 else jnp.minimum(ITERS - 1 - j, less - 1)
            for own, size, row in layout.pieces():
                raw = [cells(half, n_now + n_prev + n * less + shorter, own) for n in range(5)]
                put_model(coef, layout, j, half, row, size, raw)
        return 0

    lax.fori_loop(0, ITERS, fill, 0)
    for copy in loads[4:]:
        copy.wait()

    corr[0, 0] = jnp.zeros(corr.shape[2:], F32)
    corr[1, ITERS - 1] = jnp.zeros(corr.shape[2:], F32)

    def finished(flat):
        def done(i):
            @pl.when(i >= ITERS)
            def _():
                for half in range(2):
                    x = i - ITERS if half == 0 else 2 * ITERS - 1 - i
                    for own in layout.tiles():
                        corr[half, x, own, :] = corr[half, x, own, :] + products(flat, layout, i, half, own)

        return done

    def advance(turn, _):
        for step, (old, new) in enumerate(((fa, fb), (fb, fa))):
            start = 1 + step + 2 * turn
            sweep(old, new, slopes, sums, coef, (start, start + ITERS), layout, 0, finished(flat_view(new)))
        return 0

    lax.fori_loop(0, ITERS // 2, advance, 0)
    scale = cover[0, 0, 0].astype(F32) / ITERS
    corr[...] = scale * corr[...]
    out = copies([(corr, image)], sems)
    flat = flat_view(fa)

    def give(i, _):
        for half in range(2):
            x = i if half == 0 else ITERS - 1 - i
            for own in layout.tiles():
                for field in range(4):
                    spot = layout.flat(ITERS + i, layout.own + own.start, slot(half, field), TILE)
                    in_now[half, field, x, own, :] = flat[spot, :]
        return 0

    lax.fori_loop(0, ITERS, give, 0)
    out += copies(
        [
            (in_now.at[0], wave.at[0, :, pl.ds(0, ITERS)]),
            (in_now.at[1], wave.at[0, :, pl.ds(width_x - ITERS, ITERS)]),
        ],
        sems,
        1,
    )
    for copy in out:
        copy.wait()


def any_specs(count):
    return [pl.BlockSpec(memory_space=pl.ANY)] * count


MIB = 1024 * 1024


def pack_kernel(
    now, prev, vel, eps, delta, tilt, azimuth,
    near, far, border,
    planes_int, wave_rows, float_rows, int_rows, sems,
):
    second, odd = lax.axis_index("gy"), lax.axis_index("gx") % 2
    width_x, width_y = vel.shape[0], vel.shape[1]
    deep, less = ITERS, ITERS - 1
    n_now, n_prev = 4 * deep, 4 * less
    ints, floats = (tilt, azimuth), (vel, eps, delta)
    tile = pl.ds(pl.multiple_of((1 - second) * (width_y - TILE), TILE), TILE)
    pairs = [(array.at[0, :, :, tile], wave_rows.at[n]) for n, array in enumerate((now, prev))]
    pairs += [(array.at[:, tile], float_rows.at[n]) for n, array in enumerate(floats)]
    pairs += [(array.at[:, tile], int_rows.at[n]) for n, array in enumerate(ints)]
    ends = ((near, 1 - odd), (far, odd))
    for k, (_, high) in enumerate(ends):
        at = pl.ds(high * (width_x - less), less)
        pairs += [(ints[n].at[at], planes_int.at[k, n]) for n in range(2)]
    first = len(pairs)
    for out, high in ends:
        at = pl.ds(high * (width_x - less), less)
        for f in range(4):
            pairs.append((now.at[0, f, pl.ds(high * (width_x - deep), deep)], out.at[pl.ds(f * deep, deep)]))
            pairs.append((prev.at[0, f, at], out.at[pl.ds(n_now + f * less, less)]))
        for n in range(3):
            pairs.append((floats[n].at[at], out.at[pl.ds(n_now + n_prev + n * less, less)]))
    started = copies(pairs, sems)
    for copy in started[:first]:
        copy.wait()
    for k, (out, _) in enumerate(ends):
        for n in range(2):
            begin = n_now + n_prev + (3 + n) * less
            out[begin : begin + less] = planes_int[k, n].astype(F32)

    def needed(ref, *spot):
        return jnp.where(second == 1, ref[spot + (slice(0, REACH),)], ref[spot + (slice(TILE - REACH, TILE),)])

    def rows(x, _):
        for kind in range(2):
            for f in range(4):
                border[4 * kind + f, x] = needed(wave_rows, kind, f, x)
        for n in range(3):
            border[8 + n, x] = needed(float_rows, n, x)
        for n in range(2):
            border[11 + n, x] = needed(int_rows, n, x).astype(F32)
        return 0

    lax.fori_loop(0, width_x, rows, 0)
    for copy in started[first:]:
        copy.wait()


def pack(now, prev, vel, eps, delta, tilt, azimuth):
    width_x, width_y = vel.shape[0], vel.shape[1]
    planes = 4 * ITERS + 9 * (ITERS - 1)
    face = jax.ShapeDtypeStruct((planes, width_y, LANES), F32)
    return pl.pallas_call(
        pack_kernel,
        in_specs=any_specs(7),
        out_specs=[pl.BlockSpec(memory_space=pltpu.VMEM)] * 3,
        out_shape=(face, face, jax.ShapeDtypeStruct((13, width_x, REACH, LANES), F32)),
        scratch_shapes=[
            pltpu.VMEM((2, 2, ITERS - 1, width_y, LANES), jnp.int32),
            pltpu.VMEM((2, 4, width_x, TILE, LANES), F32),
            pltpu.VMEM((3, width_x, TILE, LANES), F32),
            pltpu.VMEM((2, width_x, TILE, LANES), jnp.int32),
            pltpu.SemaphoreType.DMA((33,)),
        ],
        compiler_params=pltpu.CompilerParams(vmem_limit_bytes=60 * MIB),
        cost_estimate=pl.CostEstimate(flops=1_000_000, bytes_accessed=8_000_000, transcendentals=0),
        name="pack_borders",
    )(now, prev, vel, eps, delta, tilt, azimuth)


def advance_inner(cover, now, prev, vel, eps, delta, tilt, azimuth, border):
    width_x, width_y = vel.shape[0], vel.shape[1]
    rows = width_y + REACH + 2
    half_x = width_x // 2
    shape = functools.partial(jax.ShapeDtypeStruct, dtype=F32)
    block = (half_x + 1, rows, SLOTS, LANES)
    part = shape((half_x - ITERS, width_y, LANES))
    vmem = lambda size: pltpu.VMEM(size, F32)
    return pl.pallas_call(
        inner_kernel,
        in_specs=[pl.BlockSpec(memory_space=pltpu.SMEM)] + any_specs(8),
        out_specs=any_specs(7),
        out_shape=(
            shape(now.shape),
            shape((ITERS,) + block[1:]),
            shape((ITERS + 1,) + block[1:]),
            shape((FACTORS, ITERS) + block[1:]),
            shape((2, ITERS, width_y, LANES)),
            part,
            part,
        ),
        scratch_shapes=[vmem(block)] * 4
        + [
            vmem((FACTORS, half_x) + block[1:]),
            vmem(vel.shape),
            vmem(now.shape[1:]),
            vmem(now.shape[1:]),
            vmem((3, width_x, width_y, LANES)),
            pltpu.VMEM((2, width_x, width_y, LANES), jnp.int32),
            vmem(border.shape),
            pltpu.SemaphoreType.DMA((CHUNKS, 15)),
            pltpu.SemaphoreType.DMA((16,)),
            pltpu.SemaphoreType.DMA((width_x,)),
        ],
        compiler_params=pltpu.CompilerParams(vmem_limit_bytes=60 * MIB),
        cost_estimate=pl.CostEstimate(flops=80_000_000, bytes_accessed=200_000_000, transcendentals=0),
        name="inner_steps",
    )(cover, now, prev, vel, eps, delta, tilt, azimuth, border)


def advance_border(cover, edge_a, edge_b, edge_c, edge_corr, near, far, corner, wave):
    width_y = wave.shape[3]
    rows = width_y + REACH + 2
    block = (2 * ITERS + 1, rows, SLOTS, LANES)
    shape = functools.partial(jax.ShapeDtypeStruct, dtype=F32)
    vmem = lambda size: pltpu.VMEM(size, F32)
    return pl.pallas_call(
        border_kernel,
        in_specs=[pl.BlockSpec(memory_space=pltpu.SMEM)] + any_specs(8),
        out_specs=any_specs(2),
        out_shape=(shape(wave.shape), shape(edge_corr.shape)),
        scratch_shapes=[vmem(block)] * 4
        + [
            vmem((FACTORS,) + block),
            vmem(edge_corr.shape),
            vmem((2,) + near.shape),
            vmem(corner.shape),
            vmem((2, 4, ITERS, width_y, LANES)),
            pltpu.SemaphoreType.DMA((8,)),
        ],
        input_output_aliases={8: 0},
        compiler_params=pltpu.CompilerParams(vmem_limit_bytes=60 * MIB),
        cost_estimate=pl.CostEstimate(flops=20_000_000, bytes_accessed=20_000_000, transcendentals=0),
        name="border_steps",
    )(cover, edge_a, edge_b, edge_c, edge_corr, near, far, corner, wave)


def cut(array, start, size, axis):
    return lax.dynamic_slice_in_dim(array, start, size, axis=axis)


def other_rows(block, axis, second):
    return cut(block, (1 - second) * (block.shape[axis] - REACH), REACH, axis)


def swap_cores(rows):
    return lax.ppermute(rows, "gy", [(0, 1), (1, 0)])


def pairs_at(distance):
    return [(i, i ^ distance) for i in range(lax.axis_size("shot"))]


def local(wave_now, wave_prev, vel_coef, epsilon, delta, tilt, azimuth, aperture):
    second = lax.axis_index("gy")
    columns = lax.axis_size("gx")
    inputs = (wave_now, wave_prev, vel_coef, epsilon, delta, tilt, azimuth)
    near, far, border = pack(*inputs)
    far = lax.ppermute(far, "gx", [(i, j) for i in range(1, columns - 1) for j in [i + 1 if i % 2 else i - 1]])
    near = lax.ppermute(near, "gx", [(i, i ^ 1) for i in range(columns) if i ^ 1 < columns])
    border = swap_cores(border)
    wave, edge_a, edge_b, edge_c, edge_corr, kept, sent = advance_inner(aperture, *inputs, border)
    kept, near, far = lax.optimization_barrier((kept, near, far))
    held = kept + lax.ppermute(sent, "shot", pairs_at(1))
    corner = swap_cores(jnp.stack([other_rows(f, 1, second) for f in (near, far)]))
    held, edge_corr = lax.optimization_barrier((held, edge_corr))
    wave, outside = advance_border(aperture, edge_a, edge_b, edge_c, edge_corr, near, far, corner, wave)
    distance = 2
    while distance < lax.axis_size("shot"):
        held = held + lax.ppermute(held, "shot", pairs_at(distance))
        distance *= 2
    held, outside = lax.optimization_barrier((held, outside))
    distance = 1
    while distance < lax.axis_size("shot"):
        outside = outside + lax.ppermute(outside, "shot", pairs_at(distance))
        if distance == 1:
            held, outside = lax.optimization_barrier((held, outside))
            other = lax.ppermute(held, "shot", pairs_at(1))
        distance *= 2
    even = lax.axis_index("shot") % 2 == 0
    first, then = jnp.where(even, held, other), jnp.where(even, other, held)
    return wave, jnp.concatenate([outside[0], first, then, outside[1]])


def solution(mesh):
    return jax.shard_map(
        local,
        mesh=mesh,
        in_specs=(
            P("shot", None, "gx", "gy", None),
            P("shot", None, "gx", "gy", None),
            P("gx", "gy", None),
            P("gx", "gy", None),
            P("gx", "gy", None),
            P("gx", "gy", None),
            P("gx", "gy", None),
            P("shot", "gx", "gy"),
        ),
        out_specs=(P("shot", None, "gx", "gy", None), P("gx", "gy", None)),
        check_vma=False,
    )
```

time: 205 us -> 72.4 us (0.35); the launches traced: 201 us -> 71 us
  other arithmetic: 88.9 us -> 2.83 us
  Pallas kernels: 0 us -> 34.4 us
  starting transfers between devices: 42.3 us -> 8.43 us
  waiting for transfers between devices: 50.5 us -> 22.3 us
  between operations: 15.3 us -> 1.38 us
  local copies, waits for them, and re-layouts: 4.16 us -> 1.65 us
    sub x4 -> x0, other arithmetic: 44 us -> none  [advance(): across = second_x + second_y + second_z - along]
    psum x1 -> x0, waiting for transfers between devices: 38 us -> none  [local(): image = lax.psum(covered * correlation, 'shot') / ITERS]
    pallas_call x0 -> x3, Pallas kernels: none -> 34.4 us  [the longest x1 22.1 us: advance_inner(): pl.pallas_call(inner_kernel, in_specs=[pl.BlockSpec(memory_space=pltpu.SM...]
    ppermute x16 -> x9, starting transfers between devices: 42.2 us -> 8.43 us  [the longest x2 2.97 us: local(): outside = outside + lax.ppermute(outside, 'shot', pairs_at(distance))]
    concatenate x7 -> x1, other arithmetic: 22.4 us -> 0.83 us  [local(): return (wave, jnp.concatenate([outside[0], first, then, outside[1]]))]
    another operation x8 -> x1, other arithmetic: 12.8 us -> 0.04 us  [local(): jnp.stack([other_rows(f, 1, second) for f in (near, far)])]
    ppermute x16 -> x9, waiting for transfers between devices: 12.5 us -> 22.3 us  [the longest x2 11.3 us: local(): outside = outside + lax.ppermute(outside, 'shot', pairs_at(distance))]
    mul x2 -> x0, other arithmetic: 7.35 us -> none  [the longest x1 6.06 us: advance(): normal_x * normal_x * second_x + normal_y * normal_y * second_y]
  transfers between devices with their start and end apart: 17 -> 9, of which waited for: 11 -> 7; matrix products, arithmetic and copies ran while one was open for 3% -> 0% of each run, Pallas kernels for 0% -> 43%
where the time goes in v2:
time: 72.4 us; the launch traced here: 71 us
  Pallas kernels  34.4 us (48%)
  waiting for transfers between devices  22.3 us (31%)
  starting transfers between devices  8.43 us (12%)
  other arithmetic  2.83 us (4%)
  local copies, waits for them, and re-layouts  1.65 us (2%)
  between operations  1.38 us (2%)
    pallas_call x1, Pallas kernels, advance_inner(): pl.pallas_call(inner_kernel, in_specs=[pl.BlockSpec(memory_space=pltpu.SM...  22.1 us
    ppermute x2, waiting for transfers between devices, local(): outside = outside + lax.ppermute(outside, 'shot', pairs_at(distance))  11.3 us
    pallas_call x1, Pallas kernels, advance_border(): pl.pallas_call(border_kernel, in_specs=[pl.BlockSpec(memory_space=pltpu.S...  8.75 us
    ppermute x1, waiting for transfers between devices, local(): lax.ppermute(far, 'gx', [(i, j) for i in range(1, columns - 1) for j in [...  5.28 us
    pallas_call x1, Pallas kernels, pack(): pl.pallas_call(pack_kernel, in_specs=any_specs(7), out_specs=[pl.BlockSpe...  3.52 us
    ppermute x2, starting transfers between devices, local(): outside = outside + lax.ppermute(outside, 'shot', pairs_at(distance))  2.97 us
    ppermute x1, waiting for transfers between devices, local(): other = lax.ppermute(held, 'shot', pairs_at(1))  2.73 us
    ppermute x1, starting transfers between devices, local(): lax.ppermute(far, 'gx', [(i, j) for i in range(1, columns - 1) for j in [...  2.36 us
  transfers between devices with their start and end apart: 9, of which 7 were waited for; matrix products, arithmetic and copies ran while one was open for 0% of the time, Pallas kernels for 43%

profile of v2, /device:TPU:28, one launch (start us, length us, event | category | flops | bytes accessed | tf_op | source)
XLA Modules:
  0.0 71.0 jit_solution(14005189943441426005)
XLA Ops:
  0.6 3.5 %pack_borders.1 = (f32[43,32,128]{2,1,0:T(8,128)}, f32[43,32,128]{2,1,0:T(8,128)}, f32[13,32,4,128]{3,2,1,0:T(4,128)}) custom-call(f32[1,4,32,32,128]{4,3,2,1,0:T(8,128)} %now.3, f32[1,4,32,32,128]{4,3,2,1,0:T(8,128)} %prev.3, f32[32,32,128]{2,1,0:T(8,128)} %vel.3, f32[32,32,128]{2,1,0:T(8,128)} %eps.3, f32[32,32,128]{2,1,0:T(8,128)} %delta.3, ...), custom_call_target="tpu_custom_call" | custom-call | flops 1000000 | bytes 8000000 | tf_op jit(solution)/shard_map/pack_borders/pallas_call | solution.py:452
  4.2 0.1 collective-permute-start
  4.2 1.6 %collective-permute-start.1 = (f32[43,32,128]{2,1,0:T(8,128)}, f32[43,32,128]{2,1,0:T(8,128)S(1)}, u32[]{:S(2)}, u32[]{:S(2)}) collective-permute-start(f32[43,32,128]{2,1,0:T(8,128)} %get-tuple-element.28), channel_id=1, source_target_pairs={{0,2},{2,0},{4,6},{6,4},{1,3},{3,1},{5,7},{7,5},{8,10},{10,8},{12,... | collective-permute-start | bytes 2113544 | tf_op jit(solution)/shard_map/ppermute | solution.py:559
  5.8 2.4 %collective-permute-start.2 = (f32[43,32,128]{2,1,0:T(8,128)}, f32[43,32,128]{2,1,0:T(8,128)S(1)}, u32[]{:S(2)}, u32[]{:S(2)}) collective-permute-start(f32[43,32,128]{2,1,0:T(8,128)} %get-tuple-element.29), channel_id=1, source_target_pairs={{2,4},{4,2},{3,5},{5,3},{10,12},{12,10},{11,13},{13,11},{18,20},{2... | collective-permute-start | bytes 2113544 | tf_op jit(solution)/shard_map/ppermute | solution.py:558
  8.8 0.0 collective-permute-done.border
  8.8 0.0 copy-start.2
  8.8 0.9 %copy-done.2 = f32[13,32,4,128]{3,2,1,0:T(4,128)} copy-done((f32[13,32,4,128]{3,2,1,0:T(4,128)}, f32[13,32,4,128]{3,2,1,0:T(4,128)S(1)}, u32[]{:S(2)}) %copy-start.2) | copy-done | bytes 851992
  9.8 22.1 %inner_steps.1 = (f32[1,4,32,32,128]{4,3,2,1,0:T(8,128)}, f32[4,38,8,128]{3,2,1,0:T(8,128)}, f32[5,38,8,128]{3,2,1,0:T(8,128)}, f32[7,4,38,8,128]{4,3,2,1,0:T(8,...) custom-call(s32[1,1,1]{2,1,0:T(1,128)S(6)} %copy.12.cover, ...), custom_call_target="tpu_custom_call" | custom-call | flops 80000000 | bytes 200000000 | tf_op jit(solution)/shard_map/inner_steps/pallas_call | solution.py:478
  31.9 0.5 collective-permute-start.3
  32.4 0.0 collective-permute-done.1.near
  32.4 0.0 copy-start
  32.4 5.3 %collective-permute-done.2.far = f32[43,32,128]{2,1,0:T(8,128)S(1)} collective-permute-done((f32[43,32,128]{2,1,0:T(8,128)}, f32[43,32,128]{2,1,0:T(8,128)S(1)}, u32[]{:S(2)}, u32[]{:S(2)}) %collective-permute-start.2) | collective-permute-done | bytes 704544 | tf_op jit(solution)/shard_map/ppermute | solution.py:558
  37.7 0.0 copy-start.1
  37.7 0.1 dynamic-slice_bitcast_fusion
  37.7 1.6 %collective-permute-done.3 = f32[12,32,128]{2,1,0:T(8,128)S(1)} collective-permute-done((f32[12,32,128]{2,1,0:T(8,128)}, f32[12,32,128]{2,1,0:T(8,128)S(1)}, u32[]{:S(2)}, u32[]{:S(2)}) %collective-permute-start.3) | collective-permute-done | bytes 196640 | tf_op jit(solution)/shard_map/ppermute | solution.py:563
  39.3 1.0 %add.20 = f32[12,32,128]{2,1,0:T(8,128)S(1)} add(f32[12,32,128]{2,1,0:T(8,128)} %get-tuple-element.30, f32[12,32,128]{2,1,0:T(8,128)S(1)} %collective-permute-done.3) | non-fusion elementwise | flops 49152 | bytes 589824 | tf_op jit(solution)/shard_map/add | solution.py:563
  40.3 0.4 collective-permute-start.5
  40.7 0.1 collective-permute-start.4
  40.8 1.4 %collective-permute-done.4.corner = f32[2,43,4,128]{3,2,1,0:T(4,128)S(1)} collective-permute-done((f32[2,43,4,128]{3,2,1,0:T(4,128)S(1)}, f32[2,43,4,128]{3,2,1,0:T(4,128)S(1)}, u32[]{:S(2)}, u32[]{:S(2)}) %collective-permute-start.4) | collective-permute-done | bytes 176160 | tf_op jit(solution)/shard_map/ppermute | solution.py:546
  42.2 0.0 copy-done
  42.2 0.0 copy-done.1
  42.2 0.7 copy-done.3
  42.9 8.7 %border_steps.1 = (f32[1,4,32,32,128]{4,3,2,1,0:T(8,128)}, f32[2,4,32,128]{3,2,1,0:T(8,128)}) custom-call(s32[1,1,1]{2,1,0:T(1,128)S(6)} %copy.12.cover, f32[4,38,8,128]{3,2,1,0:T(8,128)} %get-tuple-element.24.edge_a, f32[5,38,8,128]{3,2,1,0:T(8,128)} %get-tuple-element.25.edge_b, ...), custom_call_target="tpu_custom_call", output_to_operand_aliasing={{0}: (8, {})} | custom-call | flops 20000000 | bytes 20000000 | tf_op jit(solution)/shard_map/border_steps/pallas_call | solution.py:516
  51.6 0.1 collective-permute-done.5
  51.8 0.3 collective-permute-start.6
  52.1 5.7 %collective-permute-done.6 = f32[2,4,32,128]{3,2,1,0:T(8,128)S(1)} collective-permute-done((f32[2,4,32,128]{3,2,1,0:T(8,128)}, f32[2,4,32,128]{3,2,1,0:T(8,128)S(1)}, u32[]{:S(2)}, u32[]{:S(2)}) %collective-permute-start.6) | collective-permute-done | bytes 131104 | tf_op jit(solution)/shard_map/ppermute | solution.py:574
  57.8 0.9 %add.23 = f32[2,4,32,128]{3,2,1,0:T(8,128)S(1)} add(f32[2,4,32,128]{3,2,1,0:T(8,128)} %get-tuple-element.41, f32[2,4,32,128]{3,2,1,0:T(8,128)S(1)} %collective-permute-done.6) | non-fusion elementwise | flops 32768 | bytes 393216 | tf_op jit(solution)/shard_map/add | solution.py:574
  58.7 2.7 %collective-permute-start.7 = (f32[2,4,32,128]{3,2,1,0:T(8,128)S(1)}, f32[2,4,32,128]{3,2,1,0:T(8,128)S(1)}, u32[]{:S(2)}, u32[]{:S(2)}) collective-permute-start(f32[2,4,32,128]{3,2,1,0:T(8,128)S(1)} %add.23), channel_id=1, source_target_pairs={{0,16},{8,24},{16,0},{24,8},{1,17},{9,25},{17,1},{25,9},{2,18},{10... | collective-permute-start | bytes 393224 | tf_op jit(solution)/shard_map/ppermute | solution.py:574
  61.3 0.4 collective-permute-start.8
  61.8 5.6 %collective-permute-done.7 = f32[2,4,32,128]{3,2,1,0:T(8,128)S(1)} collective-permute-done((f32[2,4,32,128]{3,2,1,0:T(8,128)S(1)}, f32[2,4,32,128]{3,2,1,0:T(8,128)S(1)}, u32[]{:S(2)}, u32[]{:S(2)}) %collective-permute-start.7) | collective-permute-done | bytes 131104 | tf_op jit(solution)/shard_map/ppermute | solution.py:574
  67.4 2.7 %collective-permute-done.8 = f32[12,32,128]{2,1,0:T(8,128)S(1)} collective-permute-done((f32[12,32,128]{2,1,0:T(8,128)S(1)}, f32[12,32,128]{2,1,0:T(8,128)S(1)}, u32[]{:S(2)}, u32[]{:S(2)}) %collective-permute-start.8) | collective-permute-done | bytes 196640 | tf_op jit(solution)/shard_map/ppermute | solution.py:577
  70.2 0.8 %pad_maximum_fusion = f32[32,32,128]{2,1,0:T(8,128)} fusion(f32[4,32,128]{2,1,0:T(8,128)S(1)} %get-tuple-element.47, f32[12,32,128]{2,1,0:T(8,128)S(1)} %get-tuple-element.45, f32[12,32,128]{2,1,0:T(8,128)S(1)} %get-tuple-element.44, f32[4,32,128]{2,1,0:T(8,128)S(1)} %get-tuple-element.46), kind=kLoop, calls=%fused_computation | loop fusion | flops 393216 | bytes 1048576 | tf_op jit(solution)/shard_map/concatenate | solution.py:581
  (6 shorter events, 0.1 us)
Async XLA Ops:
  4.2 4.7 %collective-permute-start = (f32[13,32,4,128]{3,2,1,0:T(4,128)}, f32[13,32,4,128]{3,2,1,0:T(4,128)S(1)}, u32[]{:S(2)}, u32[]{:S(2)}) collective-permute-start(f32[13,32,4,128]{3,2,1,0:T(4,128)} %get-tuple-element.23), channel_id=1, source_target_pairs={{0,1},{1,0},{2,3},{3,2},{4,5},{5,4},{6,7},{7,6},{8,9},{9,8},{10,11... | collective-permute-start | bytes 2555912 | tf_op jit(solution)/shard_map/ppermute | solution.py:546
  4.2 28.2 %collective-permute-start.1 = (f32[43,32,128]{2,1,0:T(8,128)}, f32[43,32,128]{2,1,0:T(8,128)S(1)}, u32[]{:S(2)}, u32[]{:S(2)}) collective-permute-start(f32[43,32,128]{2,1,0:T(8,128)} %get-tuple-element.28), channel_id=1, source_target_pairs={{0,2},{2,0},{4,6},{6,4},{1,3},{3,1},{5,7},{7,5},{8,10},{10,8},{12,... | collective-permute-start | bytes 2113544 | tf_op jit(solution)/shard_map/ppermute | solution.py:559
  5.8 31.9 %collective-permute-start.2 = (f32[43,32,128]{2,1,0:T(8,128)}, f32[43,32,128]{2,1,0:T(8,128)S(1)}, u32[]{:S(2)}, u32[]{:S(2)}) collective-permute-start(f32[43,32,128]{2,1,0:T(8,128)} %get-tuple-element.29), channel_id=1, source_target_pairs={{2,4},{4,2},{3,5},{5,3},{10,12},{12,10},{11,13},{13,11},{18,20},{2... | collective-permute-start | bytes 2113544 | tf_op jit(solution)/shard_map/ppermute | solution.py:558
  8.8 0.9 %copy-start.2 = (f32[13,32,4,128]{3,2,1,0:T(4,128)}, f32[13,32,4,128]{3,2,1,0:T(4,128)S(1)}, u32[]{:S(2)}) copy-start(f32[13,32,4,128]{3,2,1,0:T(4,128)S(1)} %collective-permute-done.border) | copy-start | bytes 2555908
  31.9 7.5 %collective-permute-start.3 = (f32[12,32,128]{2,1,0:T(8,128)}, f32[12,32,128]{2,1,0:T(8,128)S(1)}, u32[]{:S(2)}, u32[]{:S(2)}) collective-permute-start(f32[12,32,128]{2,1,0:T(8,128)} %get-tuple-element.31), channel_id=1, source_target_pairs={{0,8},{8,0},{16,24},{24,16},{1,9},{9,1},{17,25},{25,17},{2,10},{10... | collective-permute-start | bytes 589832 | tf_op jit(solution)/shard_map/ppermute | solution.py:563
  32.4 9.8 %copy-start = (f32[43,32,128]{2,1,0:T(8,128)}, f32[43,32,128]{2,1,0:T(8,128)S(1)}, u32[]{:S(2)}) copy-start(f32[43,32,128]{2,1,0:T(8,128)S(1)} %collective-permute-done.1.near) | copy-start | bytes 2113540
  37.7 4.5 %copy-start.1 = (f32[43,32,128]{2,1,0:T(8,128)}, f32[43,32,128]{2,1,0:T(8,128)S(1)}, u32[]{:S(2)}) copy-start(f32[43,32,128]{2,1,0:T(8,128)S(1)} %collective-permute-done.2.far) | copy-start | bytes 2113540
  40.3 11.4 %collective-permute-start.5 = (f32[12,32,128]{2,1,0:T(8,128)S(1)}, f32[12,32,128]{2,1,0:T(8,128)S(1)}, u32[]{:S(2)}, u32[]{:S(2)}) collective-permute-start(f32[12,32,128]{2,1,0:T(8,128)S(1)} %add.20), channel_id=1, source_target_pairs={{0,16},{8,24},{16,0},{24,8},{1,17},{9,25},{17,1},{25,9},{2,18},{10... | collective-permute-start | bytes 589832 | tf_op jit(solution)/shard_map/ppermute | solution.py:569
  40.7 1.5 %collective-permute-start.4 = (f32[2,43,4,128]{3,2,1,0:T(4,128)S(1)}, f32[2,43,4,128]{3,2,1,0:T(4,128)S(1)}, u32[]{:S(2)}, u32[]{:S(2)}) collective-permute-start(f32[2,43,4,128]{3,2,1,0:T(4,128)S(1)} %pad_maximum_fusion.1), channel_id=1, source_target_pairs={{0,1},{1,0},{2,3},{3,2},{4,5},{5,4},{6,7},{7,6},{8,9},{9,8},{10,11... | collective-permute-start | bytes 528392 | tf_op jit(solution)/shard_map/ppermute | solution.py:546
  42.2 0.7 copy-start.3
  51.8 6.0 %collective-permute-start.6 = (f32[2,4,32,128]{3,2,1,0:T(8,128)}, f32[2,4,32,128]{3,2,1,0:T(8,128)S(1)}, u32[]{:S(2)}, u32[]{:S(2)}) collective-permute-start(f32[2,4,32,128]{3,2,1,0:T(8,128)} %get-tuple-element.41), channel_id=1, source_target_pairs={{0,8},{8,0},{16,24},{24,16},{1,9},{9,1},{17,25},{25,17},{2,10},{10... | collective-permute-start | bytes 393224 | tf_op jit(solution)/shard_map/ppermute | solution.py:574
  58.7 8.7 %collective-permute-start.7 = (f32[2,4,32,128]{3,2,1,0:T(8,128)S(1)}, f32[2,4,32,128]{3,2,1,0:T(8,128)S(1)}, u32[]{:S(2)}, u32[]{:S(2)}) collective-permute-start(f32[2,4,32,128]{3,2,1,0:T(8,128)S(1)} %add.23), channel_id=1, source_target_pairs={{0,16},{8,24},{16,0},{24,8},{1,17},{9,25},{17,1},{25,9},{2,18},{10... | collective-permute-start | bytes 393224 | tf_op jit(solution)/shard_map/ppermute | solution.py:574
  61.3 8.8 %collective-permute-start.8 = (f32[12,32,128]{2,1,0:T(8,128)S(1)}, f32[12,32,128]{2,1,0:T(8,128)S(1)}, u32[]{:S(2)}, u32[]{:S(2)}) collective-permute-start(f32[12,32,128]{2,1,0:T(8,128)S(1)} %add.22), channel_id=1, source_target_pairs={{0,8},{8,0},{16,24},{24,16},{1,9},{9,1},{17,25},{25,17},{2,10},{10... | collective-permute-start | bytes 589832 | tf_op jit(solution)/shard_map/ppermute | solution.py:577

commit v3 on v2

--- a/solution.py
+++ b/solution.py
@@ -14,46 +14,47 @@
 F32 = jnp.float32
 
 
+def polynomial(square, start, terms):
+    factors = [1.0]
+    for k in range(start, start + 2 * terms, 2):
+        factors.append(-factors[-1] / ((k + 1) * (k + 2)))
+    result = factors[-1]
+    for factor in factors[-2::-1]:
+        result = factor + square * result
+    return result
+
+
+def sin_cos_near(degrees, terms):
+    angle = degrees * (math.pi / 180.0)
+    square = angle * angle
+    return angle * polynomial(square, 1, terms), polynomial(square, 0, terms + 1)
+
+
 def sin_cos(degrees):
     quadrant = jnp.floor(degrees * (1.0 / 90.0) + 0.5)
-    angle = (degrees - 90.0 * quadrant) * (math.pi / 180.0)
-    square = angle * angle
-    sine = angle * (1.0 + square * (-1.0 / 6 + square * (1.0 / 120 + square * (-1.0 / 5040 + square * (1.0 / 362880)))))
-    cosine = 1.0 + square * (
-        -0.5 + square * (1.0 / 24 + square * (-1.0 / 720 + square * (1.0 / 40320 + square * (-1.0 / 3628800))))
-    )
-    turn = quadrant - 4.0 * jnp.floor(quadrant * 0.25)
-    odd = (turn == 1.0) | (turn == 3.0)
+    sine, cosine = sin_cos_near(degrees - 90.0 * quadrant, 4)
+    odd = (quadrant == 1.0) | (quadrant == 3.0)
     first = jnp.where(odd, cosine, sine)
     second = jnp.where(odd, sine, cosine)
-    return (
-        jnp.where(turn >= 2.0, -first, first),
-        jnp.where((turn == 1.0) | (turn == 2.0), -second, second),
-    )
+    back = (quadrant == 2.0) | (quadrant == 3.0)
+    left = (quadrant == 1.0) | (quadrant == 2.0)
+    return jnp.where(back, -first, first), jnp.where(left, -second, second)
 
 
 def model_rows(vel, eps, delta, tilt, azimuth, mirrored):
-    sin_t, cos_t = sin_cos(tilt)
+    sin_t, cos_t = sin_cos_near(tilt, 6)
     sin_a, cos_a = sin_cos(azimuth)
     nx, ny, nz = sin_t * cos_a, sin_t * sin_a, cos_t
     gain = 1.0 + 2.0 * eps
     root = jnp.sqrt(1.0 + 2.0 * delta)
     half_x = (-0.5 if mirrored else 0.5) * nx
-    return (
-        (nx * nx,) * 2,
-        (ny * ny,) * 2,
-        (half_x * ny,) * 2,
-        (half_x * nz,) * 2,
-        (0.5 * ny * nz,) * 2,
-        (vel * gain, vel),
-        (vel * root,) * 2,
-    )
+    return nx * nx, ny * ny, half_x * ny, half_x * nz, 0.5 * ny * nz, vel * gain, vel, vel * root
 
 
 FACTORS = 7
 SLOTS = 8
 REACH = ITERS
-CHUNKS = 2
+CHUNKS = 4
 
 
 def slot(half, field):
@@ -164,12 +165,26 @@
     return ref.reshape(size, ref.shape[-1])
 
 
-def put_model(coef, layout, plane, half, row, size, raw):
-    parts = model_rows(*raw, half == 1)
-    for i, both in enumerate(parts):
-        flat = flat_view(coef.at[i])
-        for field in range(4):
-            flat[layout.flat(plane, row, slot(half, field), size), :] = both[field % 2]
+def put_model(natural, half, row, size, raw):
+    for i, part in enumerate(model_rows(*raw, half == 1)):
+        natural[half, i, row : row + size, :] = part
+
+
+def spread_model(coef, natural, plane, layout):
+    sublane = lax.broadcasted_iota(jnp.int32, (SLOTS, LANES), 0)
+    is_q, is_mirrored = sublane >= SLOTS // 2, sublane % 4 >= 2
+
+    def cell(i, row):
+        low, high = [natural[half, i, pl.ds(row, SLOTS, stride=0), :] for half in range(2)]
+        return jnp.where(is_mirrored, high, low)
+
+    for begin, first, size in ((0, layout.own, layout.width_y), (layout.width_y, layout.other, REACH)):
+        out = coef.at[:, plane, pl.ds(first, size)]
+        for j in range(size):
+            for i in range(5):
+                out[i, j] = cell(i, begin + j)
+            out[5, j] = jnp.where(is_q, cell(6, begin + j), cell(5, begin + j))
+            out[6, j] = cell(7, begin + j)
 
 
 def products(flat, layout, plane, half, rows):
@@ -180,7 +195,7 @@
 def inner_kernel(
     cover, now, prev, vel, eps, delta, tilt, azimuth, border,
     wave, edge_a, edge_b, edge_c, edge_corr, kept, sent,
-    fa, fb, slopes, sums, coef, corr, in_now, in_prev, raw, raw_int, in_border, load_sems, sems, wave_sems,
+    fa, fb, slopes, sums, coef, corr, in_now, in_prev, raw, raw_int, in_border, natural, load_sems, sems, wave_sems,
 ):
     second, odd = lax.axis_index("gy"), lax.axis_index("shot") % 2
     width_x, width_y = vel.shape[0], vel.shape[1]
@@ -219,7 +234,8 @@
                 else:
                     cells = [raw[n, x, own, :] for n in range(3)]
                     cells += [raw_int[n, x, own, :].astype(F32) for n in range(2)]
-                put_model(coef, layout, i, half, row, size, cells)
+                put_model(natural, half, own.start if own else width_y, size, cells)
+        spread_model(coef, natural, i, layout)
         return 0
 
     for c in range(CHUNKS):
@@ -229,7 +245,8 @@
     out = copies([(coef.at[:, pl.ds(0, ITERS)], edge_c)], sems, 9)
     seam(fa, half_x - 1, rows)
     bufs = (fa, fb)
-    scale = cover[0, 0, 0].astype(F32) / ITERS
+    covered = cover[0, 0, 0].astype(F32)
+    scales = [jnp.where(odd == half, covered, covered / ITERS) for half in range(2)]
 
     def give_wave(i, half):
         x = i if half == 0 else width_x - 1 - i
@@ -244,7 +261,7 @@
                 for own in layout.tiles():
                     product = products(flat, layout, i, half, own)
                     total = product if step == 0 else corr[x, own, :] + product
-                    corr[x, own, :] = scale * total if step == ITERS - 1 else total
+                    corr[x, own, :] = scales[half] * total if step == ITERS - 1 else total
                     if step == ITERS - 1:
                         for field in range(4):
                             spot = layout.flat(i, layout.own + own.start, slot(half, field), TILE)
@@ -290,8 +307,8 @@
 
 def border_kernel(
     cover, edge_a, edge_b, edge_c, edge_corr, near, far, corner, wave_in,
-    wave, image,
-    fa, fb, slopes, sums, coef, corr, sides, corners, in_now, sems,
+    wave, image, image_own,
+    fa, fb, slopes, sums, coef, corr, sides, corners, natural, in_now, picture, sems,
 ):
     second, odd = lax.axis_index("gy"), lax.axis_index("gx") % 2
     width_x, width_y = wave.shape[2], wave.shape[3]
@@ -320,18 +337,19 @@
 
     def fill(j, _):
         for half in range(2):
-            natural = j if half == 0 else ITERS - 1 - j
+            nth = j if half == 0 else ITERS - 1 - j
             shorter = jnp.maximum(j - 1, 0) if half == 0 else jnp.minimum(ITERS - 1 - j, less - 1)
             for own, size, row in layout.pieces():
                 for field in range(4):
                     spot = layout.flat(j, row, slot(half, field), size)
-                    flat_view(fa)[spot, :] = cells(half, field * ITERS + natural, own)
+                    flat_view(fa)[spot, :] = cells(half, field * ITERS + nth, own)
                     flat_view(fb)[spot, :] = cells(half, n_now + field * less + shorter, own)
         for half in range(2):
             shorter = jnp.maximum(j - 1, 0) if half == 0 else jnp.minimum(ITERS - 1 - j, less - 1)
             for own, size, row in layout.pieces():
                 raw = [cells(half, n_now + n_prev + n * less + shorter, own) for n in range(5)]
-                put_model(coef, layout, j, half, row, size, raw)
+                put_model(natural, half, own.start if own else width_y, size, raw)
+        spread_model(coef, natural, j, layout)
         return 0
 
     lax.fori_loop(0, ITERS, fill, 0)
@@ -359,9 +377,9 @@
         return 0
 
     lax.fori_loop(0, ITERS // 2, advance, 0)
-    scale = cover[0, 0, 0].astype(F32) / ITERS
-    corr[...] = scale * corr[...]
-    out = copies([(corr, image)], sems)
+    corr[...] = cover[0, 0, 0].astype(F32) * corr[...]
+    picture[...] = corr[...] * (1.0 / ITERS)
+    out = copies([(picture, image), (corr, image_own)], sems)
     flat = flat_view(fa)
 
     def give(i, _):
@@ -380,7 +398,7 @@
             (in_now.at[1], wave.at[0, :, pl.ds(width_x - ITERS, ITERS)]),
         ],
         sems,
-        1,
+        2,
     )
     for copy in out:
         copy.wait()
@@ -440,7 +458,7 @@
             border[11 + n, x] = needed(int_rows, n, x).astype(F32)
         return 0
 
-    lax.fori_loop(0, width_x, rows, 0)
+    lax.fori_loop(0, width_x // 4, lambda x, _: [rows(4 * x + i, 0) for i in range(4)][0], 0)
     for copy in started[first:]:
         copy.wait()
 
@@ -497,6 +515,7 @@
             vmem((3, width_x, width_y, LANES)),
             pltpu.VMEM((2, width_x, width_y, LANES), jnp.int32),
             vmem(border.shape),
+            vmem((2, FACTORS + 1, rows, LANES)),
             pltpu.SemaphoreType.DMA((CHUNKS, 15)),
             pltpu.SemaphoreType.DMA((16,)),
             pltpu.SemaphoreType.DMA((width_x,)),
@@ -516,15 +535,17 @@
     return pl.pallas_call(
         border_kernel,
         in_specs=[pl.BlockSpec(memory_space=pltpu.SMEM)] + any_specs(8),
-        out_specs=any_specs(2),
-        out_shape=(shape(wave.shape), shape(edge_corr.shape)),
+        out_specs=any_specs(3),
+        out_shape=(shape(wave.shape), shape(edge_corr.shape), shape(edge_corr.shape)),
         scratch_shapes=[vmem(block)] * 4
         + [
             vmem((FACTORS,) + block),
             vmem(edge_corr.shape),
             vmem((2,) + near.shape),
             vmem(corner.shape),
+            vmem((2, FACTORS + 1, rows, LANES)),
             vmem((2, 4, ITERS, width_y, LANES)),
+            vmem(edge_corr.shape),
             pltpu.SemaphoreType.DMA((8,)),
         ],
         input_output_aliases={8: 0},
@@ -548,6 +569,10 @@
 
 def pairs_at(distance):
     return [(i, i ^ distance) for i in range(lax.axis_size("shot"))]
+
+
+def scaled(block):
+    return lax.optimization_barrier(block * (1.0 / ITERS))
 
 
 def local(wave_now, wave_prev, vel_coef, epsilon, delta, tilt, azimuth, aperture):
@@ -559,11 +584,12 @@
     near = lax.ppermute(near, "gx", [(i, i ^ 1) for i in range(columns) if i ^ 1 < columns])
     border = swap_cores(border)
     wave, edge_a, edge_b, edge_c, edge_corr, kept, sent = advance_inner(aperture, *inputs, border)
-    kept, near, far = lax.optimization_barrier((kept, near, far))
-    held = kept + lax.ppermute(sent, "shot", pairs_at(1))
+    received = lax.ppermute(sent, "shot", pairs_at(1))
+    received, near, far = lax.optimization_barrier((received, near, far))
+    held = scaled(kept) + received
     corner = swap_cores(jnp.stack([other_rows(f, 1, second) for f in (near, far)]))
     held, edge_corr = lax.optimization_barrier((held, edge_corr))
-    wave, outside = advance_border(aperture, edge_a, edge_b, edge_c, edge_corr, near, far, corner, wave)
+    wave, outside, outside_own = advance_border(aperture, edge_a, edge_b, edge_c, edge_corr, near, far, corner, wave)
     distance = 2
     while distance < lax.axis_size("shot"):
         held = held + lax.ppermute(held, "shot", pairs_at(distance))
@@ -571,7 +597,8 @@
     held, outside = lax.optimization_barrier((held, outside))
     distance = 1
     while distance < lax.axis_size("shot"):
-        outside = outside + lax.ppermute(outside, "shot", pairs_at(distance))
+        own = scaled(outside_own) if distance == 1 else outside
+        outside = own + lax.ppermute(outside, "shot", pairs_at(distance))
         if distance == 1:
             held, outside = lax.optimization_barrier((held, outside))
             other = lax.ppermute(held, "shot", pairs_at(1))

time: 72.4 us -> 70.2 us (0.970)
  waiting for transfers between devices: 22.3 us -> 20.5 us
    mul x0 -> x2, other arithmetic: none -> 1.86 us  [scaled(): return lax.optimization_barrier(block * (1.0 / ITERS))]
    add x3, other arithmetic: 1.9 us -> 0.07 us  [the longest x2 0.04 us: local(): outside = own + lax.ppermute(outside, 'shot', pairs_at(distance))]
    ppermute x3, waiting for transfers between devices: 12.9 us -> 11.6 us  [the longest x2 10.3 us: local(): outside = own + lax.ppermute(outside, 'shot', pairs_at(distance))]
  transfers between devices with their start and end apart: 9 -> 9, of which waited for: 7 -> 6; matrix products, arithmetic and copies ran while one was open for 0% -> 3% of each run, Pallas kernels for 43% -> 44%
where the time goes in v3:
time: 70.2 us; the launch traced here: 68.8 us
  Pallas kernels  34 us (48%)
  waiting for transfers between devices  20.5 us (29%)
  starting transfers between devices  8.49 us (12%)
  other arithmetic  2.85 us (4%)
  local copies, waits for them, and re-layouts  1.65 us (2%)
  between operations  1.42 us (2%)
    pallas_call x1, Pallas kernels, advance_inner(): pl.pallas_call(inner_kernel, in_specs=[pl.BlockSpec(memory_space=pltpu.SM...  21.7 us
    ppermute x2, waiting for transfers between devices, local(): outside = own + lax.ppermute(outside, 'shot', pairs_at(distance))  10.3 us
    pallas_call x1, Pallas kernels, advance_border(): pl.pallas_call(border_kernel, in_specs=[pl.BlockSpec(memory_space=pltpu.S...  8.76 us
    ppermute x1, waiting for transfers between devices, local(): lax.ppermute(far, 'gx', [(i, j) for i in range(1, columns - 1) for j in [...  4.73 us
    pallas_call x1, Pallas kernels, pack(): pl.pallas_call(pack_kernel, in_specs=any_specs(7), out_specs=[pl.BlockSpe...  3.52 us
    ppermute x2, starting transfers between devices, local(): outside = own + lax.ppermute(outside, 'shot', pairs_at(distance))  3.04 us
    ppermute x1, waiting for transfers between devices, local(): other = lax.ppermute(held, 'shot', pairs_at(1))  2.73 us
    ppermute x1, starting transfers between devices, local(): lax.ppermute(far, 'gx', [(i, j) for i in range(1, columns - 1) for j in [...  2.36 us
  transfers between devices with their start and end apart: 9, of which 6 were waited for; matrix products, arithmetic and copies ran while one was open for 3% of the time, Pallas kernels for 44%

profile of v3, /device:TPU:28, one launch (start us, length us, event | category | flops | bytes accessed | tf_op | source)
XLA Modules:
  0.0 68.8 jit_solution(10750811702086638647)
XLA Ops:
  0.6 3.5 %pack_borders.1 = (f32[43,32,128]{2,1,0:T(8,128)}, f32[43,32,128]{2,1,0:T(8,128)}, f32[13,32,4,128]{3,2,1,0:T(4,128)}) custom-call(f32[1,4,32,32,128]{4,3,2,1,0:T(8,128)} %now.3, f32[1,4,32,32,128]{4,3,2,1,0:T(8,128)} %prev.3, f32[32,32,128]{2,1,0:T(8,128)} %vel.3, f32[32,32,128]{2,1,0:T(8,128)} %eps.3, f32[32,32,128]{2,1,0:T(8,128)} %delta.3, ...), custom_call_target="tpu_custom_call" | custom-call | flops 1000000 | bytes 8000000 | tf_op jit(solution)/shard_map/pack_borders/pallas_call | solution.py:470
  4.2 0.1 collective-permute-start
  4.2 1.6 %collective-permute-start.2 = (f32[43,32,128]{2,1,0:T(8,128)}, f32[43,32,128]{2,1,0:T(8,128)S(1)}, u32[]{:S(2)}, u32[]{:S(2)}) collective-permute-start(f32[43,32,128]{2,1,0:T(8,128)} %get-tuple-element.30), channel_id=1, source_target_pairs={{0,2},{2,0},{4,6},{6,4},{1,3},{3,1},{5,7},{7,5},{8,10},{10,8},{12,... | collective-permute-start | bytes 2113544 | tf_op jit(solution)/shard_map/ppermute | solution.py:584
  5.8 2.4 %collective-permute-start.3 = (f32[43,32,128]{2,1,0:T(8,128)}, f32[43,32,128]{2,1,0:T(8,128)S(1)}, u32[]{:S(2)}, u32[]{:S(2)}) collective-permute-start(f32[43,32,128]{2,1,0:T(8,128)} %get-tuple-element.31), channel_id=1, source_target_pairs={{2,4},{4,2},{3,5},{5,3},{10,12},{12,10},{11,13},{13,11},{18,20},{2... | collective-permute-start | bytes 2113544 | tf_op jit(solution)/shard_map/ppermute | solution.py:583
  8.8 0.0 collective-permute-done.border
  8.8 0.0 copy-start.2
  8.8 0.9 %copy-done.2 = f32[13,32,4,128]{3,2,1,0:T(4,128)} copy-done((f32[13,32,4,128]{3,2,1,0:T(4,128)}, f32[13,32,4,128]{3,2,1,0:T(4,128)S(1)}, u32[]{:S(2)}) %copy-start.2) | copy-done | bytes 851992
  9.8 21.7 %inner_steps.1 = (f32[1,4,32,32,128]{4,3,2,1,0:T(8,128)}, f32[4,38,8,128]{3,2,1,0:T(8,128)}, f32[5,38,8,128]{3,2,1,0:T(8,128)}, f32[7,4,38,8,128]{4,3,2,1,0:T(8,...) custom-call(s32[1,1,1]{2,1,0:T(1,128)S(6)} %copy.12.cover, ...), custom_call_target="tpu_custom_call" | custom-call | flops 80000000 | bytes 200000000 | tf_op jit(solution)/shard_map/inner_steps/pallas_call | solution.py:496
  31.5 0.5 collective-permute-start.1
  32.0 0.9 %broadcast_multiply_fusion = f32[12,32,128]{2,1,0:T(8,128)S(1)} fusion(f32[12,32,128]{2,1,0:T(8,128)} %get-tuple-element.28), kind=kLoop, calls=%fused_computation.2 | loop fusion | flops 49152 | bytes 393216 | tf_op jit(solution)/shard_map/mul | solution.py:575
  32.9 0.0 collective-permute-done.2.near
  32.9 0.0 copy-start
  33.0 4.7 %collective-permute-done.3.far = f32[43,32,128]{2,1,0:T(8,128)S(1)} collective-permute-done((f32[43,32,128]{2,1,0:T(8,128)}, f32[43,32,128]{2,1,0:T(8,128)S(1)}, u32[]{:S(2)}, u32[]{:S(2)}) %collective-permute-start.3) | collective-permute-done | bytes 704544 | tf_op jit(solution)/shard_map/ppermute | solution.py:583
  37.7 0.0 copy-start.1
  37.7 1.2 %collective-permute-done.1 = f32[12,32,128]{2,1,0:T(8,128)S(1)} collective-permute-done((f32[12,32,128]{2,1,0:T(8,128)}, f32[12,32,128]{2,1,0:T(8,128)S(1)}, u32[]{:S(2)}, u32[]{:S(2)}) %collective-permute-start.1) | collective-permute-done | bytes 196640 | tf_op jit(solution)/shard_map/ppermute | solution.py:587
  39.0 0.4 collective-permute-start.5
  39.4 0.1 dynamic-slice_bitcast_fusion
  39.5 0.1 collective-permute-start.4
  39.5 1.4 %collective-permute-done.4.corner = f32[2,43,4,128]{3,2,1,0:T(4,128)S(1)} collective-permute-done((f32[2,43,4,128]{3,2,1,0:T(4,128)S(1)}, f32[2,43,4,128]{3,2,1,0:T(4,128)S(1)}, u32[]{:S(2)}, u32[]{:S(2)}) %collective-permute-start.4) | collective-permute-done | bytes 176160 | tf_op jit(solution)/shard_map/ppermute | solution.py:567
  40.9 0.0 copy-done
  40.9 0.0 copy-done.1
  40.9 0.7 copy-done.3
  41.6 8.8 %border_steps.1 = (f32[1,4,32,32,128]{4,3,2,1,0:T(8,128)}, f32[2,4,32,128]{3,2,1,0:T(8,128)}, f32[2,4,32,128]{3,2,1,0:T(8,128)}) custom-call(s32[1,1,1]{2,1,0:T(1,128)S(6)} %copy.12.cover, f32[4,38,8,128]{3,2,1,0:T(8,128)} %get-tuple-element.25.edge_a, f32[5,38,8,128]{3,2,1,0:T(8,128)} %get-tuple-element.26.edge_b, ...), custom_call_target="tpu_custom_call", output_to_operand_aliasing={{0}: (8, {})} | custom-call | flops 20000000 | bytes 20000000 | tf_op jit(solution)/shard_map/border_steps/pallas_call | solution.py:535
  50.4 0.0 collective-permute-done.5
  50.4 0.4 collective-permute-start.6
  50.8 0.9 %broadcast_multiply_fusion.1 = f32[2,4,32,128]{3,2,1,0:T(8,128)S(1)} fusion(f32[2,4,32,128]{3,2,1,0:T(8,128)} %get-tuple-element.42), kind=kLoop, calls=%fused_computation.9 | loop fusion | flops 32768 | bytes 262144 | tf_op jit(solution)/shard_map/mul | solution.py:575
  51.7 4.8 %collective-permute-done.6 = f32[2,4,32,128]{3,2,1,0:T(8,128)S(1)} collective-permute-done((f32[2,4,32,128]{3,2,1,0:T(8,128)}, f32[2,4,32,128]{3,2,1,0:T(8,128)S(1)}, u32[]{:S(2)}, u32[]{:S(2)}) %collective-permute-start.6) | collective-permute-done | bytes 131104 | tf_op jit(solution)/shard_map/ppermute | solution.py:601
  56.5 2.7 %collective-permute-start.7 = (f32[2,4,32,128]{3,2,1,0:T(8,128)S(1)}, f32[2,4,32,128]{3,2,1,0:T(8,128)S(1)}, u32[]{:S(2)}, u32[]{:S(2)}) collective-permute-start(f32[2,4,32,128]{3,2,1,0:T(8,128)S(1)} %add.23), channel_id=1, source_target_pairs={{0,16},{8,24},{16,0},{24,8},{1,17},{9,25},{17,1},{25,9},{2,18},{10... | collective-permute-start | bytes 393224 | tf_op jit(solution)/shard_map/ppermute | solution.py:601
  59.2 0.4 collective-permute-start.8
  59.6 5.6 %collective-permute-done.7 = f32[2,4,32,128]{3,2,1,0:T(8,128)S(1)} collective-permute-done((f32[2,4,32,128]{3,2,1,0:T(8,128)S(1)}, f32[2,4,32,128]{3,2,1,0:T(8,128)S(1)}, u32[]{:S(2)}, u32[]{:S(2)}) %collective-permute-start.7) | collective-permute-done | bytes 131104 | tf_op jit(solution)/shard_map/ppermute | solution.py:601
  65.2 2.7 %collective-permute-done.8 = f32[12,32,128]{2,1,0:T(8,128)S(1)} collective-permute-done((f32[12,32,128]{2,1,0:T(8,128)S(1)}, f32[12,32,128]{2,1,0:T(8,128)S(1)}, u32[]{:S(2)}, u32[]{:S(2)}) %collective-permute-start.8) | collective-permute-done | bytes 196640 | tf_op jit(solution)/shard_map/ppermute | solution.py:604
  68.0 0.8 %pad_maximum_fusion = f32[32,32,128]{2,1,0:T(8,128)} fusion(f32[4,32,128]{2,1,0:T(8,128)S(1)} %get-tuple-element.49, f32[12,32,128]{2,1,0:T(8,128)S(1)} %get-tuple-element.47, f32[12,32,128]{2,1,0:T(8,128)S(1)} %get-tuple-element.46, f32[4,32,128]{2,1,0:T(8,128)S(1)} %get-tuple-element.48), kind=kLoop, calls=%fused_computation | loop fusion | flops 393216 | bytes 1048576 | tf_op jit(solution)/shard_map/concatenate | solution.py:608
  (8 shorter events, 0.2 us)
Async XLA Ops:
  4.2 4.7 %collective-permute-start = (f32[13,32,4,128]{3,2,1,0:T(4,128)}, f32[13,32,4,128]{3,2,1,0:T(4,128)S(1)}, u32[]{:S(2)}, u32[]{:S(2)}) collective-permute-start(f32[13,32,4,128]{3,2,1,0:T(4,128)} %get-tuple-element.24), channel_id=1, source_target_pairs={{0,1},{1,0},{2,3},{3,2},{4,5},{5,4},{6,7},{7,6},{8,9},{9,8},{10,11... | collective-permute-start | bytes 2555912 | tf_op jit(solution)/shard_map/ppermute | solution.py:567
  4.2 28.7 %collective-permute-start.2 = (f32[43,32,128]{2,1,0:T(8,128)}, f32[43,32,128]{2,1,0:T(8,128)S(1)}, u32[]{:S(2)}, u32[]{:S(2)}) collective-permute-start(f32[43,32,128]{2,1,0:T(8,128)} %get-tuple-element.30), channel_id=1, source_target_pairs={{0,2},{2,0},{4,6},{6,4},{1,3},{3,1},{5,7},{7,5},{8,10},{10,8},{12,... | collective-permute-start | bytes 2113544 | tf_op jit(solution)/shard_map/ppermute | solution.py:584
  5.8 31.9 %collective-permute-start.3 = (f32[43,32,128]{2,1,0:T(8,128)}, f32[43,32,128]{2,1,0:T(8,128)S(1)}, u32[]{:S(2)}, u32[]{:S(2)}) collective-permute-start(f32[43,32,128]{2,1,0:T(8,128)} %get-tuple-element.31), channel_id=1, source_target_pairs={{2,4},{4,2},{3,5},{5,3},{10,12},{12,10},{11,13},{13,11},{18,20},{2... | collective-permute-start | bytes 2113544 | tf_op jit(solution)/shard_map/ppermute | solution.py:583
  8.8 0.9 %copy-start.2 = (f32[13,32,4,128]{3,2,1,0:T(4,128)}, f32[13,32,4,128]{3,2,1,0:T(4,128)S(1)}, u32[]{:S(2)}) copy-start(f32[13,32,4,128]{3,2,1,0:T(4,128)S(1)} %collective-permute-done.border) | copy-start | bytes 2555908
  31.5 7.5 %collective-permute-start.1 = (f32[12,32,128]{2,1,0:T(8,128)}, f32[12,32,128]{2,1,0:T(8,128)S(1)}, u32[]{:S(2)}, u32[]{:S(2)}) collective-permute-start(f32[12,32,128]{2,1,0:T(8,128)} %get-tuple-element.29), channel_id=1, source_target_pairs={{0,8},{8,0},{16,24},{24,16},{1,9},{9,1},{17,25},{25,17},{2,10},{10... | collective-permute-start | bytes 589832 | tf_op jit(solution)/shard_map/ppermute | solution.py:587
  32.9 8.0 %copy-start = (f32[43,32,128]{2,1,0:T(8,128)}, f32[43,32,128]{2,1,0:T(8,128)S(1)}, u32[]{:S(2)}) copy-start(f32[43,32,128]{2,1,0:T(8,128)S(1)} %collective-permute-done.2.near) | copy-start | bytes 2113540
  37.7 3.3 %copy-start.1 = (f32[43,32,128]{2,1,0:T(8,128)}, f32[43,32,128]{2,1,0:T(8,128)S(1)}, u32[]{:S(2)}) copy-start(f32[43,32,128]{2,1,0:T(8,128)S(1)} %collective-permute-done.3.far) | copy-start | bytes 2113540
  39.0 11.4 %collective-permute-start.5 = (f32[12,32,128]{2,1,0:T(8,128)S(1)}, f32[12,32,128]{2,1,0:T(8,128)S(1)}, u32[]{:S(2)}, u32[]{:S(2)}) collective-permute-start(f32[12,32,128]{2,1,0:T(8,128)S(1)} %add.20), channel_id=1, source_target_pairs={{0,16},{8,24},{16,0},{24,8},{1,17},{9,25},{17,1},{25,9},{2,18},{10... | collective-permute-start | bytes 589832 | tf_op jit(solution)/shard_map/ppermute | solution.py:595
  39.5 1.5 %collective-permute-start.4 = (f32[2,43,4,128]{3,2,1,0:T(4,128)S(1)}, f32[2,43,4,128]{3,2,1,0:T(4,128)S(1)}, u32[]{:S(2)}, u32[]{:S(2)}) collective-permute-start(f32[2,43,4,128]{3,2,1,0:T(4,128)S(1)} %pad_maximum_fusion.1), channel_id=1, source_target_pairs={{0,1},{1,0},{2,3},{3,2},{4,5},{5,4},{6,7},{7,6},{8,9},{9,8},{10,11... | collective-permute-start | bytes 528392 | tf_op jit(solution)/shard_map/ppermute | solution.py:567
  40.9 0.7 copy-start.3
  50.4 6.1 %collective-permute-start.6 = (f32[2,4,32,128]{3,2,1,0:T(8,128)}, f32[2,4,32,128]{3,2,1,0:T(8,128)S(1)}, u32[]{:S(2)}, u32[]{:S(2)}) collective-permute-start(f32[2,4,32,128]{3,2,1,0:T(8,128)} %get-tuple-element.43), channel_id=1, source_target_pairs={{0,8},{8,0},{16,24},{24,16},{1,9},{9,1},{17,25},{25,17},{2,10},{10... | collective-permute-start | bytes 393224 | tf_op jit(solution)/shard_map/ppermute | solution.py:601
  56.5 8.7 %collective-permute-start.7 = (f32[2,4,32,128]{3,2,1,0:T(8,128)S(1)}, f32[2,4,32,128]{3,2,1,0:T(8,128)S(1)}, u32[]{:S(2)}, u32[]{:S(2)}) collective-permute-start(f32[2,4,32,128]{3,2,1,0:T(8,128)S(1)} %add.23), channel_id=1, source_target_pairs={{0,16},{8,24},{16,0},{24,8},{1,17},{9,25},{17,1},{25,9},{2,18},{10... | collective-permute-start | bytes 393224 | tf_op jit(solution)/shard_map/ppermute | solution.py:601
  59.2 8.8 %collective-permute-start.8 = (f32[12,32,128]{2,1,0:T(8,128)S(1)}, f32[12,32,128]{2,1,0:T(8,128)S(1)}, u32[]{:S(2)}, u32[]{:S(2)}) collective-permute-start(f32[12,32,128]{2,1,0:T(8,128)S(1)} %add.22), channel_id=1, source_target_pairs={{0,8},{8,0},{16,24},{24,16},{1,9},{9,1},{17,25},{25,17},{2,10},{10... | collective-permute-start | bytes 589832 | tf_op jit(solution)/shard_map/ppermute | solution.py:604

commit v4 on v3

--- a/solution.py
+++ b/solution.py
@@ -27,7 +27,7 @@
 def sin_cos_near(degrees, terms):
     angle = degrees * (math.pi / 180.0)
     square = angle * angle
-    return angle * polynomial(square, 1, terms), polynomial(square, 0, terms + 1)
+    return angle * polynomial(square, 1, terms), polynomial(square, 0, terms)
 
 
 def sin_cos(degrees):
@@ -42,7 +42,7 @@
 
 
 def model_rows(vel, eps, delta, tilt, azimuth, mirrored):
-    sin_t, cos_t = sin_cos_near(tilt, 6)
+    sin_t, cos_t = sin_cos_near(tilt, 5)
     sin_a, cos_a = sin_cos(azimuth)
     nx, ny, nz = sin_t * cos_a, sin_t * sin_a, cos_t
     gain = 1.0 + 2.0 * eps
@@ -95,6 +95,7 @@
     first = 1 + (1 + step) * layout.second
     edges = lane_ends()
     is_q = lax.broadcasted_iota(jnp.int32, (SLOTS, LANES), 0) >= SLOTS // 2
+    sign, weight = jnp.where(is_q, 1.0, -1.0), jnp.where(is_q, 2.0, 4.0)
     around = pl.ds(first - 1, count + 2)
     within = pl.ds(first, count)
 
@@ -106,25 +107,23 @@
 
         def column(j):
             below, above = f_m[j], f_p[j]
-            g[2, j], h[1, j] = ahead = z_terms(above, *edges)
-            return above - below, above + below, f_0[j], g[1, j], ahead[0]
+            g[2, j], h[1, j] = z_terms(above, *edges)
+            return above - below, above + below, f_0[j], g[1, j]
 
         before, here = column(0), column(1)
         for j in range(count):
             after = column(j + 2)
             a, b, d, e, k, c1, c2 = [factor[j] for factor in factors]
             sum_z = h[0, j + 1]
+            sum_y = after[2] + before[2]
+            mixed = (
+                (a * (here[1] - sum_z) + b * (sum_y - sum_z))
+                + d * (after[0] - before[0])
+                + (e * (g[2, j + 1] - g[0, j + 1]) + k * (after[3] - before[3]))
+            )
+            plain = jnp.where(is_q, sum_z, here[1] + sum_y) - weight * here[2]
+            mine = plain + sign * mixed
             twice = here[2] + here[2]
-            base = sum_z - twice
-            over_x = here[1] - sum_z
-            over_y = (after[2] + before[2]) - sum_z
-            along = (
-                (base + a * over_x)
-                + (b * over_y + d * (after[0] - before[0]))
-                + (e * (here[4] - g[0, j + 1]) + k * (after[3] - before[3]))
-            )
-            across = ((over_x + over_y) + 3.0 * base) - along
-            mine = jnp.where(is_q, along, across)
             out[j] = (twice - out[j]) + (c1 * mine + c2 * pltpu.roll(mine, SLOTS // 2, 0))
             before, here = here, after
         done(x)
@@ -204,7 +203,8 @@
     rows = layout.total
     chunk = half_x // CHUNKS
     loads = []
-    for c in range(CHUNKS):
+
+    def load(c):
         pairs = [(border, in_border)] if c == 0 else []
         for start in (c * chunk, width_x - (c + 1) * chunk):
             at = pl.ds(start, chunk)
@@ -212,6 +212,9 @@
             pairs += [(array.at[at], raw.at[n, at]) for n, array in enumerate((vel, eps, delta))]
             pairs += [(array.at[at], raw_int.at[n, at]) for n, array in enumerate((tilt, azimuth))]
         loads.append(copies(pairs, load_sems.at[c]))
+
+    load(0)
+    load(1)
     clear_ends((fa, fb), rows)
 
     def fill(i, _):
@@ -241,6 +244,8 @@
     for c in range(CHUNKS):
         for copy in loads[c]:
             copy.wait()
+        if c + 2 < CHUNKS:
+            load(c + 2)
         lax.fori_loop(c * chunk, (c + 1) * chunk, fill, 0)
     out = copies([(coef.at[:, pl.ds(0, ITERS)], edge_c)], sems, 9)
     seam(fa, half_x - 1, rows)
@@ -580,27 +585,29 @@
     columns = lax.axis_size("gx")
     inputs = (wave_now, wave_prev, vel_coef, epsilon, delta, tilt, azimuth)
     near, far, border = pack(*inputs)
-    far = lax.ppermute(far, "gx", [(i, j) for i in range(1, columns - 1) for j in [i + 1 if i % 2 else i - 1]])
     near = lax.ppermute(near, "gx", [(i, i ^ 1) for i in range(columns) if i ^ 1 < columns])
     border = swap_cores(border)
+    far, border = lax.optimization_barrier((far, border))
+    far = lax.ppermute(far, "gx", [(i, j) for i in range(1, columns - 1) for j in [i + 1 if i % 2 else i - 1]])
     wave, edge_a, edge_b, edge_c, edge_corr, kept, sent = advance_inner(aperture, *inputs, border)
     received = lax.ppermute(sent, "shot", pairs_at(1))
+    mine = scaled(kept)
     received, near, far = lax.optimization_barrier((received, near, far))
-    held = scaled(kept) + received
     corner = swap_cores(jnp.stack([other_rows(f, 1, second) for f in (near, far)]))
+    received, corner = lax.optimization_barrier((received, corner))
+    held = mine + received
     held, edge_corr = lax.optimization_barrier((held, edge_corr))
     wave, outside, outside_own = advance_border(aperture, edge_a, edge_b, edge_c, edge_corr, near, far, corner, wave)
     distance = 2
     while distance < lax.axis_size("shot"):
         held = held + lax.ppermute(held, "shot", pairs_at(distance))
         distance *= 2
-    held, outside = lax.optimization_barrier((held, outside))
-    distance = 1
+    held, outside_own = lax.optimization_barrier((held, outside_own))
+    own, distance = scaled(outside_own), 1
     while distance < lax.axis_size("shot"):
-        own = scaled(outside_own) if distance == 1 else outside
-        outside = own + lax.ppermute(outside, "shot", pairs_at(distance))
+        own = outside = own + lax.ppermute(outside, "shot", pairs_at(distance))
         if distance == 1:
-            held, outside = lax.optimization_barrier((held, outside))
+            held, own, outside = lax.optimization_barrier((held, own, outside))
             other = lax.ppermute(held, "shot", pairs_at(1))
         distance *= 2
     even = lax.axis_index("shot") % 2 == 0

time: 70.2 us -> 68 us (0.969)
  Pallas kernels: 34 us -> 32.5 us
  local copies, waits for them, and re-layouts: 1.65 us -> 0.3 us
    ppermute x1, waiting for transfers between devices: 1.23 us -> 6.64 us  [local(): received = lax.ppermute(sent, 'shot', pairs_at(1))]
    ppermute x1, waiting for transfers between devices: 4.73 us -> 0.01 us  [local(): lax.ppermute(far, 'gx', [(i, j) for i in range(1, columns - 1) for j in [...]
    ppermute x1, waiting for transfers between devices: 0.01 us -> 2.37 us  [local(): held = held + lax.ppermute(held, 'shot', pairs_at(distance))]
    ppermute x2, waiting for transfers between devices: 10.3 us -> 8.07 us  [local(): own = outside = own + lax.ppermute(outside, 'shot', pairs_at(distance))]
    unnamed x8, local copies, waits for them, and re-layouts: 1.59 us -> 0.24 us
    pallas_call x1, Pallas kernels: 21.7 us -> 20.5 us  [advance_inner(): pl.pallas_call(inner_kernel, in_specs=[pl.BlockSpec(memory_space=pltpu.SM...]
    ppermute x1, starting transfers between devices: 2.36 us -> 3.34 us  [local(): lax.ppermute(far, 'gx', [(i, j) for i in range(1, columns - 1) for j in [...]
    ppermute x1, waiting for transfers between devices: 2.73 us -> 1.97 us  [local(): other = lax.ppermute(held, 'shot', pairs_at(1))]
  transfers between devices with their start and end apart: 9 -> 9, of which waited for: 6 -> 7; matrix products, arithmetic and copies ran while one was open for 3% -> 3% of each run, Pallas kernels for 44% -> 43%
where the time goes in v4:
time: 68 us; the launch traced here: 66.6 us
  Pallas kernels  32.5 us (48%)
  waiting for transfers between devices  20.4 us (30%)
  starting transfers between devices  9.1 us (13%)
  other arithmetic  2.93 us (4%)
  between operations  1.39 us (2%)
    pallas_call x1, Pallas kernels, advance_inner(): pl.pallas_call(inner_kernel, in_specs=[pl.BlockSpec(memory_space=pltpu.SM...  20.5 us
    pallas_call x1, Pallas kernels, advance_border(): pl.pallas_call(border_kernel, in_specs=[pl.BlockSpec(memory_space=pltpu.S...  8.48 us
    ppermute x2, waiting for transfers between devices, local(): own = outside = own + lax.ppermute(outside, 'shot', pairs_at(distance))  8.07 us
    ppermute x1, waiting for transfers between devices, local(): received = lax.ppermute(sent, 'shot', pairs_at(1))  6.64 us
    pallas_call x1, Pallas kernels, pack(): pl.pallas_call(pack_kernel, in_specs=any_specs(7), out_specs=[pl.BlockSpe...  3.52 us
    ppermute x1, starting transfers between devices, local(): lax.ppermute(far, 'gx', [(i, j) for i in range(1, columns - 1) for j in [...  3.34 us
    ppermute x2, starting transfers between devices, local(): own = outside = own + lax.ppermute(outside, 'shot', pairs_at(distance))  2.68 us
    ppermute x1, waiting for transfers between devices, local(): held = held + lax.ppermute(held, 'shot', pairs_at(distance))  2.37 us
  transfers between devices with their start and end apart: 9, of which 7 were waited for; matrix products, arithmetic and copies ran while one was open for 3% of the time, Pallas kernels for 43%

profile of v4, /device:TPU:28, one launch (start us, length us, event | category | flops | bytes accessed | tf_op | source)
XLA Modules:
  0.0 66.6 jit_solution(4131563981276756130)
XLA Ops:
  0.6 3.5 %pack_borders.1 = (f32[43,32,128]{2,1,0:T(8,128)}, f32[43,32,128]{2,1,0:T(8,128)}, f32[13,32,4,128]{3,2,1,0:T(4,128)}) custom-call(f32[1,4,32,32,128]{4,3,2,1,0:T(8,128)} %now.3, f32[1,4,32,32,128]{4,3,2,1,0:T(8,128)} %prev.3, f32[32,32,128]{2,1,0:T(8,128)} %vel.3, f32[32,32,128]{2,1,0:T(8,128)} %eps.3, f32[32,32,128]{2,1,0:T(8,128)} %delta.3, ...), custom_call_target="tpu_custom_call" | custom-call | flops 1000000 | bytes 8000000 | tf_op jit(solution)/shard_map/pack_borders/pallas_call | solution.py:475
  4.2 0.1 collective-permute-start
  4.2 1.6 %collective-permute-start.2 = (f32[43,32,128]{2,1,0:T(8,128)}, f32[43,32,128]{2,1,0:T(8,128)S(1)}, u32[]{:S(2)}, u32[]{:S(2)}) collective-permute-start(f32[43,32,128]{2,1,0:T(8,128)} %get-tuple-element.37), channel_id=1, source_target_pairs={{0,2},{2,0},{4,6},{6,4},{1,3},{3,1},{5,7},{7,5},{8,10},{10,8},{12,... | collective-permute-start | bytes 2113544 | tf_op jit(solution)/shard_map/ppermute | solution.py:588
  5.8 1.0 %collective-permute-done.border = f32[13,32,4,128]{3,2,1,0:T(4,128)S(1)} collective-permute-done((f32[13,32,4,128]{3,2,1,0:T(4,128)}, f32[13,32,4,128]{3,2,1,0:T(4,128)S(1)}, u32[]{:S(2)}, u32[]{:S(2)}) %collective-permute-start) | collective-permute-done | bytes 852000 | tf_op jit(solution)/shard_map/ppermute | solution.py:572
  6.8 0.0 copy-start.2
  6.8 3.3 %collective-permute-start.3 = (f32[43,32,128]{2,1,0:T(8,128)}, f32[43,32,128]{2,1,0:T(8,128)S(1)}, u32[]{:S(2)}, u32[]{:S(2)}) collective-permute-start(f32[43,32,128]{2,1,0:T(8,128)} %get-tuple-element.38), channel_id=1, source_target_pairs={{2,4},{4,2},{3,5},{5,3},{10,12},{12,10},{11,13},{13,11},{18,20},{2... | collective-permute-start | bytes 2113544 | tf_op jit(solution)/shard_map/ppermute | solution.py:591
  10.8 0.0 copy-done.2
  10.8 20.5 %inner_steps.1 = (f32[1,4,32,32,128]{4,3,2,1,0:T(8,128)}, f32[4,38,8,128]{3,2,1,0:T(8,128)}, f32[5,38,8,128]{3,2,1,0:T(8,128)}, f32[7,4,38,8,128]{4,3,2,1,0:T(8,...) custom-call(s32[1,1,1]{2,1,0:T(1,128)S(6)} %copy.12.cover, ...), custom_call_target="tpu_custom_call" | custom-call | flops 80000000 | bytes 200000000 | tf_op jit(solution)/shard_map/inner_steps/pallas_call | solution.py:501
  31.3 0.5 collective-permute-start.1
  31.8 0.0 collective-permute-done.2.near
  31.8 0.0 copy-start
  31.8 6.6 %collective-permute-done.1 = f32[12,32,128]{2,1,0:T(8,128)S(1)} collective-permute-done((f32[12,32,128]{2,1,0:T(8,128)}, f32[12,32,128]{2,1,0:T(8,128)S(1)}, u32[]{:S(2)}, u32[]{:S(2)}) %collective-permute-start.1) | collective-permute-done | bytes 196640 | tf_op jit(solution)/shard_map/ppermute | solution.py:593
  38.5 0.0 collective-permute-done.3.far
  38.5 0.0 copy-start.1
  38.5 0.1 dynamic-slice_bitcast_fusion
  38.6 0.1 collective-permute-start.4
  38.7 1.0 %broadcast_multiply_fusion = f32[12,32,128]{2,1,0:T(8,128)S(1)} fusion(f32[12,32,128]{2,1,0:T(8,128)} %get-tuple-element.35), kind=kLoop, calls=%fused_computation.2 | loop fusion | flops 49152 | bytes 393216 | tf_op jit(solution)/shard_map/mul | solution.py:580
  39.7 0.4 collective-permute-done.4.corner
  40.1 0.4 collective-permute-start.5
  40.5 0.0 copy-done
  40.5 0.0 copy-done.1
  40.5 0.2 copy-done.3
  40.7 8.5 %border_steps.1 = (f32[1,4,32,32,128]{4,3,2,1,0:T(8,128)}, f32[2,4,32,128]{3,2,1,0:T(8,128)}, f32[2,4,32,128]{3,2,1,0:T(8,128)}) custom-call(s32[1,1,1]{2,1,0:T(1,128)S(6)} %copy.12.cover, f32[4,38,8,128]{3,2,1,0:T(8,128)} %get-tuple-element.32.edge_a, f32[5,38,8,128]{3,2,1,0:T(8,128)} %get-tuple-element.33.edge_b, ...), custom_call_target="tpu_custom_call", output_to_operand_aliasing={{0}: (8, {})} | custom-call | flops 20000000 | bytes 20000000 | tf_op jit(solution)/shard_map/border_steps/pallas_call | solution.py:540
  49.2 0.5 collective-permute-start.6
  49.7 2.4 %collective-permute-done.5 = f32[12,32,128]{2,1,0:T(8,128)S(1)} collective-permute-done((f32[12,32,128]{2,1,0:T(8,128)S(1)}, f32[12,32,128]{2,1,0:T(8,128)S(1)}, u32[]{:S(2)}, u32[]{:S(2)}) %collective-permute-start.5) | collective-permute-done | bytes 196640 | tf_op jit(solution)/shard_map/ppermute | solution.py:603
  52.1 0.9 %broadcast_multiply_fusion.1 = f32[2,4,32,128]{3,2,1,0:T(8,128)S(1)} fusion(f32[2,4,32,128]{3,2,1,0:T(8,128)} %get-tuple-element.51), kind=kLoop, calls=%fused_computation.9 | loop fusion | flops 32768 | bytes 262144 | tf_op jit(solution)/shard_map/mul | solution.py:580
  53.1 2.1 %collective-permute-done.6 = f32[2,4,32,128]{3,2,1,0:T(8,128)S(1)} collective-permute-done((f32[2,4,32,128]{3,2,1,0:T(8,128)}, f32[2,4,32,128]{3,2,1,0:T(8,128)S(1)}, u32[]{:S(2)}, u32[]{:S(2)}) %collective-permute-start.6) | collective-permute-done | bytes 131104 | tf_op jit(solution)/shard_map/ppermute | solution.py:608
  55.2 2.2 %collective-permute-start.7 = (f32[2,4,32,128]{3,2,1,0:T(8,128)S(1)}, f32[2,4,32,128]{3,2,1,0:T(8,128)S(1)}, u32[]{:S(2)}, u32[]{:S(2)}) collective-permute-start(f32[2,4,32,128]{3,2,1,0:T(8,128)S(1)} %add.23), channel_id=1, source_target_pairs={{0,16},{8,24},{16,0},{24,8},{1,17},{9,25},{17,1},{25,9},{2,18},{10... | collective-permute-start | bytes 393224 | tf_op jit(solution)/shard_map/ppermute | solution.py:608
  57.4 0.4 collective-permute-start.8
  57.8 6.0 %collective-permute-done.7 = f32[2,4,32,128]{3,2,1,0:T(8,128)S(1)} collective-permute-done((f32[2,4,32,128]{3,2,1,0:T(8,128)S(1)}, f32[2,4,32,128]{3,2,1,0:T(8,128)S(1)}, u32[]{:S(2)}, u32[]{:S(2)}) %collective-permute-start.7) | collective-permute-done | bytes 131104 | tf_op jit(solution)/shard_map/ppermute | solution.py:608
  63.8 2.0 %collective-permute-done.8 = f32[12,32,128]{2,1,0:T(8,128)S(1)} collective-permute-done((f32[12,32,128]{2,1,0:T(8,128)S(1)}, f32[12,32,128]{2,1,0:T(8,128)S(1)}, u32[]{:S(2)}, u32[]{:S(2)}) %collective-permute-start.8) | collective-permute-done | bytes 196640 | tf_op jit(solution)/shard_map/ppermute | solution.py:611
  65.8 0.8 %pad_maximum_fusion = f32[32,32,128]{2,1,0:T(8,128)} fusion(f32[4,32,128]{2,1,0:T(8,128)S(1)} %get-tuple-element.59, f32[12,32,128]{2,1,0:T(8,128)S(1)} %get-tuple-element.57, f32[12,32,128]{2,1,0:T(8,128)S(1)} %get-tuple-element.56, f32[4,32,128]{2,1,0:T(8,128)S(1)} %get-tuple-element.58), kind=kLoop, calls=%fused_computation | loop fusion | flops 393216 | bytes 1048576 | tf_op jit(solution)/shard_map/concatenate | solution.py:615
  (8 shorter events, 0.2 us)
Async XLA Ops:
  4.2 2.7 %collective-permute-start = (f32[13,32,4,128]{3,2,1,0:T(4,128)}, f32[13,32,4,128]{3,2,1,0:T(4,128)S(1)}, u32[]{:S(2)}, u32[]{:S(2)}) collective-permute-start(f32[13,32,4,128]{3,2,1,0:T(4,128)} %get-tuple-element.30), channel_id=1, source_target_pairs={{0,1},{1,0},{2,3},{3,2},{4,5},{5,4},{6,7},{7,6},{8,9},{9,8},{10,11... | collective-permute-start | bytes 2555912 | tf_op jit(solution)/shard_map/ppermute | solution.py:572
  4.2 27.6 %collective-permute-start.2 = (f32[43,32,128]{2,1,0:T(8,128)}, f32[43,32,128]{2,1,0:T(8,128)S(1)}, u32[]{:S(2)}, u32[]{:S(2)}) collective-permute-start(f32[43,32,128]{2,1,0:T(8,128)} %get-tuple-element.37), channel_id=1, source_target_pairs={{0,2},{2,0},{4,6},{6,4},{1,3},{3,1},{5,7},{7,5},{8,10},{10,8},{12,... | collective-permute-start | bytes 2113544 | tf_op jit(solution)/shard_map/ppermute | solution.py:588
  6.8 4.0 %copy-start.2 = (f32[13,32,4,128]{3,2,1,0:T(4,128)}, f32[13,32,4,128]{3,2,1,0:T(4,128)S(1)}, u32[]{:S(2)}) copy-start(f32[13,32,4,128]{3,2,1,0:T(4,128)S(1)} %collective-permute-done.border) | copy-start | bytes 2555908
  6.8 31.7 %collective-permute-start.3 = (f32[43,32,128]{2,1,0:T(8,128)}, f32[43,32,128]{2,1,0:T(8,128)S(1)}, u32[]{:S(2)}, u32[]{:S(2)}) collective-permute-start(f32[43,32,128]{2,1,0:T(8,128)} %get-tuple-element.38), channel_id=1, source_target_pairs={{2,4},{4,2},{3,5},{5,3},{10,12},{12,10},{11,13},{13,11},{18,20},{2... | collective-permute-start | bytes 2113544 | tf_op jit(solution)/shard_map/ppermute | solution.py:591
  31.3 7.2 %collective-permute-start.1 = (f32[12,32,128]{2,1,0:T(8,128)}, f32[12,32,128]{2,1,0:T(8,128)S(1)}, u32[]{:S(2)}, u32[]{:S(2)}) collective-permute-start(f32[12,32,128]{2,1,0:T(8,128)} %get-tuple-element.36), channel_id=1, source_target_pairs={{0,8},{8,0},{16,24},{24,16},{1,9},{9,1},{17,25},{25,17},{2,10},{10... | collective-permute-start | bytes 589832 | tf_op jit(solution)/shard_map/ppermute | solution.py:593
  31.8 8.7 %copy-start = (f32[43,32,128]{2,1,0:T(8,128)}, f32[43,32,128]{2,1,0:T(8,128)S(1)}, u32[]{:S(2)}) copy-start(f32[43,32,128]{2,1,0:T(8,128)S(1)} %collective-permute-done.2.near) | copy-start | bytes 2113540
  38.5 2.0 %copy-start.1 = (f32[43,32,128]{2,1,0:T(8,128)}, f32[43,32,128]{2,1,0:T(8,128)S(1)}, u32[]{:S(2)}) copy-start(f32[43,32,128]{2,1,0:T(8,128)S(1)} %collective-permute-done.3.far) | copy-start | bytes 2113540
  38.6 1.5 %collective-permute-start.4 = (f32[2,43,4,128]{3,2,1,0:T(4,128)S(1)}, f32[2,43,4,128]{3,2,1,0:T(4,128)S(1)}, u32[]{:S(2)}, u32[]{:S(2)}) collective-permute-start(f32[2,43,4,128]{3,2,1,0:T(4,128)S(1)} %pad_maximum_fusion.1), channel_id=1, source_target_pairs={{0,1},{1,0},{2,3},{3,2},{4,5},{5,4},{6,7},{7,6},{8,9},{9,8},{10,11... | collective-permute-start | bytes 528392 | tf_op jit(solution)/shard_map/ppermute | solution.py:572
  40.1 0.7 %copy-start.3 = (f32[2,43,4,128]{3,2,1,0:T(4,128)}, f32[2,43,4,128]{3,2,1,0:T(4,128)S(1)}, u32[]{:S(2)}) copy-start(f32[2,43,4,128]{3,2,1,0:T(4,128)S(1)} %collective-permute-done.4.corner) | copy-start | bytes 528388
  40.1 12.0 %collective-permute-start.5 = (f32[12,32,128]{2,1,0:T(8,128)S(1)}, f32[12,32,128]{2,1,0:T(8,128)S(1)}, u32[]{:S(2)}, u32[]{:S(2)}) collective-permute-start(f32[12,32,128]{2,1,0:T(8,128)S(1)} %add.21), channel_id=1, source_target_pairs={{0,16},{8,24},{16,0},{24,8},{1,17},{9,25},{17,1},{25,9},{2,18},{10... | collective-permute-start | bytes 589832 | tf_op jit(solution)/shard_map/ppermute | solution.py:603
  49.2 6.0 %collective-permute-start.6 = (f32[2,4,32,128]{3,2,1,0:T(8,128)}, f32[2,4,32,128]{3,2,1,0:T(8,128)S(1)}, u32[]{:S(2)}, u32[]{:S(2)}) collective-permute-start(f32[2,4,32,128]{3,2,1,0:T(8,128)} %get-tuple-element.52), channel_id=1, source_target_pairs={{0,8},{8,0},{16,24},{24,16},{1,9},{9,1},{17,25},{25,17},{2,10},{10... | collective-permute-start | bytes 393224 | tf_op jit(solution)/shard_map/ppermute | solution.py:608
  55.2 8.6 %collective-permute-start.7 = (f32[2,4,32,128]{3,2,1,0:T(8,128)S(1)}, f32[2,4,32,128]{3,2,1,0:T(8,128)S(1)}, u32[]{:S(2)}, u32[]{:S(2)}) collective-permute-start(f32[2,4,32,128]{3,2,1,0:T(8,128)S(1)} %add.23), channel_id=1, source_target_pairs={{0,16},{8,24},{16,0},{24,8},{1,17},{9,25},{17,1},{25,9},{2,18},{10... | collective-permute-start | bytes 393224 | tf_op jit(solution)/shard_map/ppermute | solution.py:608
  57.4 8.4 %collective-permute-start.8 = (f32[12,32,128]{2,1,0:T(8,128)S(1)}, f32[12,32,128]{2,1,0:T(8,128)S(1)}, u32[]{:S(2)}, u32[]{:S(2)}) collective-permute-start(f32[12,32,128]{2,1,0:T(8,128)S(1)} %add.22), channel_id=1, source_target_pairs={{0,8},{8,0},{16,24},{24,16},{1,9},{9,1},{17,25},{25,17},{2,10},{10... | collective-permute-start | bytes 589832 | tf_op jit(solution)/shard_map/ppermute | solution.py:611

commit v5 on v4

--- a/solution.py
+++ b/solution.py
@@ -319,17 +319,26 @@
     width_x, width_y = wave.shape[2], wave.shape[3]
     layout = Rows(width_y, second)
     rows = layout.total
+    parts = []
+    for begin, end in ((0, ITERS // 2), (ITERS // 2, ITERS)):
+        more = (begin + 1 if begin else 0, end + 1)
+        parts.append(
+            [
+                (edge_a.at[pl.ds(begin, end - begin)], fa.at[pl.ds(ITERS + begin, end - begin)]),
+                (edge_b.at[pl.ds(more[0], more[1] - more[0])], fb.at[pl.ds(ITERS + more[0], more[1] - more[0])]),
+                (edge_c.at[:, pl.ds(begin, end - begin)], coef.at[:, pl.ds(ITERS + begin, end - begin)]),
+            ]
+        )
     loads = copies(
         [
             (near, sides.at[1 - odd]),
             (far, sides.at[odd]),
             (corner.at[0], corners.at[1 - odd]),
             (corner.at[1], corners.at[odd]),
-            (edge_a, fa.at[pl.ds(ITERS, ITERS)]),
-            (edge_b, fb.at[pl.ds(ITERS, ITERS + 1)]),
             (edge_corr, corr),
-            (edge_c, coef.at[:, pl.ds(ITERS, ITERS)]),
-        ],
+        ]
+        + parts[0]
+        + parts[1],
         sems,
     )
     clear_ends([ref.at[pl.ds(0, ITERS)] for ref in (fa, fb)], rows)
@@ -358,7 +367,7 @@
         return 0
 
     lax.fori_loop(0, ITERS, fill, 0)
-    for copy in loads[4:]:
+    for copy in loads[4:8]:
         copy.wait()
 
     corr[0, 0] = jnp.zeros(corr.shape[2:], F32)
@@ -376,6 +385,11 @@
         return done
 
     def advance(turn, _):
+        @pl.when(turn == 1)
+        def _():
+            for copy in loads[8:]:
+                copy.wait()
+
         for step, (old, new) in enumerate(((fa, fb), (fb, fa))):
             start = 1 + step + 2 * turn
             sweep(old, new, slopes, sums, coef, (start, start + ITERS), layout, 0, finished(flat_view(new)))
@@ -451,7 +465,7 @@
             out[begin : begin + less] = planes_int[k, n].astype(F32)
 
     def needed(ref, *spot):
-        return jnp.where(second == 1, ref[spot + (slice(0, REACH),)], ref[spot + (slice(TILE - REACH, TILE),)])
+        return ref[spot + (pl.ds(REACH * (1 - second), REACH), slice(None))]
 
     def rows(x, _):
         for kind in range(2):
@@ -520,7 +534,7 @@
             vmem((3, width_x, width_y, LANES)),
             pltpu.VMEM((2, width_x, width_y, LANES), jnp.int32),
             vmem(border.shape),
-            vmem((2, FACTORS + 1, rows, LANES)),
+            vmem((2, FACTORS + 1, rows + TILE, LANES)),
             pltpu.SemaphoreType.DMA((CHUNKS, 15)),
             pltpu.SemaphoreType.DMA((16,)),
             pltpu.SemaphoreType.DMA((width_x,)),
@@ -548,10 +562,10 @@
             vmem(edge_corr.shape),
             vmem((2,) + near.shape),
             vmem(corner.shape),
-            vmem((2, FACTORS + 1, rows, LANES)),
+            vmem((2, FACTORS + 1, rows + TILE, LANES)),
             vmem((2, 4, ITERS, width_y, LANES)),
             vmem(edge_corr.shape),
-            pltpu.SemaphoreType.DMA((8,)),
+            pltpu.SemaphoreType.DMA((11,)),
         ],
         input_output_aliases={8: 0},
         compiler_params=pltpu.CompilerParams(vmem_limit_bytes=60 * MIB),

time: 68 us -> 67.3 us (0.990)
  Pallas kernels: 32.5 us -> 31.8 us
    ppermute x1, waiting for transfers between devices: 2.37 us -> 3.11 us  [local(): held = held + lax.ppermute(held, 'shot', pairs_at(distance))]
    pallas_call x1, Pallas kernels: 8.48 us -> 7.78 us  [advance_border(): pl.pallas_call(border_kernel, in_specs=[pl.BlockSpec(memory_space=pltpu.S...]
where the time goes in v5:
time: 67.3 us; the launch traced here: 66 us
  Pallas kernels  31.8 us (47%)
  waiting for transfers between devices  20.9 us (31%)
  starting transfers between devices  8.65 us (13%)
  other arithmetic  2.93 us (4%)
  between operations  1.39 us (2%)
    pallas_call x1, Pallas kernels, advance_inner(): pl.pallas_call(inner_kernel, in_specs=[pl.BlockSpec(memory_space=pltpu.SM...  20.5 us
    ppermute x2, waiting for transfers between devices, local(): own = outside = own + lax.ppermute(outside, 'shot', pairs_at(distance))  7.82 us
    pallas_call x1, Pallas kernels, advance_border(): pl.pallas_call(border_kernel, in_specs=[pl.BlockSpec(memory_space=pltpu.S...  7.78 us
    ppermute x1, waiting for transfers between devices, local(): received = lax.ppermute(sent, 'shot', pairs_at(1))  6.65 us
    pallas_call x1, Pallas kernels, pack(): pl.pallas_call(pack_kernel, in_specs=any_specs(7), out_specs=[pl.BlockSpe...  3.52 us
    ppermute x1, starting transfers between devices, local(): lax.ppermute(far, 'gx', [(i, j) for i in range(1, columns - 1) for j in [...  3.34 us
    ppermute x1, waiting for transfers between devices, local(): held = held + lax.ppermute(held, 'shot', pairs_at(distance))  3.11 us
    ppermute x2, starting transfers between devices, local(): own = outside = own + lax.ppermute(outside, 'shot', pairs_at(distance))  2.24 us
  transfers between devices with their start and end apart: 9, of which 7 were waited for; matrix products, arithmetic and copies ran while one was open for 3% of the time, Pallas kernels for 43%

profile of v5, /device:TPU:28, one launch (start us, length us, event | category | flops | bytes accessed | tf_op | source)
XLA Modules:
  0.0 66.0 jit_solution(10660894499017824712)
XLA Ops:
  0.6 3.5 %pack_borders.1 = (f32[43,32,128]{2,1,0:T(8,128)}, f32[43,32,128]{2,1,0:T(8,128)}, f32[13,32,4,128]{3,2,1,0:T(4,128)}) custom-call(f32[1,4,32,32,128]{4,3,2,1,0:T(8,128)} %now.3, f32[1,4,32,32,128]{4,3,2,1,0:T(8,128)} %prev.3, f32[32,32,128]{2,1,0:T(8,128)} %vel.3, f32[32,32,128]{2,1,0:T(8,128)} %eps.3, f32[32,32,128]{2,1,0:T(8,128)} %delta.3, ...), custom_call_target="tpu_custom_call" | custom-call | flops 1000000 | bytes 8000000 | tf_op jit(solution)/shard_map/pack_borders/pallas_call | solution.py:489
  4.2 0.1 collective-permute-start
  4.2 1.6 %collective-permute-start.2 = (f32[43,32,128]{2,1,0:T(8,128)}, f32[43,32,128]{2,1,0:T(8,128)S(1)}, u32[]{:S(2)}, u32[]{:S(2)}) collective-permute-start(f32[43,32,128]{2,1,0:T(8,128)} %get-tuple-element.37), channel_id=1, source_target_pairs={{0,2},{2,0},{4,6},{6,4},{1,3},{3,1},{5,7},{7,5},{8,10},{10,8},{12,... | collective-permute-start | bytes 2113544 | tf_op jit(solution)/shard_map/ppermute | solution.py:602
  5.8 1.0 %collective-permute-done.border = f32[13,32,4,128]{3,2,1,0:T(4,128)S(1)} collective-permute-done((f32[13,32,4,128]{3,2,1,0:T(4,128)}, f32[13,32,4,128]{3,2,1,0:T(4,128)S(1)}, u32[]{:S(2)}, u32[]{:S(2)}) %collective-permute-start) | collective-permute-done | bytes 852000 | tf_op jit(solution)/shard_map/ppermute | solution.py:586
  6.8 0.0 copy-start.2
  6.8 3.3 %collective-permute-start.3 = (f32[43,32,128]{2,1,0:T(8,128)}, f32[43,32,128]{2,1,0:T(8,128)S(1)}, u32[]{:S(2)}, u32[]{:S(2)}) collective-permute-start(f32[43,32,128]{2,1,0:T(8,128)} %get-tuple-element.38), channel_id=1, source_target_pairs={{2,4},{4,2},{3,5},{5,3},{10,12},{12,10},{11,13},{13,11},{18,20},{2... | collective-permute-start | bytes 2113544 | tf_op jit(solution)/shard_map/ppermute | solution.py:605
  10.8 0.0 copy-done.2
  10.8 20.5 %inner_steps.1 = (f32[1,4,32,32,128]{4,3,2,1,0:T(8,128)}, f32[4,38,8,128]{3,2,1,0:T(8,128)}, f32[5,38,8,128]{3,2,1,0:T(8,128)}, f32[7,4,38,8,128]{4,3,2,1,0:T(8,...) custom-call(s32[1,1,1]{2,1,0:T(1,128)S(6)} %copy.12.cover, ...), custom_call_target="tpu_custom_call" | custom-call | flops 80000000 | bytes 200000000 | tf_op jit(solution)/shard_map/inner_steps/pallas_call | solution.py:515
  31.3 0.5 collective-permute-start.1
  31.8 0.0 collective-permute-done.2.near
  31.8 0.0 copy-start
  31.8 6.6 %collective-permute-done.1 = f32[12,32,128]{2,1,0:T(8,128)S(1)} collective-permute-done((f32[12,32,128]{2,1,0:T(8,128)}, f32[12,32,128]{2,1,0:T(8,128)S(1)}, u32[]{:S(2)}, u32[]{:S(2)}) %collective-permute-start.1) | collective-permute-done | bytes 196640 | tf_op jit(solution)/shard_map/ppermute | solution.py:607
  38.5 0.0 collective-permute-done.3.far
  38.5 0.0 copy-start.1
  38.5 0.1 dynamic-slice_bitcast_fusion
  38.6 0.1 collective-permute-start.4
  38.7 1.0 %broadcast_multiply_fusion = f32[12,32,128]{2,1,0:T(8,128)S(1)} fusion(f32[12,32,128]{2,1,0:T(8,128)} %get-tuple-element.35), kind=kLoop, calls=%fused_computation.2 | loop fusion | flops 49152 | bytes 393216 | tf_op jit(solution)/shard_map/mul | solution.py:594
  39.7 0.4 collective-permute-done.4.corner
  40.1 0.4 collective-permute-start.5
  40.5 0.0 copy-done
  40.5 0.0 copy-done.1
  40.5 0.2 copy-done.3
  40.7 7.8 %border_steps.1 = (f32[1,4,32,32,128]{4,3,2,1,0:T(8,128)}, f32[2,4,32,128]{3,2,1,0:T(8,128)}, f32[2,4,32,128]{3,2,1,0:T(8,128)}) custom-call(s32[1,1,1]{2,1,0:T(1,128)S(6)} %copy.12.cover, f32[4,38,8,128]{3,2,1,0:T(8,128)} %get-tuple-element.32.edge_a, f32[5,38,8,128]{3,2,1,0:T(8,128)} %get-tuple-element.33.edge_b, ...), custom_call_target="tpu_custom_call", output_to_operand_aliasing={{0}: (8, {})} | custom-call | flops 20000000 | bytes 20000000 | tf_op jit(solution)/shard_map/border_steps/pallas_call | solution.py:554
  48.5 0.5 collective-permute-start.6
  49.0 3.1 %collective-permute-done.5 = f32[12,32,128]{2,1,0:T(8,128)S(1)} collective-permute-done((f32[12,32,128]{2,1,0:T(8,128)S(1)}, f32[12,32,128]{2,1,0:T(8,128)S(1)}, u32[]{:S(2)}, u32[]{:S(2)}) %collective-permute-start.5) | collective-permute-done | bytes 196640 | tf_op jit(solution)/shard_map/ppermute | solution.py:617
  52.2 0.9 %broadcast_multiply_fusion.1 = f32[2,4,32,128]{3,2,1,0:T(8,128)S(1)} fusion(f32[2,4,32,128]{3,2,1,0:T(8,128)} %get-tuple-element.51), kind=kLoop, calls=%fused_computation.9 | loop fusion | flops 32768 | bytes 262144 | tf_op jit(solution)/shard_map/mul | solution.py:594
  53.1 1.8 %collective-permute-done.6 = f32[2,4,32,128]{3,2,1,0:T(8,128)S(1)} collective-permute-done((f32[2,4,32,128]{3,2,1,0:T(8,128)}, f32[2,4,32,128]{3,2,1,0:T(8,128)S(1)}, u32[]{:S(2)}, u32[]{:S(2)}) %collective-permute-start.6) | collective-permute-done | bytes 131104 | tf_op jit(solution)/shard_map/ppermute | solution.py:622
  54.9 1.7 %collective-permute-start.7 = (f32[2,4,32,128]{3,2,1,0:T(8,128)S(1)}, f32[2,4,32,128]{3,2,1,0:T(8,128)S(1)}, u32[]{:S(2)}, u32[]{:S(2)}) collective-permute-start(f32[2,4,32,128]{3,2,1,0:T(8,128)S(1)} %add.23), channel_id=1, source_target_pairs={{0,16},{8,24},{16,0},{24,8},{1,17},{9,25},{17,1},{25,9},{2,18},{10... | collective-permute-start | bytes 393224 | tf_op jit(solution)/shard_map/ppermute | solution.py:622
  56.7 0.4 collective-permute-start.8
  57.1 6.0 %collective-permute-done.7 = f32[2,4,32,128]{3,2,1,0:T(8,128)S(1)} collective-permute-done((f32[2,4,32,128]{3,2,1,0:T(8,128)S(1)}, f32[2,4,32,128]{3,2,1,0:T(8,128)S(1)}, u32[]{:S(2)}, u32[]{:S(2)}) %collective-permute-start.7) | collective-permute-done | bytes 131104 | tf_op jit(solution)/shard_map/ppermute | solution.py:622
  63.2 2.0 %collective-permute-done.8 = f32[12,32,128]{2,1,0:T(8,128)S(1)} collective-permute-done((f32[12,32,128]{2,1,0:T(8,128)S(1)}, f32[12,32,128]{2,1,0:T(8,128)S(1)}, u32[]{:S(2)}, u32[]{:S(2)}) %collective-permute-start.8) | collective-permute-done | bytes 196640 | tf_op jit(solution)/shard_map/ppermute | solution.py:625
  65.2 0.8 %pad_maximum_fusion = f32[32,32,128]{2,1,0:T(8,128)} fusion(f32[4,32,128]{2,1,0:T(8,128)S(1)} %get-tuple-element.59, f32[12,32,128]{2,1,0:T(8,128)S(1)} %get-tuple-element.57, f32[12,32,128]{2,1,0:T(8,128)S(1)} %get-tuple-element.56, f32[4,32,128]{2,1,0:T(8,128)S(1)} %get-tuple-element.58), kind=kLoop, calls=%fused_computation | loop fusion | flops 393216 | bytes 1048576 | tf_op jit(solution)/shard_map/concatenate | solution.py:629
  (8 shorter events, 0.2 us)
Async XLA Ops:
  4.2 2.7 %collective-permute-start = (f32[13,32,4,128]{3,2,1,0:T(4,128)}, f32[13,32,4,128]{3,2,1,0:T(4,128)S(1)}, u32[]{:S(2)}, u32[]{:S(2)}) collective-permute-start(f32[13,32,4,128]{3,2,1,0:T(4,128)} %get-tuple-element.30), channel_id=1, source_target_pairs={{0,1},{1,0},{2,3},{3,2},{4,5},{5,4},{6,7},{7,6},{8,9},{9,8},{10,11... | collective-permute-start | bytes 2555912 | tf_op jit(solution)/shard_map/ppermute | solution.py:586
  4.2 27.6 %collective-permute-start.2 = (f32[43,32,128]{2,1,0:T(8,128)}, f32[43,32,128]{2,1,0:T(8,128)S(1)}, u32[]{:S(2)}, u32[]{:S(2)}) collective-permute-start(f32[43,32,128]{2,1,0:T(8,128)} %get-tuple-element.37), channel_id=1, source_target_pairs={{0,2},{2,0},{4,6},{6,4},{1,3},{3,1},{5,7},{7,5},{8,10},{10,8},{12,... | collective-permute-start | bytes 2113544 | tf_op jit(solution)/shard_map/ppermute | solution.py:602
  6.8 4.0 %copy-start.2 = (f32[13,32,4,128]{3,2,1,0:T(4,128)}, f32[13,32,4,128]{3,2,1,0:T(4,128)S(1)}, u32[]{:S(2)}) copy-start(f32[13,32,4,128]{3,2,1,0:T(4,128)S(1)} %collective-permute-done.border) | copy-start | bytes 2555908
  6.8 31.7 %collective-permute-start.3 = (f32[43,32,128]{2,1,0:T(8,128)}, f32[43,32,128]{2,1,0:T(8,128)S(1)}, u32[]{:S(2)}, u32[]{:S(2)}) collective-permute-start(f32[43,32,128]{2,1,0:T(8,128)} %get-tuple-element.38), channel_id=1, source_target_pairs={{2,4},{4,2},{3,5},{5,3},{10,12},{12,10},{11,13},{13,11},{18,20},{2... | collective-permute-start | bytes 2113544 | tf_op jit(solution)/shard_map/ppermute | solution.py:605
  31.3 7.2 %collective-permute-start.1 = (f32[12,32,128]{2,1,0:T(8,128)}, f32[12,32,128]{2,1,0:T(8,128)S(1)}, u32[]{:S(2)}, u32[]{:S(2)}) collective-permute-start(f32[12,32,128]{2,1,0:T(8,128)} %get-tuple-element.36), channel_id=1, source_target_pairs={{0,8},{8,0},{16,24},{24,16},{1,9},{9,1},{17,25},{25,17},{2,10},{10... | collective-permute-start | bytes 589832 | tf_op jit(solution)/shard_map/ppermute | solution.py:607
  31.8 8.7 %copy-start = (f32[43,32,128]{2,1,0:T(8,128)}, f32[43,32,128]{2,1,0:T(8,128)S(1)}, u32[]{:S(2)}) copy-start(f32[43,32,128]{2,1,0:T(8,128)S(1)} %collective-permute-done.2.near) | copy-start | bytes 2113540
  38.5 2.0 %copy-start.1 = (f32[43,32,128]{2,1,0:T(8,128)}, f32[43,32,128]{2,1,0:T(8,128)S(1)}, u32[]{:S(2)}) copy-start(f32[43,32,128]{2,1,0:T(8,128)S(1)} %collective-permute-done.3.far) | copy-start | bytes 2113540
  38.6 1.5 %collective-permute-start.4 = (f32[2,43,4,128]{3,2,1,0:T(4,128)S(1)}, f32[2,43,4,128]{3,2,1,0:T(4,128)S(1)}, u32[]{:S(2)}, u32[]{:S(2)}) collective-permute-start(f32[2,43,4,128]{3,2,1,0:T(4,128)S(1)} %pad_maximum_fusion.1), channel_id=1, source_target_pairs={{0,1},{1,0},{2,3},{3,2},{4,5},{5,4},{6,7},{7,6},{8,9},{9,8},{10,11... | collective-permute-start | bytes 528392 | tf_op jit(solution)/shard_map/ppermute | solution.py:586
  40.1 0.7 %copy-start.3 = (f32[2,43,4,128]{3,2,1,0:T(4,128)}, f32[2,43,4,128]{3,2,1,0:T(4,128)S(1)}, u32[]{:S(2)}) copy-start(f32[2,43,4,128]{3,2,1,0:T(4,128)S(1)} %collective-permute-done.4.corner) | copy-start | bytes 528388
  40.1 12.1 %collective-permute-start.5 = (f32[12,32,128]{2,1,0:T(8,128)S(1)}, f32[12,32,128]{2,1,0:T(8,128)S(1)}, u32[]{:S(2)}, u32[]{:S(2)}) collective-permute-start(f32[12,32,128]{2,1,0:T(8,128)S(1)} %add.21), channel_id=1, source_target_pairs={{0,16},{8,24},{16,0},{24,8},{1,17},{9,25},{17,1},{25,9},{2,18},{10... | collective-permute-start | bytes 589832 | tf_op jit(solution)/shard_map/ppermute | solution.py:617
  48.5 6.4 %collective-permute-start.6 = (f32[2,4,32,128]{3,2,1,0:T(8,128)}, f32[2,4,32,128]{3,2,1,0:T(8,128)S(1)}, u32[]{:S(2)}, u32[]{:S(2)}) collective-permute-start(f32[2,4,32,128]{3,2,1,0:T(8,128)} %get-tuple-element.52), channel_id=1, source_target_pairs={{0,8},{8,0},{16,24},{24,16},{1,9},{9,1},{17,25},{25,17},{2,10},{10... | collective-permute-start | bytes 393224 | tf_op jit(solution)/shard_map/ppermute | solution.py:622
  54.9 8.2 %collective-permute-start.7 = (f32[2,4,32,128]{3,2,1,0:T(8,128)S(1)}, f32[2,4,32,128]{3,2,1,0:T(8,128)S(1)}, u32[]{:S(2)}, u32[]{:S(2)}) collective-permute-start(f32[2,4,32,128]{3,2,1,0:T(8,128)S(1)} %add.23), channel_id=1, source_target_pairs={{0,16},{8,24},{16,0},{24,8},{1,17},{9,25},{17,1},{25,9},{2,18},{10... | collective-permute-start | bytes 393224 | tf_op jit(solution)/shard_map/ppermute | solution.py:622
  56.7 8.5 %collective-permute-start.8 = (f32[12,32,128]{2,1,0:T(8,128)S(1)}, f32[12,32,128]{2,1,0:T(8,128)S(1)}, u32[]{:S(2)}, u32[]{:S(2)}) collective-permute-start(f32[12,32,128]{2,1,0:T(8,128)S(1)} %add.22), channel_id=1, source_target_pairs={{0,8},{8,0},{16,24},{24,16},{1,9},{9,1},{17,25},{25,17},{2,10},{10... | collective-permute-start | bytes 589832 | tf_op jit(solution)/shard_map/ppermute | solution.py:625

commit v6 on v5

--- a/solution.py
+++ b/solution.py
@@ -392,7 +392,7 @@
 
         for step, (old, new) in enumerate(((fa, fb), (fb, fa))):
             start = 1 + step + 2 * turn
-            sweep(old, new, slopes, sums, coef, (start, start + ITERS), layout, 0, finished(flat_view(new)))
+            sweep(old, new, slopes, sums, coef, (start, start + ITERS), layout, step, finished(flat_view(new)))
         return 0
 
     lax.fori_loop(0, ITERS // 2, advance, 0)
@@ -432,8 +432,8 @@
 
 def pack_kernel(
     now, prev, vel, eps, delta, tilt, azimuth,
-    near, far, border,
-    planes_int, wave_rows, float_rows, int_rows, sems,
+    near_out, far_out, border_out,
+    near, far, border, planes_int, wave_rows, float_rows, int_rows, sems,
 ):
     second, odd = lax.axis_index("gy"), lax.axis_index("gx") % 2
     width_x, width_y = vel.shape[0], vel.shape[1]
@@ -441,14 +441,11 @@
     n_now, n_prev = 4 * deep, 4 * less
     ints, floats = (tilt, azimuth), (vel, eps, delta)
     tile = pl.ds(pl.multiple_of((1 - second) * (width_y - TILE), TILE), TILE)
-    pairs = [(array.at[0, :, :, tile], wave_rows.at[n]) for n, array in enumerate((now, prev))]
-    pairs += [(array.at[:, tile], float_rows.at[n]) for n, array in enumerate(floats)]
-    pairs += [(array.at[:, tile], int_rows.at[n]) for n, array in enumerate(ints)]
+    pairs = []
     ends = ((near, 1 - odd), (far, odd))
     for k, (_, high) in enumerate(ends):
         at = pl.ds(high * (width_x - less), less)
         pairs += [(ints[n].at[at], planes_int.at[k, n]) for n in range(2)]
-    first = len(pairs)
     for out, high in ends:
         at = pl.ds(high * (width_x - less), less)
         for f in range(4):
@@ -456,13 +453,21 @@
             pairs.append((prev.at[0, f, at], out.at[pl.ds(n_now + f * less, less)]))
         for n in range(3):
             pairs.append((floats[n].at[at], out.at[pl.ds(n_now + n_prev + n * less, less)]))
+    planes = len(pairs)
+    pairs += [(array.at[0, :, :, tile], wave_rows.at[n]) for n, array in enumerate((now, prev))]
+    pairs += [(array.at[:, tile], float_rows.at[n]) for n, array in enumerate(floats)]
+    pairs += [(array.at[:, tile], int_rows.at[n]) for n, array in enumerate(ints)]
     started = copies(pairs, sems)
-    for copy in started[:first]:
+    for copy in started[:planes]:
         copy.wait()
     for k, (out, _) in enumerate(ends):
         for n in range(2):
             begin = n_now + n_prev + (3 + n) * less
             out[begin : begin + less] = planes_int[k, n].astype(F32)
+
+    given = copies([(near, near_out), (far, far_out)], sems, len(pairs))
+    for copy in started[planes:]:
+        copy.wait()
 
     def needed(ref, *spot):
         return ref[spot + (pl.ds(REACH * (1 - second), REACH), slice(None))]
@@ -478,7 +483,7 @@
         return 0
 
     lax.fori_loop(0, width_x // 4, lambda x, _: [rows(4 * x + i, 0) for i in range(4)][0], 0)
-    for copy in started[first:]:
+    for copy in given + copies([(border, border_out)], sems, len(pairs) + 2):
         copy.wait()
 
 
@@ -489,14 +494,17 @@
     return pl.pallas_call(
         pack_kernel,
         in_specs=any_specs(7),
-        out_specs=[pl.BlockSpec(memory_space=pltpu.VMEM)] * 3,
+        out_specs=any_specs(3),
         out_shape=(face, face, jax.ShapeDtypeStruct((13, width_x, REACH, LANES), F32)),
         scratch_shapes=[
+            pltpu.VMEM(face.shape, F32),
+            pltpu.VMEM(face.shape, F32),
+            pltpu.VMEM((13, width_x, REACH, LANES), F32),
             pltpu.VMEM((2, 2, ITERS - 1, width_y, LANES), jnp.int32),
             pltpu.VMEM((2, 4, width_x, TILE, LANES), F32),
             pltpu.VMEM((3, width_x, TILE, LANES), F32),
             pltpu.VMEM((2, width_x, TILE, LANES), jnp.int32),
-            pltpu.SemaphoreType.DMA((33,)),
+            pltpu.SemaphoreType.DMA((36,)),
         ],
         compiler_params=pltpu.CompilerParams(vmem_limit_bytes=60 * MIB),
         cost_estimate=pl.CostEstimate(flops=1_000_000, bytes_accessed=8_000_000, transcendentals=0),

time: 67.3 us -> 67 us (level)
  no operation moved by 1% of the time
where the time goes in v6:
time: 67 us; the launch traced here: 65.7 us
  Pallas kernels  31.6 us (47%)
  waiting for transfers between devices  20.9 us (31%)
  starting transfers between devices  8.53 us (13%)
  other arithmetic  2.93 us (4%)
  between operations  1.39 us (2%)
    pallas_call x1, Pallas kernels, advance_inner(): pl.pallas_call(inner_kernel, in_specs=[pl.BlockSpec(memory_space=pltpu.SM...  20.5 us
    ppermute x2, waiting for transfers between devices, local(): own = outside = own + lax.ppermute(outside, 'shot', pairs_at(distance))  7.99 us
    pallas_call x1, Pallas kernels, advance_border(): pl.pallas_call(border_kernel, in_specs=[pl.BlockSpec(memory_space=pltpu.S...  7.75 us
    ppermute x1, waiting for transfers between devices, local(): received = lax.ppermute(sent, 'shot', pairs_at(1))  6.65 us
    pallas_call x1, Pallas kernels, pack(): pl.pallas_call(pack_kernel, in_specs=any_specs(7), out_specs=any_specs(3)...  3.38 us
    ppermute x1, starting transfers between devices, local(): lax.ppermute(far, 'gx', [(i, j) for i in range(1, columns - 1) for j in [...  3.33 us
    ppermute x1, waiting for transfers between devices, local(): held = held + lax.ppermute(held, 'shot', pairs_at(distance))  3.16 us
    ppermute x2, starting transfers between devices, local(): own = outside = own + lax.ppermute(outside, 'shot', pairs_at(distance))  2.14 us
  transfers between devices with their start and end apart: 9, of which 7 were waited for; matrix products, arithmetic and copies ran while one was open for 3% of the time, Pallas kernels for 43%

profile of v6, /device:TPU:28, one launch (start us, length us, event | category | flops | bytes accessed | tf_op | source)
XLA Modules:
  0.0 65.7 jit_solution(15854786654625988018)
XLA Ops:
  0.6 3.4 %pack_borders.1 = (f32[43,32,128]{2,1,0:T(8,128)}, f32[43,32,128]{2,1,0:T(8,128)}, f32[13,32,4,128]{3,2,1,0:T(4,128)}) custom-call(f32[1,4,32,32,128]{4,3,2,1,0:T(8,128)} %now.3, f32[1,4,32,32,128]{4,3,2,1,0:T(8,128)} %prev.3, f32[32,32,128]{2,1,0:T(8,128)} %vel.3, f32[32,32,128]{2,1,0:T(8,128)} %eps.3, f32[32,32,128]{2,1,0:T(8,128)} %delta.3, ...), custom_call_target="tpu_custom_call" | custom-call | flops 1000000 | bytes 8000000 | tf_op jit(solution)/shard_map/pack_borders/pallas_call | solution.py:494
  4.0 0.1 collective-permute-start
  4.1 1.6 %collective-permute-start.2 = (f32[43,32,128]{2,1,0:T(8,128)}, f32[43,32,128]{2,1,0:T(8,128)S(1)}, u32[]{:S(2)}, u32[]{:S(2)}) collective-permute-start(f32[43,32,128]{2,1,0:T(8,128)} %get-tuple-element.37), channel_id=1, source_target_pairs={{0,2},{2,0},{4,6},{6,4},{1,3},{3,1},{5,7},{7,5},{8,10},{10,8},{12,... | collective-permute-start | bytes 2113544 | tf_op jit(solution)/shard_map/ppermute | solution.py:610
  5.7 1.0 %collective-permute-done.border = f32[13,32,4,128]{3,2,1,0:T(4,128)S(1)} collective-permute-done((f32[13,32,4,128]{3,2,1,0:T(4,128)}, f32[13,32,4,128]{3,2,1,0:T(4,128)S(1)}, u32[]{:S(2)}, u32[]{:S(2)}) %collective-permute-start) | collective-permute-done | bytes 852000 | tf_op jit(solution)/shard_map/ppermute | solution.py:594
  6.7 0.0 copy-start.2
  6.7 3.3 %collective-permute-start.3 = (f32[43,32,128]{2,1,0:T(8,128)}, f32[43,32,128]{2,1,0:T(8,128)S(1)}, u32[]{:S(2)}, u32[]{:S(2)}) collective-permute-start(f32[43,32,128]{2,1,0:T(8,128)} %get-tuple-element.38), channel_id=1, source_target_pairs={{2,4},{4,2},{3,5},{5,3},{10,12},{12,10},{11,13},{13,11},{18,20},{2... | collective-permute-start | bytes 2113544 | tf_op jit(solution)/shard_map/ppermute | solution.py:613
  10.7 0.0 copy-done.2
  10.7 20.5 %inner_steps.1 = (f32[1,4,32,32,128]{4,3,2,1,0:T(8,128)}, f32[4,38,8,128]{3,2,1,0:T(8,128)}, f32[5,38,8,128]{3,2,1,0:T(8,128)}, f32[7,4,38,8,128]{4,3,2,1,0:T(8,...) custom-call(s32[1,1,1]{2,1,0:T(1,128)S(6)} %copy.12.cover, ...), custom_call_target="tpu_custom_call" | custom-call | flops 80000000 | bytes 200000000 | tf_op jit(solution)/shard_map/inner_steps/pallas_call | solution.py:523
  31.2 0.5 collective-permute-start.1
  31.7 0.0 collective-permute-done.2.near
  31.7 0.0 copy-start
  31.7 6.6 %collective-permute-done.1 = f32[12,32,128]{2,1,0:T(8,128)S(1)} collective-permute-done((f32[12,32,128]{2,1,0:T(8,128)}, f32[12,32,128]{2,1,0:T(8,128)S(1)}, u32[]{:S(2)}, u32[]{:S(2)}) %collective-permute-start.1) | collective-permute-done | bytes 196640 | tf_op jit(solution)/shard_map/ppermute | solution.py:615
  38.3 0.0 collective-permute-done.3.far
  38.3 0.0 copy-start.1
  38.3 0.1 dynamic-slice_bitcast_fusion
  38.4 0.1 collective-permute-start.4
  38.5 1.0 %broadcast_multiply_fusion = f32[12,32,128]{2,1,0:T(8,128)S(1)} fusion(f32[12,32,128]{2,1,0:T(8,128)} %get-tuple-element.35), kind=kLoop, calls=%fused_computation.2 | loop fusion | flops 49152 | bytes 393216 | tf_op jit(solution)/shard_map/mul | solution.py:602
  39.5 0.4 collective-permute-done.4.corner
  39.9 0.4 collective-permute-start.5
  40.3 0.0 copy-done
  40.3 0.0 copy-done.1
  40.3 0.2 copy-done.3
  40.6 7.7 %border_steps.1 = (f32[1,4,32,32,128]{4,3,2,1,0:T(8,128)}, f32[2,4,32,128]{3,2,1,0:T(8,128)}, f32[2,4,32,128]{3,2,1,0:T(8,128)}) custom-call(s32[1,1,1]{2,1,0:T(1,128)S(6)} %copy.12.cover, f32[4,38,8,128]{3,2,1,0:T(8,128)} %get-tuple-element.32.edge_a, f32[5,38,8,128]{3,2,1,0:T(8,128)} %get-tuple-element.33.edge_b, ...), custom_call_target="tpu_custom_call", output_to_operand_aliasing={{0}: (8, {})} | custom-call | flops 20000000 | bytes 20000000 | tf_op jit(solution)/shard_map/border_steps/pallas_call | solution.py:562
  48.3 0.5 collective-permute-start.6
  48.9 3.2 %collective-permute-done.5 = f32[12,32,128]{2,1,0:T(8,128)S(1)} collective-permute-done((f32[12,32,128]{2,1,0:T(8,128)S(1)}, f32[12,32,128]{2,1,0:T(8,128)S(1)}, u32[]{:S(2)}, u32[]{:S(2)}) %collective-permute-start.5) | collective-permute-done | bytes 196640 | tf_op jit(solution)/shard_map/ppermute | solution.py:625
  52.0 0.9 %broadcast_multiply_fusion.1 = f32[2,4,32,128]{3,2,1,0:T(8,128)S(1)} fusion(f32[2,4,32,128]{3,2,1,0:T(8,128)} %get-tuple-element.51), kind=kLoop, calls=%fused_computation.9 | loop fusion | flops 32768 | bytes 262144 | tf_op jit(solution)/shard_map/mul | solution.py:602
  53.0 1.8 %collective-permute-done.6 = f32[2,4,32,128]{3,2,1,0:T(8,128)S(1)} collective-permute-done((f32[2,4,32,128]{3,2,1,0:T(8,128)}, f32[2,4,32,128]{3,2,1,0:T(8,128)S(1)}, u32[]{:S(2)}, u32[]{:S(2)}) %collective-permute-start.6) | collective-permute-done | bytes 131104 | tf_op jit(solution)/shard_map/ppermute | solution.py:630
  54.8 1.6 %collective-permute-start.7 = (f32[2,4,32,128]{3,2,1,0:T(8,128)S(1)}, f32[2,4,32,128]{3,2,1,0:T(8,128)S(1)}, u32[]{:S(2)}, u32[]{:S(2)}) collective-permute-start(f32[2,4,32,128]{3,2,1,0:T(8,128)S(1)} %add.23), channel_id=1, source_target_pairs={{0,16},{8,24},{16,0},{24,8},{1,17},{9,25},{17,1},{25,9},{2,18},{10... | collective-permute-start | bytes 393224 | tf_op jit(solution)/shard_map/ppermute | solution.py:630
  56.4 0.4 collective-permute-start.8
  56.9 6.2 %collective-permute-done.7 = f32[2,4,32,128]{3,2,1,0:T(8,128)S(1)} collective-permute-done((f32[2,4,32,128]{3,2,1,0:T(8,128)S(1)}, f32[2,4,32,128]{3,2,1,0:T(8,128)S(1)}, u32[]{:S(2)}, u32[]{:S(2)}) %collective-permute-start.7) | collective-permute-done | bytes 131104 | tf_op jit(solution)/shard_map/ppermute | solution.py:630
  63.1 1.7 %collective-permute-done.8 = f32[12,32,128]{2,1,0:T(8,128)S(1)} collective-permute-done((f32[12,32,128]{2,1,0:T(8,128)S(1)}, f32[12,32,128]{2,1,0:T(8,128)S(1)}, u32[]{:S(2)}, u32[]{:S(2)}) %collective-permute-start.8) | collective-permute-done | bytes 196640 | tf_op jit(solution)/shard_map/ppermute | solution.py:633
  64.8 0.8 %pad_maximum_fusion = f32[32,32,128]{2,1,0:T(8,128)} fusion(f32[4,32,128]{2,1,0:T(8,128)S(1)} %get-tuple-element.59, f32[12,32,128]{2,1,0:T(8,128)S(1)} %get-tuple-element.57, f32[12,32,128]{2,1,0:T(8,128)S(1)} %get-tuple-element.56, f32[4,32,128]{2,1,0:T(8,128)S(1)} %get-tuple-element.58), kind=kLoop, calls=%fused_computation | loop fusion | flops 393216 | bytes 1048576 | tf_op jit(solution)/shard_map/concatenate | solution.py:637
  (8 shorter events, 0.2 us)
Async XLA Ops:
  4.0 2.7 %collective-permute-start = (f32[13,32,4,128]{3,2,1,0:T(4,128)}, f32[13,32,4,128]{3,2,1,0:T(4,128)S(1)}, u32[]{:S(2)}, u32[]{:S(2)}) collective-permute-start(f32[13,32,4,128]{3,2,1,0:T(4,128)} %get-tuple-element.30), channel_id=1, source_target_pairs={{0,1},{1,0},{2,3},{3,2},{4,5},{5,4},{6,7},{7,6},{8,9},{9,8},{10,11... | collective-permute-start | bytes 2555912 | tf_op jit(solution)/shard_map/ppermute | solution.py:594
  4.1 27.6 %collective-permute-start.2 = (f32[43,32,128]{2,1,0:T(8,128)}, f32[43,32,128]{2,1,0:T(8,128)S(1)}, u32[]{:S(2)}, u32[]{:S(2)}) collective-permute-start(f32[43,32,128]{2,1,0:T(8,128)} %get-tuple-element.37), channel_id=1, source_target_pairs={{0,2},{2,0},{4,6},{6,4},{1,3},{3,1},{5,7},{7,5},{8,10},{10,8},{12,... | collective-permute-start | bytes 2113544 | tf_op jit(solution)/shard_map/ppermute | solution.py:610
  6.7 4.0 %copy-start.2 = (f32[13,32,4,128]{3,2,1,0:T(4,128)}, f32[13,32,4,128]{3,2,1,0:T(4,128)S(1)}, u32[]{:S(2)}) copy-start(f32[13,32,4,128]{3,2,1,0:T(4,128)S(1)} %collective-permute-done.border) | copy-start | bytes 2555908
  6.7 31.6 %collective-permute-start.3 = (f32[43,32,128]{2,1,0:T(8,128)}, f32[43,32,128]{2,1,0:T(8,128)S(1)}, u32[]{:S(2)}, u32[]{:S(2)}) collective-permute-start(f32[43,32,128]{2,1,0:T(8,128)} %get-tuple-element.38), channel_id=1, source_target_pairs={{2,4},{4,2},{3,5},{5,3},{10,12},{12,10},{11,13},{13,11},{18,20},{2... | collective-permute-start | bytes 2113544 | tf_op jit(solution)/shard_map/ppermute | solution.py:613
  31.2 7.2 %collective-permute-start.1 = (f32[12,32,128]{2,1,0:T(8,128)}, f32[12,32,128]{2,1,0:T(8,128)S(1)}, u32[]{:S(2)}, u32[]{:S(2)}) collective-permute-start(f32[12,32,128]{2,1,0:T(8,128)} %get-tuple-element.36), channel_id=1, source_target_pairs={{0,8},{8,0},{16,24},{24,16},{1,9},{9,1},{17,25},{25,17},{2,10},{10... | collective-permute-start | bytes 589832 | tf_op jit(solution)/shard_map/ppermute | solution.py:615
  31.7 8.7 %copy-start = (f32[43,32,128]{2,1,0:T(8,128)}, f32[43,32,128]{2,1,0:T(8,128)S(1)}, u32[]{:S(2)}) copy-start(f32[43,32,128]{2,1,0:T(8,128)S(1)} %collective-permute-done.2.near) | copy-start | bytes 2113540
  38.3 2.0 %copy-start.1 = (f32[43,32,128]{2,1,0:T(8,128)}, f32[43,32,128]{2,1,0:T(8,128)S(1)}, u32[]{:S(2)}) copy-start(f32[43,32,128]{2,1,0:T(8,128)S(1)} %collective-permute-done.3.far) | copy-start | bytes 2113540
  38.4 1.5 %collective-permute-start.4 = (f32[2,43,4,128]{3,2,1,0:T(4,128)S(1)}, f32[2,43,4,128]{3,2,1,0:T(4,128)S(1)}, u32[]{:S(2)}, u32[]{:S(2)}) collective-permute-start(f32[2,43,4,128]{3,2,1,0:T(4,128)S(1)} %pad_maximum_fusion.1), channel_id=1, source_target_pairs={{0,1},{1,0},{2,3},{3,2},{4,5},{5,4},{6,7},{7,6},{8,9},{9,8},{10,11... | collective-permute-start | bytes 528392 | tf_op jit(solution)/shard_map/ppermute | solution.py:594
  39.9 0.7 %copy-start.3 = (f32[2,43,4,128]{3,2,1,0:T(4,128)}, f32[2,43,4,128]{3,2,1,0:T(4,128)S(1)}, u32[]{:S(2)}) copy-start(f32[2,43,4,128]{3,2,1,0:T(4,128)S(1)} %collective-permute-done.4.corner) | copy-start | bytes 528388
  39.9 12.1 %collective-permute-start.5 = (f32[12,32,128]{2,1,0:T(8,128)S(1)}, f32[12,32,128]{2,1,0:T(8,128)S(1)}, u32[]{:S(2)}, u32[]{:S(2)}) collective-permute-start(f32[12,32,128]{2,1,0:T(8,128)S(1)} %add.21), channel_id=1, source_target_pairs={{0,16},{8,24},{16,0},{24,8},{1,17},{9,25},{17,1},{25,9},{2,18},{10... | collective-permute-start | bytes 589832 | tf_op jit(solution)/shard_map/ppermute | solution.py:625
  48.3 6.4 %collective-permute-start.6 = (f32[2,4,32,128]{3,2,1,0:T(8,128)}, f32[2,4,32,128]{3,2,1,0:T(8,128)S(1)}, u32[]{:S(2)}, u32[]{:S(2)}) collective-permute-start(f32[2,4,32,128]{3,2,1,0:T(8,128)} %get-tuple-element.52), channel_id=1, source_target_pairs={{0,8},{8,0},{16,24},{24,16},{1,9},{9,1},{17,25},{25,17},{2,10},{10... | collective-permute-start | bytes 393224 | tf_op jit(solution)/shard_map/ppermute | solution.py:630
  54.8 8.3 %collective-permute-start.7 = (f32[2,4,32,128]{3,2,1,0:T(8,128)S(1)}, f32[2,4,32,128]{3,2,1,0:T(8,128)S(1)}, u32[]{:S(2)}, u32[]{:S(2)}) collective-permute-start(f32[2,4,32,128]{3,2,1,0:T(8,128)S(1)} %add.23), channel_id=1, source_target_pairs={{0,16},{8,24},{16,0},{24,8},{1,17},{9,25},{17,1},{25,9},{2,18},{10... | collective-permute-start | bytes 393224 | tf_op jit(solution)/shard_map/ppermute | solution.py:630
  56.4 8.4 %collective-permute-start.8 = (f32[12,32,128]{2,1,0:T(8,128)S(1)}, f32[12,32,128]{2,1,0:T(8,128)S(1)}, u32[]{:S(2)}, u32[]{:S(2)}) collective-permute-start(f32[12,32,128]{2,1,0:T(8,128)S(1)} %add.22), channel_id=1, source_target_pairs={{0,8},{8,0},{16,24},{24,16},{1,9},{9,1},{17,25},{25,17},{2,10},{10... | collective-permute-start | bytes 589832 | tf_op jit(solution)/shard_map/ppermute | solution.py:633
